TPU v7x, 32 devices: a whole 2x2x4 slice. The times are simulated.
32 devices in a mesh: groups: 2 (over x), orb: 16 (over z, y, core).
Axes of the slice: x: 2, y: 2, z: 4, core: 2. Of those that a mesh axis runs over, the one named last changes fastest.
Arguments:
- orbitals: bfloat16 [8192, 4096], P('orb', 'groups'), parts along dimension 1, may hold values from -6 to 6
- dipole_blocks: bfloat16 [6, 64, 3, 128, 128], P('groups', 'orb'), parts along dimension 0, may hold values from -0.3125 to 0.3125
- coupling_mask: int32 [64, 4], P('orb', 'groups'), parts along dimension 1, may hold values 0 or 1
- matchings: int32 [4, 16], P('groups'), parts along dimension 0, may hold values from 0 to 15, each once within a row
Outputs:
- localized: bfloat16 [8192, 4096], P('orb', 'groups'), parts along dimension 1
There are 2 independent parts, one for each index of `groups`. A program takes and returns all parts, laid end to end along the dimension named above; each array names one. Nothing has to cross between parts.
All inputs are finite; a program needn't handle non-finite values. No bound on the sum of `coupling_mask` on one device may be relied on, other than what follows from the above.
Results may differ from a plain program's by a relative error of at most 0.012.
The roundings to bfloat16 on the way count: a program that leaves them out, or rounds other values in their place, can miss the bound.
Values may be sent and summed in bfloat16 or wider, within the bound.
No kernel may reach another device: no remote copies, remote signals or barrier semaphores. Data moves between devices by JAX's collectives and lax.ppermute only.
A program may use at most 128 MiB of HBM per device.

v0:
```python
import jax
import jax.numpy as jnp
from jax import lax
from jax.sharding import PartitionSpec as P

HALF = 128
BLK = 128
ROUNDS = 2


def extended(block, sides, width):
    for axis, dim in sides:
        count = lax.axis_size(axis)
        forward = [(i, i + 1) for i in range(count - 1)]
        backward = [(target, source) for source, target in forward]
        low = lax.ppermute(
            lax.slice_in_dim(block, block.shape[dim] - width, None, axis=dim), axis, forward
        )
        high = lax.ppermute(lax.slice_in_dim(block, 0, width, axis=dim), axis, backward)
        block = jnp.concatenate([low, block, high], axis=dim)
    return block


def cayley(generator):
    identity = jnp.eye(generator.shape[-1], dtype=jnp.float32)
    square = jnp.matmul(generator, generator, precision=lax.Precision.HIGHEST)
    factor = jnp.linalg.cholesky(identity - 0.25 * square)
    raised = identity + 0.5 * generator
    numerator = jnp.matmul(raised, raised, precision=lax.Precision.HIGHEST)

    def solve_one(chol_factor, target):
        return jax.scipy.linalg.cho_solve((chol_factor, True), target)

    return jax.vmap(solve_one)(factor, numerator)


def per_device(orbitals, dipole_blocks, coupling_mask, matchings):
    row_count, orb_count = orbitals.shape
    block_count = orb_count // HALF
    pair_count = orb_count // (2 * HALF)
    pair_width = 2 * HALF
    own_rows = orb_count // lax.axis_size("orb")
    basis_count = row_count * lax.axis_size("orb")
    block_rows = row_count // BLK
    padded = extended(orbitals, (("orb", 0),), BLK)
    mask_full = jnp.stack(
        [coupling_mask[:, 0], jnp.ones((block_rows,), jnp.int32), coupling_mask[:, 1]], axis=1
    ).astype(jnp.bfloat16)
    image_list = []
    for component in range(3):
        summed = jnp.zeros((block_rows, BLK, orb_count), jnp.float32)
        for offset in range(3):
            shifted = padded[offset * BLK : offset * BLK + row_count].reshape(
                block_rows, BLK, orb_count
            )
            blocks = dipole_blocks[component, :, offset] * mask_full[:, offset][:, None, None]
            summed = summed + jnp.einsum(
                "bij,bjn->bin", blocks, shifted, preferred_element_type=jnp.float32
            )
        image_list.append(summed.reshape(row_count, orb_count).astype(jnp.bfloat16))
    images = jnp.stack(image_list)
    current = orbitals
    my_first = lax.axis_index("orb") * own_rows
    for round_index in range(ROUNDS):
        matching = matchings[round_index]
        inverse = jnp.argsort(matching)
        cols_now = jnp.take(
            current.reshape(row_count, block_count, HALF), matching, axis=1
        ).reshape(row_count, orb_count)
        image_now = jnp.take(
            images.reshape(3, row_count, block_count, HALF), matching, axis=2
        ).reshape(3, row_count, orb_count)
        diag_local = jnp.sum(
            cols_now.astype(jnp.float32)[None, :, :] * image_now.astype(jnp.float32), axis=1
        )
        diagonal = lax.psum(diag_local, "orb")
        cover = min(
            pair_count, -(-(own_rows * lax.axis_size("orb") + pair_width - own_rows) // pair_width)
        )
        left_cols = cols_now.reshape(row_count, cover, pair_width)
        right_cols = image_now.reshape(3, row_count, cover, pair_width)
        product = jnp.einsum(
            "rpa,krpb->pakb", left_cols, right_cols, preferred_element_type=jnp.float32
        )
        flat = product.reshape(cover * pair_width, 3 * pair_width)
        own_sums = lax.psum_scatter(flat, "orb", scatter_dimension=0, tiled=True).reshape(
            own_rows, 3, pair_width
        )
        pair_start = my_first // pair_width * pair_width
        diag_pair = lax.dynamic_slice_in_dim(diagonal, pair_start, pair_width, 1)
        diag_mine = lax.dynamic_slice_in_dim(diagonal, my_first, own_rows, 1)
        weighted = jnp.sum(
            own_sums * (jnp.transpose(diag_mine)[:, :, None] - diag_pair[None, :, :]), axis=1
        )
        gathered = lax.all_gather(weighted, "orb", axis=0, tiled=True).reshape(
            pair_count, pair_width, pair_width
        )
        gradient = gathered - jnp.swapaxes(gathered, 1, 2)
        rotation = cayley(0.02 / basis_count * gradient).astype(jnp.bfloat16)
        rotated = jnp.einsum(
            "rpa,pab->rpb",
            cols_now.reshape(row_count, pair_count, pair_width),
            rotation,
            preferred_element_type=jnp.float32,
        ).astype(jnp.bfloat16)
        current = jnp.take(rotated.reshape(row_count, block_count, HALF), inverse, axis=1).reshape(
            row_count, orb_count
        )
        if round_index + 1 < ROUNDS:
            image_rot = jnp.einsum(
                "krpa,pab->krpb",
                image_now.reshape(3, row_count, pair_count, pair_width),
                rotation,
                preferred_element_type=jnp.float32,
            ).astype(jnp.bfloat16)
            images = jnp.take(
                image_rot.reshape(3, row_count, block_count, HALF), inverse, axis=2
            ).reshape(3, row_count, orb_count)
    return current


def solution(mesh):
    in_specs = (
        P("orb", "groups"),
        P("groups", "orb", None, None, None),
        P("orb", "groups"),
        P("groups", None),
    )
    out_specs = P("orb", "groups")
    return jax.shard_map(
        per_device, mesh=mesh, in_specs=in_specs, out_specs=out_specs, check_vma=False
    )
```

profile of v0, /device:TPU:0, one launch (start us, length us, event | category | flops | bytes accessed | tf_op | source)
XLA Modules:
  0.0 1416.9 jit_solution(17364494543770401842)
XLA Ops:
  64.5 9.8 multiply_reduce_fusion.1
  74.3 8.8 copy.217
  83.1 7.3 fusion.4
  97.1 8.5 copy.319
  105.7 65.6 %psum.14 = f32[3,2048]{1,0:T(4,128)S(1)} all-reduce(f32[3,2048]{1,0:T(4,128)S(1)} %bitcast.284), channel_id=1, replica_groups=mesh['groups'=2,'orb'=16] {'orb'}, use_global_device_ids=true, to_apply=%region_2.5 | all-reduce | flops 6144 | bytes 49152 | tf_op jit(solution)/shard_map/psum | solution.py:76
  171.2 23.9 %reduce-scatter.3.cloned.1.call-done = f32[128,768]{0,1:T(8,128)} async-done(((f32[2048,768]{0,1:T(8,128)}), f32[128,768]{0,1:T(8,128)}) %reduce-scatter.3.cloned.1.call-update) | async-done | bytes 393232 | tf_op jit(solution)/shard_map/reduce_scatter | solution.py:86
  198.4 39.6 %all-gather.3.cloned.1.call-done = f32[2048,256]{0,1:T(8,128)} async-done(((f32[128,256]{0,1:T(8,128)}), f32[2048,256]{0,1:T(8,128)}) %all-gather.3.cloned.1.call-update) | async-done | bytes 2097168 | tf_op jit(solution)/shard_map/all_gather | solution.py:95
  260.0 93.8 %custom-call.19 = f32[8,128,128]{2,1,0:T(8,128)S(1)} custom-call(f32[8,128,128]{2,1,0:T(8,128)S(1)} %cholesky.198), custom_call_target="Cholesky" | custom-call | tf_op jit(solution)/shard_map/jit(cholesky)/cholesky | solution.py:27
  354.0 79.4 %custom-call.20 = f32[8,1,128,128]{2,3,1,0:T(8,128)} custom-call(f32[8,1,128,128]{3,2,1,0:T(8,128)S(1)} %select_bitcast_fusion.6), custom_call_target="InvertDiagBlocksLowerTriangular" | custom-call | tf_op jit(solution)/shard_map/jit(cholesky)/cholesky | solution.py:27
  438.4 94.6 %custom-call.21 = f32[8,128,128]{2,1,0:T(8,128)S(1)} custom-call(f32[8,128,128]{2,1,0:T(8,128)} %convolution_subtract_fusion.5), custom_call_target="Cholesky" | custom-call | tf_op jit(solution)/shard_map/jit(cholesky)/cholesky | solution.py:27
  541.8 158.2 %custom-call.22 = f32[8,2,128,128]{2,3,1,0:T(8,128)S(1)} custom-call(f32[8,2,128,128]{3,2,1,0:T(8,128)} %bitcast.281), custom_call_target="InvertDiagBlocksLowerTriangular" | custom-call | tf_op jit(solution)/shard_map/vmap(jit(_cho_solve))/triangular_solve | solution.py:32
  714.3 9.2 copy.239
  743.4 6.9 gather_fusion.5
  762.6 9.8 multiply_reduce_fusion
  772.4 8.7 copy.240
  781.1 7.3 fusion
  795.1 8.5 copy.320
  803.6 61.3 %psum.15 = f32[3,2048]{1,0:T(4,128)S(1)} all-reduce(f32[3,2048]{1,0:T(4,128)S(1)} %bitcast.285), channel_id=1, replica_groups=mesh['groups'=2,'orb'=16] {'orb'}, use_global_device_ids=true, to_apply=%region_11.16 | all-reduce | flops 6144 | bytes 49152 | tf_op jit(solution)/shard_map/psum | solution.py:76
  865.0 23.3 %reduce-scatter.5.cloned.1.call-done = f32[128,768]{0,1:T(8,128)} async-done(((f32[2048,768]{0,1:T(8,128)}), f32[128,768]{0,1:T(8,128)}) %reduce-scatter.5.cloned.1.call-update) | async-done | bytes 393232 | tf_op jit(solution)/shard_map/reduce_scatter | solution.py:86
  890.1 40.7 %all-gather.5.cloned.1.call-done = f32[2048,256]{0,1:T(8,128)} async-done(((f32[128,256]{0,1:T(8,128)}), f32[2048,256]{0,1:T(8,128)}) %all-gather.5.cloned.1.call-update) | async-done | bytes 2097168 | tf_op jit(solution)/shard_map/all_gather | solution.py:95
  952.4 94.0 %custom-call.23 = f32[8,128,128]{2,1,0:T(8,128)S(1)} custom-call(f32[8,128,128]{2,1,0:T(8,128)S(1)} %cholesky.201), custom_call_target="Cholesky" | custom-call | tf_op jit(solution)/shard_map/jit(cholesky)/cholesky | solution.py:27
  1046.6 79.2 %custom-call.24 = f32[8,1,128,128]{2,3,1,0:T(8,128)} custom-call(f32[8,1,128,128]{3,2,1,0:T(8,128)S(1)} %select_bitcast_fusion.5), custom_call_target="InvertDiagBlocksLowerTriangular" | custom-call | tf_op jit(solution)/shard_map/jit(cholesky)/cholesky | solution.py:27
  1130.7 94.6 %custom-call.25 = f32[8,128,128]{2,1,0:T(8,128)S(1)} custom-call(f32[8,128,128]{2,1,0:T(8,128)} %convolution_subtract_fusion.4), custom_call_target="Cholesky" | custom-call | tf_op jit(solution)/shard_map/jit(cholesky)/cholesky | solution.py:27
  1234.2 158.2 %custom-call.26 = f32[8,2,128,128]{2,3,1,0:T(8,128)S(1)} custom-call(f32[8,2,128,128]{3,2,1,0:T(8,128)} %bitcast.280), custom_call_target="InvertDiagBlocksLowerTriangular" | custom-call | tf_op jit(solution)/shard_map/vmap(jit(_cho_solve))/triangular_solve | solution.py:32
  (197 shorter events, 220.1 us)
Async XLA Ops:
  6.5 6.9 copy-start
  6.5 188.6 %reduce-scatter.3.cloned.1.call-start = ((), (), s32[]{:S(2)}) async-start(), calls=%async_computation.2 | async-start | bytes 6684672 | tf_op jit(solution)/shard_map/reduce_scatter | solution.py:86
  9.0 32.0 %collective-permute-start = (bf16[128,2048]{1,0:T(8,128)(2,1)}, bf16[128,2048]{1,0:T(8,128)(2,1)}, u32[]{:S(2)}, u32[]{:S(2)}) collective-permute-start(bf16[128,2048]{1,0:T(8,128)(2,1)} %get-tuple-element.68), channel_id=1, source_target_pairs={{0,1},{1,2},{2,3},{3,4},{4,5},{5,6},{6,7},{7,8},{8,9},{9,10},{10,1... | collective-permute-start | bytes 1572872 | tf_op jit(solution)/shard_map/ppermute | solution.py:16
  12.1 28.9 %collective-permute-start.1 = (bf16[128,2048]{1,0:T(8,128)(2,1)}, bf16[128,2048]{1,0:T(8,128)(2,1)}, u32[]{:S(2)}, u32[]{:S(2)}) collective-permute-start(bf16[128,2048]{1,0:T(8,128)(2,1)} %get-tuple-element.67), channel_id=1, source_target_pairs={{1,0},{2,1},{3,2},{4,3},{5,4},{6,5},{7,6},{8,7},{9,8},{10,9},{11,1... | collective-permute-start | bytes 1572872 | tf_op jit(solution)/shard_map/ppermute | solution.py:19
  13.4 3.7 copy-start.21
  19.7 2.5 copy-start.26
  19.7 2.5 copy-start.24
  74.3 8.8 copy-start.5
  105.6 132.5 %all-gather.3.cloned.1.call-start = ((), (), s32[]{:S(2)}) async-start(), calls=%async_computation.3 | async-start | bytes 2228224 | tf_op jit(solution)/shard_map/all_gather | solution.py:95
  197.0 691.3 %reduce-scatter.5.cloned.1.call-start = ((), (), s32[]{:S(2)}) async-start(), calls=%async_computation.4 | async-start | bytes 6684672 | tf_op jit(solution)/shard_map/reduce_scatter | solution.py:86
  242.2 6.2 copy-start.4
  253.7 3.1 copy-start.2
  700.0 3.8 copy-start.19
  700.1 2.7 copy-start.12
  702.8 6.6 slice-start
  704.9 4.5 slice-start.1
  714.3 9.2 copy-start.6
  743.4 7.0 copy-start.14
  756.5 24.6 %copy-start.7 = (bf16[16,512,128]{1,2,0:T(8,128)(2,1)}, bf16[16,512,128]{1,2,0:T(8,128)(2,1)S(1)}, u32[]{:S(2)}) copy-start(bf16[16,512,128]{1,2,0:T(8,128)(2,1)S(1)} %get-tuple-element.52) | copy-start | bytes 6291460
  803.6 127.3 %all-gather.5.cloned.1.call-start = ((), (), s32[]{:S(2)}) async-start(), calls=%async_computation.5 | async-start | bytes 2228224 | tf_op jit(solution)/shard_map/all_gather | solution.py:95
  934.7 6.2 copy-start.3
  946.1 3.1 copy-start.1
  1392.4 2.4 copy-start.11
  1402.1 2.3 copy-start.25
  (11 other events, 16.8 us)
Sparse Core Ops, SparseCore 0:
  105.7 89.3 reduce-scatter.2
  197.5 40.5 all-gather.2
  803.7 84.5 reduce-scatter.4
  890.3 40.5 all-gather.4
where the time goes:
time: 1430 us; the launch traced here: 1420 us
  other arithmetic  910 us (64%)
  local copies, waits for them, and re-layouts  151 us (11%)
  waiting for transfers between devices  128 us (9%)
  blocking collectives  127 us (9%)
  matrix products  82.8 us (6%)
  between operations  14.4 us (1%)
    another operation x18, other arithmetic, cayley(): factor = jnp.linalg.cholesky(identity - 0.25 * square)  536 us
    another operation x6, other arithmetic, solve_one(): return jax.scipy.linalg.cho_solve((chol_factor, True), target)  320 us
    psum x2, blocking collectives, per_device(): diagonal = lax.psum(diag_local, 'orb')  127 us
    all_gather x2, waiting for transfers between devices, per_device(): lax.all_gather(weighted, 'orb', axis=0, tiled=True)  80.4 us
    reduce_scatter x2, waiting for transfers between devices, per_device(): lax.psum_scatter(flat, 'orb', scatter_dimension=0, tiled=True)  47.2 us
    unnamed x64, local copies, waits for them, and re-layouts  31.3 us
  transfers between devices with their start and end apart: 6, of which 4 were waited for; matrix products, arithmetic and copies ran while one was open for 2% of the time, Pallas kernels for 0%

commit v1 on v0

v1 whole, which is shorter than its diff:
```python
import functools

import jax
import jax.numpy as jnp
from jax import lax
from jax.experimental import pallas as pl
from jax.experimental.pallas import tpu as pltpu
from jax.sharding import PartitionSpec as P

HALF = 128
BLK = 128
ROUNDS = 2
PAIR = 2 * HALF
F32 = jnp.float32
BF16 = jnp.bfloat16
WIRE = jnp.float32
VMEM_LIMIT = 32 * 1024 * 1024


def params():
    return pltpu.CompilerParams(vmem_limit_bytes=VMEM_LIMIT)


def bits_of(count):
    return count.bit_length() - 1


def bitrev(value, bits):
    return sum(((value >> j) & 1) << (bits - 1 - j) for j in range(bits))


def swap(block, distance):
    count = lax.axis_size("orb")
    return lax.ppermute(block, "orb", [(i, i ^ distance) for i in range(count)])


def put_diag(diag_ref, component, block, cols, image, first):
    total = jnp.sum(cols.astype(F32) * image.astype(F32), axis=0, keepdims=True)
    for half in range(total.shape[1] // HALF):
        spot = pl.ds(block + half, 1)
        piece = total[:, half * HALF : (half + 1) * HALF]
        if first:
            diag_ref[component, spot, :] = piece
        else:
            diag_ref[component, spot, :] += piece


def inner_kernel(block_rows, blocks_ref, cols_ref, image_ref, diag_ref):
    step = pl.program_id(0)
    for b in range(1, block_rows - 1):
        out = jnp.dot(
            blocks_ref[b], cols_ref[(b - 1) * BLK : (b + 2) * BLK], preferred_element_type=F32
        ).astype(BF16)
        own = cols_ref[b * BLK : (b + 1) * BLK]
        for k in range(3):
            image = out[k * BLK : (k + 1) * BLK]
            image_ref[k, (b - 1) * BLK : b * BLK] = image
            put_diag(diag_ref, k, 2 * step, own, image, b == 1)


def inner_images(blocks, orbitals):
    row_count, orb_count = orbitals.shape
    block_rows = row_count // BLK
    inner = row_count - 2 * BLK
    return pl.pallas_call(
        functools.partial(inner_kernel, block_rows),
        out_shape=(
            jax.ShapeDtypeStruct((3, inner, orb_count), BF16),
            jax.ShapeDtypeStruct((3, orb_count // HALF, HALF), F32),
        ),
        grid=(orb_count // PAIR,),
        in_specs=[
            pl.BlockSpec(blocks.shape, lambda c: (0, 0, 0)),
            pl.BlockSpec((row_count, PAIR), lambda c: (0, c)),
        ],
        out_specs=(
            pl.BlockSpec((3, inner, PAIR), lambda c: (0, 0, c)),
            pl.BlockSpec((3, orb_count // HALF, HALF), lambda c: (0, 0, 0)),
        ),
        compiler_params=params(),
        name="inner_images",
    )(blocks, orbitals)


def edge_kernel(block_rows, blocks_ref, cols_ref, low_ref, high_ref, start_ref, image_ref, diag_ref):
    step = pl.program_id(0)

    @pl.when(step == 0)
    def _():
        diag_ref[...] = start_ref[...]

    for place, b in ((0, 0), (1, block_rows - 1)):
        if b == 0:
            window = jnp.concatenate([low_ref[...], cols_ref[: 2 * BLK]], axis=0)
        else:
            window = jnp.concatenate([cols_ref[(b - 1) * BLK :], high_ref[...]], axis=0)
        out = jnp.dot(blocks_ref[b], window, preferred_element_type=F32).astype(BF16)
        own = cols_ref[b * BLK : (b + 1) * BLK]
        for k in range(3):
            image = out[k * BLK : (k + 1) * BLK]
            image_ref[k, place * BLK : (place + 1) * BLK] = image
            put_diag(diag_ref, k, 2 * step, own, image, False)


def edge_images(blocks, orbitals, low, high, start):
    row_count, orb_count = orbitals.shape
    block_rows = row_count // BLK
    return pl.pallas_call(
        functools.partial(edge_kernel, block_rows),
        out_shape=(
            jax.ShapeDtypeStruct((3, 2 * BLK, orb_count), BF16),
            jax.ShapeDtypeStruct((3, orb_count // HALF, HALF), F32),
        ),
        grid=(orb_count // PAIR,),
        in_specs=[
            pl.BlockSpec(blocks.shape, lambda c: (0, 0, 0)),
            pl.BlockSpec((row_count, PAIR), lambda c: (0, c)),
            pl.BlockSpec((BLK, PAIR), lambda c: (0, c)),
            pl.BlockSpec((BLK, PAIR), lambda c: (0, c)),
            pl.BlockSpec(start.shape, lambda c: (0, 0, 0)),
        ],
        out_specs=(
            pl.BlockSpec((3, 2 * BLK, PAIR), lambda c: (0, 0, c)),
            pl.BlockSpec((3, orb_count // HALF, HALF), lambda c: (0, 0, 0)),
        ),
        compiler_params=params(),
        name="edge_images",
    )(blocks, orbitals, low, high, start)


def lower_mask():
    rows = lax.broadcasted_iota(jnp.int32, (HALF, HALF), 0)
    cols = lax.broadcasted_iota(jnp.int32, (HALF, HALF), 1)
    return rows > cols


def whole_image(refs, component):
    pieces = [
        jnp.concatenate([refs[i][component], refs[i + 1][component]], axis=1)
        for i in range(0, len(refs), 2)
    ]
    if len(pieces) == 1:
        return pieces[0]
    inner, edge = pieces
    return jnp.concatenate([edge[:BLK], inner, edge[BLK:]], axis=0)


def gram_kernel(place_ref, *refs):
    ins, sums_ref = refs[:-1], refs[-1]
    cols = jnp.concatenate([ins[0][...], ins[1][...]], axis=1)
    low = lower_mask()
    for k in range(3):
        image = whole_image(ins[2:], k)
        mat = lax.dot_general(
            cols, image, (((0,), (0,)), ((), ())), preferred_element_type=F32
        )
        both = mat + mat.T
        sums_ref[0, k, :HALF] = both[:HALF, HALF:]
        sums_ref[0, k, HALF:] = jnp.where(low, both[:HALF, :HALF], both[HALF:, HALF:])


def pair_sums(place, cols, images):
    row_count, orb_count = cols.shape
    pair_count = orb_count // PAIR
    specs = [
        pl.BlockSpec((row_count, HALF), lambda p, at, h=h: (0, at[2 * p + h])) for h in (0, 1)
    ]
    operands = [cols, cols]
    for image in images:
        for h in (0, 1):
            specs.append(
                pl.BlockSpec(
                    (3, image.shape[1], HALF), lambda p, at, h=h: (0, 0, at[2 * p + h])
                )
            )
            operands.append(image)
    return pl.pallas_call(
        gram_kernel,
        out_shape=jax.ShapeDtypeStruct((pair_count, 3, PAIR, HALF), F32),
        grid_spec=pltpu.PrefetchScalarGridSpec(
            num_scalar_prefetch=1,
            grid=(pair_count,),
            in_specs=specs,
            out_specs=pl.BlockSpec((1, 3, PAIR, HALF), lambda p, at: (p, 0, 0, 0)),
        ),
        compiler_params=params(),
        name="pair_sums",
    )(place, *operands)


def weight_kernel(place_ref, me_ref, sums_ref, diag_ref, keep_ref, send_ref):
    p = pl.program_id(0)
    core = me_ref[0] & 1
    low = lower_mask()
    rows = [
        diag_ref[k, pl.ds(place_ref[2 * p + h], 1), :] for k in range(3) for h in (0, 1)
    ]
    turned = jnp.concatenate(rows + rows[:2], axis=0).T
    cross = jnp.zeros((HALF, HALF), F32)
    within = jnp.zeros((HALF, HALF), F32)
    for k in range(3):
        first_col = turned[:, 2 * k : 2 * k + 1]
        second_col = turned[:, 2 * k + 1 : 2 * k + 2]
        first_row, second_row = rows[2 * k], rows[2 * k + 1]
        cross += sums_ref[0, k, :HALF] * (first_col - second_row)
        within += sums_ref[0, k, HALF:] * (
            jnp.where(low, first_col, second_col) - jnp.where(low, first_row, second_row)
        )
    mine = core == 0
    keep_ref[0] = jnp.where(mine, cross, within)
    send_ref[0] = jnp.where(mine, within, cross)


def weigh(place, me, sums, diag):
    pair_count = sums.shape[0]
    tile = pl.BlockSpec((1, HALF, HALF), lambda p, at, who: (p, 0, 0))
    shape = jax.ShapeDtypeStruct((pair_count, HALF, HALF), F32)
    return pl.pallas_call(
        weight_kernel,
        out_shape=(shape, shape),
        grid_spec=pltpu.PrefetchScalarGridSpec(
            num_scalar_prefetch=2,
            grid=(pair_count,),
            in_specs=[
                pl.BlockSpec((1, 3, PAIR, HALF), lambda p, at, who: (p, 0, 0, 0)),
                pl.BlockSpec(diag.shape, lambda p, at, who: (0, 0, 0)),
            ],
            out_specs=(tile, tile),
        ),
        compiler_params=params(),
        name="weigh",
    )(place, me, sums, diag)


def matmul(left, right):
    return jnp.dot(left, right, precision=lax.Precision.HIGHEST, preferred_element_type=F32)


def rotation_kernel(scale, subs, me_ref, packed_ref, out_ref, sum_ref, power_ref):
    sub = me_ref[0] & (subs - 1)
    pieces = [packed_ref[bitrev(i, bits_of(subs)) ^ sub] for i in range(subs)]
    packed = jnp.concatenate(pieces, axis=0) * scale
    cross, within = packed[:HALF], packed[HALF:]
    low = lower_mask()
    first = jnp.where(low, within, 0.0)
    second = jnp.where(low, 0.0, within)
    half_gen = jnp.concatenate(
        [
            jnp.concatenate([first - first.T, cross], axis=1),
            jnp.concatenate([-cross.T, second - second.T], axis=1),
        ],
        axis=0,
    )
    rows = lax.broadcasted_iota(jnp.int32, (PAIR, PAIR), 0)
    cols = lax.broadcasted_iota(jnp.int32, (PAIR, PAIR), 1)
    eye = jnp.where(rows == cols, 1.0, 0.0).astype(F32)
    square = -matmul(half_gen, half_gen)
    fourth = matmul(square, square)
    bound = 1.0001 * jnp.sqrt(jnp.max(jnp.sum(jnp.abs(fourth), axis=1)))
    factor = 2.0 / (2.0 + bound)
    rest = 1.0 - factor
    sum_ref[...] = factor * ((1.0 + rest) * eye - factor * square)
    power_ref[...] = rest * rest * eye - (2.0 * rest * factor) * square + factor * factor * fourth

    def going(state):
        step, left = state
        return jnp.logical_and(step < 24, left > 1e-8)

    def body(state):
        step, left = state
        power = power_ref[...]
        sum_ref[...] += matmul(sum_ref[...], power)
        power_ref[...] = matmul(power, power)
        return step + 1, left * left

    reach = bound / (2.0 + bound)
    lax.while_loop(going, body, (jnp.int32(0), reach * reach))
    result = 2.0 * matmul(eye + half_gen, sum_ref[...]) - eye
    share = PAIR // subs
    for i in range(subs):

        @pl.when(sub == i)
        def _():
            out_ref[...] = result[i * share : (i + 1) * share].astype(BF16)


def rotation_share(scale, me, packed):
    subs = packed.shape[0]
    return pl.pallas_call(
        functools.partial(rotation_kernel, scale, subs),
        out_shape=jax.ShapeDtypeStruct((PAIR // subs, PAIR), BF16),
        grid_spec=pltpu.PrefetchScalarGridSpec(
            num_scalar_prefetch=1,
            grid=(1,),
            in_specs=[pl.BlockSpec(packed.shape, lambda i, who: (0, 0, 0))],
            out_specs=pl.BlockSpec((PAIR // subs, PAIR), lambda i, who: (0, 0)),
            scratch_shapes=[pltpu.VMEM((PAIR, PAIR), F32), pltpu.VMEM((PAIR, PAIR), F32)],
        ),
        compiler_params=params(),
        name="rotation",
    )(me, packed)


def assemble(gathered_ref, me, pair_count, pair):
    subs = PAIR // gathered_ref.shape[1]
    my_sub, my_pair = me & (subs - 1), me // subs
    return jnp.concatenate(
        [gathered_ref[(i ^ my_sub) * pair_count + (pair ^ my_pair)] for i in range(subs)], axis=0
    )


def rotate_kernel(pair_count, place_ref, me_ref, *refs):
    ins, (gathered_ref, out_ref, image_ref, diag_ref) = refs[:-4], refs[-4:]
    p = pl.program_id(0)
    rotation = assemble(gathered_ref, me_ref[0], pair_count, p)
    cols = jnp.concatenate([ins[0][...], ins[1][...]], axis=1)
    turned = jnp.dot(cols, rotation, preferred_element_type=F32).astype(BF16)
    out_ref[...] = turned
    for k in range(3):
        image = whole_image(ins[2:], k)
        moved = jnp.dot(image, rotation, preferred_element_type=F32).astype(BF16)
        image_ref[k] = moved
        put_diag(diag_ref, k, 2 * p, turned, moved, True)


def rotate(place, me, cols, images, gathered):
    row_count, orb_count = cols.shape
    pair_count = orb_count // PAIR
    specs = [
        pl.BlockSpec((row_count, HALF), lambda p, at, who, h=h: (0, at[2 * p + h])) for h in (0, 1)
    ]
    operands = [cols, cols]
    for image in images:
        for h in (0, 1):
            specs.append(
                pl.BlockSpec(
                    (3, image.shape[1], HALF), lambda p, at, who, h=h: (0, 0, at[2 * p + h])
                )
            )
            operands.append(image)
    specs.append(pl.BlockSpec(gathered.shape, lambda p, at, who: (0, 0, 0)))
    operands.append(gathered)
    return pl.pallas_call(
        functools.partial(rotate_kernel, pair_count),
        out_shape=(
            jax.ShapeDtypeStruct((row_count, orb_count), BF16),
            jax.ShapeDtypeStruct((3, row_count, orb_count), BF16),
            jax.ShapeDtypeStruct((3, orb_count // HALF, HALF), F32),
        ),
        grid_spec=pltpu.PrefetchScalarGridSpec(
            num_scalar_prefetch=2,
            grid=(pair_count,),
            in_specs=specs,
            out_specs=(
                pl.BlockSpec((row_count, PAIR), lambda p, at, who: (0, p)),
                pl.BlockSpec((3, row_count, PAIR), lambda p, at, who: (0, 0, p)),
                pl.BlockSpec((3, orb_count // HALF, HALF), lambda p, at, who: (0, 0, 0)),
            ),
        ),
        compiler_params=params(),
        name="rotate",
    )(place, me, *operands)


def last_kernel(
    pair_count, place_ref, home_ref, me_ref, first_ref, second_ref, gathered_ref, out_ref, held_ref
):
    p, h = pl.program_id(0), pl.program_id(1)

    @pl.when(h == 0)
    def _():
        rotation = assemble(gathered_ref, me_ref[0], pair_count, p)
        cols = jnp.concatenate([first_ref[...], second_ref[...]], axis=1)
        turned = jnp.dot(cols, rotation, preferred_element_type=F32).astype(BF16)
        out_ref[...] = turned[:, :HALF]
        held_ref[...] = turned[:, HALF:]

    @pl.when(h == 1)
    def _():
        out_ref[...] = held_ref[...]


def rotate_last(place, home, me, cols, gathered):
    row_count, orb_count = cols.shape
    pair_count = orb_count // PAIR
    return pl.pallas_call(
        functools.partial(last_kernel, pair_count),
        out_shape=jax.ShapeDtypeStruct((row_count, orb_count), BF16),
        grid_spec=pltpu.PrefetchScalarGridSpec(
            num_scalar_prefetch=3,
            grid=(pair_count, 2),
            in_specs=[
                pl.BlockSpec((row_count, HALF), lambda p, h, at, to, who: (0, at[2 * p])),
                pl.BlockSpec((row_count, HALF), lambda p, h, at, to, who: (0, at[2 * p + 1])),
                pl.BlockSpec(gathered.shape, lambda p, h, at, to, who: (0, 0, 0)),
            ],
            out_specs=pl.BlockSpec((row_count, HALF), lambda p, h, at, to, who: (0, to[2 * p + h])),
            scratch_shapes=[pltpu.VMEM((row_count, HALF), BF16)],
        ),
        compiler_params=params(),
        name="rotate_last",
    )(place, home, me, cols, cols, gathered)


def sum_all(value):
    count = lax.axis_size("orb")
    for bit in range(bits_of(count)):
        value = value + swap(value, 1 << bit)
    return value


def spread(value, bits, me, low_bit):
    ways = 1 << bits
    mine = (me >> low_bit) & (ways - 1)
    value = value.reshape((ways, -1) + value.shape[1:])
    pieces = [
        swap(
            lax.dynamic_index_in_dim(value, mine ^ q, 0, keepdims=False).astype(WIRE), q << low_bit
        )
        for q in range(1, ways)
    ]
    own = lax.dynamic_index_in_dim(value, mine, 0, keepdims=False)
    for piece in pieces:
        own = own + piece.astype(F32)
    return own


def reduce_pairs(keep, send, me):
    pair_count = keep.shape[0]
    pair_bits = bits_of(pair_count)
    sub_bits = bits_of(lax.axis_size("orb")) - pair_bits
    value = keep + swap(send, 1)
    for bit in range(1, sub_bits):
        rows = value.shape[1] // 2
        value = jnp.swapaxes(value.reshape(pair_count, 2, rows, HALF), 0, 1)
        value = spread(value.reshape(2 * pair_count, rows, HALF), 1, me, bit)
    high = pair_count // 2
    rows = value.shape[1]
    value = jnp.swapaxes(value.reshape(high, 2, rows, HALF), 0, 1).reshape(pair_count, rows, HALF)
    value = spread(value, 1, me, sub_bits)
    value = spread(value, pair_bits - 1, me, sub_bits + 1)
    return value[0]


def gather_bits(value, bits, low_bit):
    return jnp.concatenate(
        [value] + [swap(value, q << low_bit) for q in range(1, 1 << bits)], axis=0
    )


def per_device(orbitals, dipole_blocks, coupling_mask, matchings):
    row_count, orb_count = orbitals.shape
    count = lax.axis_size("orb")
    block_count = orb_count // HALF
    pair_count = orb_count // PAIR
    pair_bits = bits_of(pair_count)
    sub_bits = bits_of(count) - pair_bits
    basis_count = row_count * count
    block_rows = row_count // BLK
    position = lax.axis_index("orb").astype(jnp.int32)
    me = position.reshape(1)

    forward = [(i, i + 1) for i in range(count - 1)]
    backward = [(i + 1, i) for i in range(count - 1)]
    low = lax.ppermute(orbitals[row_count - BLK :], "orb", forward)
    high = lax.ppermute(orbitals[:BLK], "orb", backward)
    mask_full = jnp.stack(
        [coupling_mask[:, 0], jnp.ones((block_rows,), jnp.int32), coupling_mask[:, 1]], axis=1
    ).astype(BF16)
    blocks = jnp.transpose(
        dipole_blocks * mask_full[None, :, :, None, None], (1, 0, 3, 2, 4)
    ).reshape(block_rows, 3 * BLK, 3 * BLK)
    inner, diag = inner_images(blocks, orbitals)
    edge, diag = edge_images(blocks, orbitals, low, high, diag)

    cols, images = orbitals, (inner, edge)
    ident = jnp.arange(block_count, dtype=jnp.int32)
    held = ident
    for round_index in range(ROUNDS):
        matching = matchings[round_index].astype(jnp.int32)
        found = jnp.where(matching[:, None] == held[None, :], ident[None, :], 0)
        place = jnp.sum(found, axis=1).astype(jnp.int32)
        diag_sum = sum_all(diag)
        sums = pair_sums(place, cols, images)
        keep, send = weigh(place, me, sums, diag_sum)
        own = reduce_pairs(keep, send, position)
        packed = own[None]
        for bit in range(sub_bits):
            packed = gather_bits(packed, 1, bit)
        share = rotation_share(0.01 / basis_count, me, packed)
        gathered = gather_bits(share[None], 1, sub_bits)
        gathered = gather_bits(gathered, pair_bits - 1, sub_bits + 1)
        for bit in range(sub_bits):
            gathered = gather_bits(gathered, 1, bit)
        if round_index + 1 < ROUNDS:
            cols, moved, diag = rotate(place, me, cols, images, gathered)
            images = (moved,)
            held = matching
    return rotate_last(place, matching, me, cols, gathered)


def solution(mesh):
    in_specs = (
        P("orb", "groups"),
        P("groups", "orb", None, None, None),
        P("orb", "groups"),
        P("groups", None),
    )
    out_specs = P("orb", "groups")
    return jax.shard_map(
        per_device, mesh=mesh, in_specs=in_specs, out_specs=out_specs, check_vma=False
    )
```

time: 1430 us -> 193 us (0.13)
  other arithmetic: 910 us -> 1.75 us
  local copies, waits for them, and re-layouts: 151 us -> 17.4 us
  blocking collectives: 127 us -> 0 us
  matrix products: 82.8 us -> 0 us
  Pallas kernels: 0 us -> 60.8 us
  waiting for transfers between devices: 128 us -> 74.9 us
  starting transfers between devices: 4.57 us -> 36.6 us
    another operation x26 -> x2, other arithmetic: 860 us -> 0.08 us  [the longest x1 0.08 us: per_device(): jnp.stack([coupling_mask[:, 0], jnp.ones((block_rows,), jnp.int32), coupl...]
    psum x2 -> x0, blocking collectives: 127 us -> none  [per_device(): diagonal = lax.psum(diag_local, 'orb')]
    all_gather x2 -> x0, waiting for transfers between devices: 80.4 us -> none  [per_device(): lax.all_gather(weighted, 'orb', axis=0, tiled=True)]
    ppermute x2 -> x32, waiting for transfers between devices: 0.01 us -> 74.9 us  [the longest x30 74.9 us: swap(): return lax.ppermute(block, 'orb', [(i, i ^ distance) for i in range(count)])]
    pallas_call x0 -> x10, Pallas kernels: none -> 60.8 us  [the longest x2 14.6 us: pair_sums(): pl.pallas_call(gram_kernel, out_shape=jax.ShapeDtypeStruct((pair_count, 3...]
    dot_general x18 -> x0, matrix products: 56.4 us -> none  [the longest x2 14.5 us: per_device(): jnp.einsum('rpa,krpb->pakb', left_cols, right_cols, preferred_element_typ...]
    reduce_scatter x2 -> x0, waiting for transfers between devices: 47.2 us -> none  [per_device(): lax.psum_scatter(flat, 'orb', scatter_dimension=0, tiled=True)]
    ppermute x2 -> x32, starting transfers between devices: 4.44 us -> 36.6 us  [the longest x30 31.5 us: swap(): return lax.ppermute(block, 'orb', [(i, i ^ distance) for i in range(count)])]
  transfers between devices with their start and end apart: 6 -> 32, of which waited for: 4 -> 26; matrix products, arithmetic and copies ran while one was open for 2% -> 3% of each run, Pallas kernels for 0% -> 10%
where the time goes in v1:
time: 193 us; the launch traced here: 192 us
  waiting for transfers between devices  74.9 us (39%)
  Pallas kernels  60.8 us (32%)
  starting transfers between devices  36.6 us (19%)
  local copies, waits for them, and re-layouts  17.4 us (9%)
    ppermute x30, waiting for transfers between devices, swap(): return lax.ppermute(block, 'orb', [(i, i ^ distance) for i in range(count)])  74.9 us
    ppermute x30, starting transfers between devices, swap(): return lax.ppermute(block, 'orb', [(i, i ^ distance) for i in range(count)])  31.5 us
    pallas_call x2, Pallas kernels, pair_sums(): pl.pallas_call(gram_kernel, out_shape=jax.ShapeDtypeStruct((pair_count, 3...  14.6 us
    pallas_call x2, Pallas kernels, rotation_share(): pl.pallas_call(functools.partial(rotation_kernel, scale, subs), out_shape...  14.4 us
    unnamed x28, local copies, waits for them, and re-layouts  9.06 us
    pallas_call x1, Pallas kernels, rotate(): pl.pallas_call(functools.partial(rotate_kernel, pair_count), out_shape=(j...  8.01 us
    pallas_call x1, Pallas kernels, rotate_last(): pl.pallas_call(functools.partial(last_kernel, pair_count), out_shape=jax....  7.93 us
    pallas_call x2, Pallas kernels, weigh(): pl.pallas_call(weight_kernel, out_shape=(shape, shape), grid_spec=pltpu.P...  6.1 us
  transfers between devices with their start and end apart: 32, of which 26 were waited for; matrix products, arithmetic and copies ran while one was open for 3% of the time, Pallas kernels for 10%

profile of v1, /device:TPU:0, one launch (start us, length us, event | category | flops | bytes accessed | tf_op | source)
XLA Modules:
  0.0 191.8 jit_solution(4421196444515259916)
XLA Ops:
  3.7 3.8 %collective-permute-start = (bf16[128,2048]{1,0:T(8,128)(2,1)}, bf16[128,2048]{1,0:T(8,128)(2,1)}, u32[]{:S(2)}, u32[]{:S(2)}) collective-permute-start(bf16[128,2048]{1,0:T(8,128)(2,1)} %get-tuple-element.30), channel_id=1, source_target_pairs={{0,1},{1,2},{2,3},{3,4},{4,5},{5,6},{6,7},{7,8},{8,9},{9,10},{10,1... | collective-permute-start | bytes 1572872 | tf_op jit(solution)/shard_map/ppermute | solution.py:465
  10.1 3.4 %reshape.60.blocks_ref = bf16[4,384,384]{2,1,0:T(8,128)(2,1)S(1)} reshape(bf16[4,3,128,3,128]{4,3,2,1,0:T(4,128)(2,1)} %copy.18) | data formatting | bytes 2359296 | tf_op jit(solution)/shard_map/reshape | solution.py:472
  13.5 3.8 %inner_images.1 = (bf16[3,256,2048]{2,1,0:T(8,128)(2,1)S(1)}, f32[3,16,128]{2,1,0:T(8,128)S(1)}) custom-call(bf16[4,384,384]{2,1,0:T(8,128)(2,1)S(1)} %reshape.60.blocks_ref, bf16[512,2048]{1,0:T(8,128)(2,1)S(1)} %copy-done), custom_call_target="tpu_custom_call" | custom-call | tf_op jit(solution)/shard_map/inner_images/pallas_call | solution.py:65
  18.9 6.0 %edge_images.1 = (bf16[3,256,2048]{2,1,0:T(8,128)(2,1)S(1)}, f32[3,16,128]{2,1,0:T(8,128)S(1)}) custom-call(bf16[4,384,384]{2,1,0:T(8,128)(2,1)S(1)} %reshape.60.blocks_ref, bf16[512,2048]{1,0:T(8,128)(2,1)S(1)} %copy-done, bf16[128,2048]{1,0:T(8,128)(2,1)} %collective-permute-done.low_ref, bf16[128,2048]{1,0:T(8,128)(2,1)} %collective-permute-done.1.high_ref, ...), custom_call_target="tpu_custom_call" | custom-call | tf_op jit(solution)/shard_map/edge_images/pallas_call | solution.py:108
  37.2 2.6 %collective-permute-start.5 = (f32[3,16,128]{2,1,0:T(8,128)S(1)}, f32[3,16,128]{2,1,0:T(8,128)S(1)}, u32[]{:S(2)}, u32[]{:S(2)}) collective-permute-start(f32[3,16,128]{2,1,0:T(8,128)S(1)} %add.82), channel_id=1, source_target_pairs={{0,8},{1,9},{2,10},{3,11},{4,12},{5,13},{6,14},{7,15},{8,0},{9,1},... | collective-permute-start | bytes 73736 | tf_op jit(solution)/shard_map/ppermute | solution.py:34
  43.8 7.4 %pair_sums.2.sums_ref = f32[8,3,256,128]{3,2,1,0:T(8,128)S(1)} custom-call(s32[16]{0:T(128)S(1)} %get-tuple-element.27.place_ref, bf16[512,2048]{1,0:T(8,128)(2,1)S(1)} %copy-done, bf16[512,2048]{1,0:T(8,128)(2,1)S(1)} %copy-done, bf16[3,256,2048]{2,1,0:T(8,128)(2,1)S(1)} %copy-done.2, bf16[3,256,2048]{2,1,0:T(8,128)(2,1)S(1)} %copy-done.2, ...), custom_call_target="tpu_custom_call" | custom-call | tf_op jit(solution)/shard_map/pair_sums/pallas_call | solution.py:177
  51.2 3.0 %weigh.2 = (f32[8,128,128]{2,1,0:T(8,128)S(1)}, f32[8,128,128]{2,1,0:T(8,128)S(1)}) custom-call(s32[16]{0:T(128)S(1)} %get-tuple-element.27.place_ref, s32[1]{0:T(128)} %bitcast.2.me_ref, f32[8,3,256,128]{3,2,1,0:T(8,128)S(1)} %pair_sums.2.sums_ref, f32[3,16,128]{2,1,0:T(8,128)S(1)} %add.83.diag_ref), custom_call_target="tpu_custom_call" | custom-call | tf_op jit(solution)/shard_map/weigh/pallas_call | solution.py:218
  59.6 6.6 %collective-permute-done.7 = f32[4,128,128]{2,1,0:T(8,128)S(1)} collective-permute-done((f32[4,128,128]{2,1,0:T(8,128)S(1)}, f32[4,128,128]{2,1,0:T(8,128)S(1)}, u32[]{:S(2)}, u32[]{:S(2)}) %collective-permute-start.7) | collective-permute-done | bytes 262176 | tf_op jit(solution)/shard_map/ppermute | solution.py:34
  70.6 2.8 %collective-permute-done.10 = f32[1,128,128]{2,1,0:T(8,128)S(1)} collective-permute-done((f32[1,128,128]{2,1,0:T(8,128)S(1)}, f32[1,128,128]{2,1,0:T(8,128)S(1)}, u32[]{:S(2)}, u32[]{:S(2)}) %collective-permute-start.10) | collective-permute-done | bytes 65568 | tf_op jit(solution)/shard_map/ppermute | solution.py:34
  77.0 6.0 %rotation.2 = bf16[128,256]{1,0:T(8,128)(2,1)S(1)} custom-call(s32[1]{0:T(128)} %bitcast.2.me_ref, f32[2,128,128]{2,1,0:T(8,128)S(1)} %pad_maximum_fusion.packed_ref), custom_call_target="tpu_custom_call" | custom-call | tf_op jit(solution)/shard_map/rotation/pallas_call | solution.py:289
  84.5 2.8 %collective-permute-done.12 = bf16[1,128,256]{2,1,0:T(8,128)(2,1)S(1)} collective-permute-done((bf16[1,128,256]{2,1,0:T(8,128)(2,1)S(1)}, bf16[1,128,256]{2,1,0:T(8,128)(2,1)S(1)}, u32[]{:S(2)}, u32[]{:S(2)}) %collective-permute-start.12) | collective-permute-done | bytes 65568 | tf_op jit(solution)/shard_map/ppermute | solution.py:34
  91.0 4.0 %collective-permute-done.13 = bf16[2,128,256]{2,1,0:T(8,128)(2,1)S(1)} collective-permute-done((bf16[2,128,256]{2,1,0:T(8,128)(2,1)S(1)}, bf16[2,128,256]{2,1,0:T(8,128)(2,1)S(1)}, u32[]{:S(2)}, u32[]{:S(2)}) %collective-permute-start.13) | collective-permute-done | bytes 131104 | tf_op jit(solution)/shard_map/ppermute | solution.py:34
  95.0 6.5 %collective-permute-done.14 = bf16[2,128,256]{2,1,0:T(8,128)(2,1)S(1)} collective-permute-done((bf16[2,128,256]{2,1,0:T(8,128)(2,1)S(1)}, bf16[2,128,256]{2,1,0:T(8,128)(2,1)S(1)}, u32[]{:S(2)}, u32[]{:S(2)}) %collective-permute-start.14) | collective-permute-done | bytes 131104 | tf_op jit(solution)/shard_map/ppermute | solution.py:34
  105.5 8.0 %rotate.1 = (bf16[512,2048]{1,0:T(8,128)(2,1)S(1)}, bf16[3,512,2048]{2,1,0:T(8,128)(2,1)S(1)}, f32[3,16,128]{2,1,0:T(8,128)S(1)}) custom-call(s32[16]{0:T(128)S(1)} %get-tuple-element.27.place_ref, s32[1]{0:T(128)} %bitcast.2.me_ref, bf16[512,2048]{1,0:T(8,128)(2,1)S(1)} %copy-done, bf16[512,2048]{1,0:T(8,128)(2,1)S(1)} %copy-done, ...), custom_call_target="tpu_custom_call" | custom-call | tf_op jit(solution)/shard_map/rotate/pallas_call | solution.py:343
  118.6 3.8 %collective-permute-done.19 = f32[3,16,128]{2,1,0:T(8,128)S(1)} collective-permute-done((f32[3,16,128]{2,1,0:T(8,128)S(1)}, f32[3,16,128]{2,1,0:T(8,128)S(1)}, u32[]{:S(2)}, u32[]{:S(2)}) %collective-permute-start.19) | collective-permute-done | bytes 24608 | tf_op jit(solution)/shard_map/ppermute | solution.py:34
  122.7 7.2 %pair_sums.3.sums_ref = f32[8,3,256,128]{3,2,1,0:T(8,128)S(1)} custom-call(s32[16]{0:T(128)S(1)} %get-tuple-element.28.place_ref, bf16[512,2048]{1,0:T(8,128)(2,1)S(1)} %get-tuple-element.22.refs_0_.refs_1_.first_ref.second_ref, bf16[512,2048]{1,0:T(8,128)(2,1)S(1)} %get-tuple-element.22.refs_0_.refs_1_.first_ref.second_ref, ...), custom_call_target="tpu_custom_call" | custom-call | tf_op jit(solution)/shard_map/pair_sums/pallas_call | solution.py:177
  129.9 3.0 %weigh.3 = (f32[8,128,128]{2,1,0:T(8,128)S(1)}, f32[8,128,128]{2,1,0:T(8,128)S(1)}) custom-call(s32[16]{0:T(128)S(1)} %get-tuple-element.28.place_ref, s32[1]{0:T(128)} %bitcast.2.me_ref, f32[8,3,256,128]{3,2,1,0:T(8,128)S(1)} %pair_sums.3.sums_ref, f32[3,16,128]{2,1,0:T(8,128)S(1)} %add.98.diag_ref), custom_call_target="tpu_custom_call" | custom-call | tf_op jit(solution)/shard_map/weigh/pallas_call | solution.py:218
  136.5 7.0 %collective-permute-done.22 = f32[4,128,128]{2,1,0:T(8,128)S(1)} collective-permute-done((f32[4,128,128]{2,1,0:T(8,128)S(1)}, f32[4,128,128]{2,1,0:T(8,128)S(1)}, u32[]{:S(2)}, u32[]{:S(2)}) %collective-permute-start.22) | collective-permute-done | bytes 262176 | tf_op jit(solution)/shard_map/ppermute | solution.py:34
  147.9 4.0 %collective-permute-done.25 = f32[1,128,128]{2,1,0:T(8,128)S(1)} collective-permute-done((f32[1,128,128]{2,1,0:T(8,128)S(1)}, f32[1,128,128]{2,1,0:T(8,128)S(1)}, u32[]{:S(2)}, u32[]{:S(2)}) %collective-permute-start.25) | collective-permute-done | bytes 65568 | tf_op jit(solution)/shard_map/ppermute | solution.py:34
  154.9 8.4 %rotation.3 = bf16[128,256]{1,0:T(8,128)(2,1)S(1)} custom-call(s32[1]{0:T(128)} %bitcast.2.me_ref, f32[2,128,128]{2,1,0:T(8,128)S(1)} %pad_maximum_fusion.2.packed_ref), custom_call_target="tpu_custom_call" | custom-call | tf_op jit(solution)/shard_map/rotation/pallas_call | solution.py:289
  164.2 3.5 %collective-permute-done.27 = bf16[1,128,256]{2,1,0:T(8,128)(2,1)S(1)} collective-permute-done((bf16[1,128,256]{2,1,0:T(8,128)(2,1)S(1)}, bf16[1,128,256]{2,1,0:T(8,128)(2,1)S(1)}, u32[]{:S(2)}, u32[]{:S(2)}) %collective-permute-start.27) | collective-permute-done | bytes 65568 | tf_op jit(solution)/shard_map/ppermute | solution.py:34
  171.3 3.3 %collective-permute-done.28 = bf16[2,128,256]{2,1,0:T(8,128)(2,1)S(1)} collective-permute-done((bf16[2,128,256]{2,1,0:T(8,128)(2,1)S(1)}, bf16[2,128,256]{2,1,0:T(8,128)(2,1)S(1)}, u32[]{:S(2)}, u32[]{:S(2)}) %collective-permute-start.28) | collective-permute-done | bytes 131104 | tf_op jit(solution)/shard_map/ppermute | solution.py:34
  174.6 7.2 %collective-permute-done.29 = bf16[2,128,256]{2,1,0:T(8,128)(2,1)S(1)} collective-permute-done((bf16[2,128,256]{2,1,0:T(8,128)(2,1)S(1)}, bf16[2,128,256]{2,1,0:T(8,128)(2,1)S(1)}, u32[]{:S(2)}, u32[]{:S(2)}) %collective-permute-start.29) | collective-permute-done | bytes 131104 | tf_op jit(solution)/shard_map/ppermute | solution.py:34
  183.9 7.9 %rotate_last.1 = bf16[512,2048]{1,0:T(8,128)(2,1)} custom-call(s32[16]{0:T(128)S(1)} %get-tuple-element.28.place_ref, s32[16]{0:T(128)S(1)} %get-tuple-element.57.home_ref, s32[1]{0:T(128)} %bitcast.2.me_ref, bf16[512,2048]{1,0:T(8,128)(2,1)S(1)} %get-tuple-element.22.refs_0_.refs_1_.first_ref.second_ref, ...), custom_call_target="tpu_custom_call" | custom-call | tf_op jit(solution)/shard_map/rotate_last/pallas_call | solution.py:386
  (115 shorter events, 69.4 us)
Async XLA Ops:
  2.4 16.6 %collective-permute-start.1 = (bf16[128,2048]{1,0:T(8,128)(2,1)}, bf16[128,2048]{1,0:T(8,128)(2,1)}, u32[]{:S(2)}, u32[]{:S(2)}) collective-permute-start(bf16[128,2048]{1,0:T(8,128)(2,1)} %get-tuple-element.29), channel_id=1, source_target_pairs={{1,0},{2,1},{3,2},{4,3},{5,4},{6,5},{7,6},{8,7},{9,8},{10,9},{11,1... | collective-permute-start | bytes 1572872 | tf_op jit(solution)/shard_map/ppermute | solution.py:466
  3.7 15.3 %collective-permute-start = (bf16[128,2048]{1,0:T(8,128)(2,1)}, bf16[128,2048]{1,0:T(8,128)(2,1)}, u32[]{:S(2)}, u32[]{:S(2)}) collective-permute-start(bf16[128,2048]{1,0:T(8,128)(2,1)} %get-tuple-element.30), channel_id=1, source_target_pairs={{0,1},{1,2},{2,3},{3,4},{4,5},{5,6},{6,7},{7,8},{8,9},{9,10},{10,1... | collective-permute-start | bytes 1572872 | tf_op jit(solution)/shard_map/ppermute | solution.py:465
  29.2 4.2 %collective-permute-start.3 = (f32[3,16,128]{2,1,0:T(8,128)S(1)}, f32[3,16,128]{2,1,0:T(8,128)S(1)}, u32[]{:S(2)}, u32[]{:S(2)}) collective-permute-start(f32[3,16,128]{2,1,0:T(8,128)S(1)} %add.80), channel_id=1, source_target_pairs={{0,2},{1,3},{2,0},{3,1},{4,6},{5,7},{6,4},{7,5},{8,10},{9,11},{10,... | collective-permute-start | bytes 73736 | tf_op jit(solution)/shard_map/ppermute | solution.py:34
  33.4 3.8 %collective-permute-start.4 = (f32[3,16,128]{2,1,0:T(8,128)S(1)}, f32[3,16,128]{2,1,0:T(8,128)S(1)}, u32[]{:S(2)}, u32[]{:S(2)}) collective-permute-start(f32[3,16,128]{2,1,0:T(8,128)S(1)} %add.81), channel_id=1, source_target_pairs={{0,4},{1,5},{2,6},{3,7},{4,0},{5,1},{6,2},{7,3},{8,12},{9,13},{10,... | collective-permute-start | bytes 73736 | tf_op jit(solution)/shard_map/ppermute | solution.py:34
  37.2 13.9 %collective-permute-start.5 = (f32[3,16,128]{2,1,0:T(8,128)S(1)}, f32[3,16,128]{2,1,0:T(8,128)S(1)}, u32[]{:S(2)}, u32[]{:S(2)}) collective-permute-start(f32[3,16,128]{2,1,0:T(8,128)S(1)} %add.82), channel_id=1, source_target_pairs={{0,8},{1,9},{2,10},{3,11},{4,12},{5,13},{6,14},{7,15},{8,0},{9,1},... | collective-permute-start | bytes 73736 | tf_op jit(solution)/shard_map/ppermute | solution.py:34
  57.5 8.7 %collective-permute-start.7 = (f32[4,128,128]{2,1,0:T(8,128)S(1)}, f32[4,128,128]{2,1,0:T(8,128)S(1)}, u32[]{:S(2)}, u32[]{:S(2)}) collective-permute-start(f32[4,128,128]{2,1,0:T(8,128)S(1)} %dynamic-slice_bitcast_fusion.1), channel_id=1, source_target_pairs={{0,2},{1,3},{2,0},{3,1},{4,6},{5,7},{6,4},{7,5},{8,10},{9,11},{10,... | collective-permute-start | bytes 786440 | tf_op jit(solution)/shard_map/ppermute | solution.py:34
  66.3 4.3 %collective-permute-start.8 = (f32[1,128,128]{2,1,0:T(8,128)S(1)}, f32[1,128,128]{2,1,0:T(8,128)S(1)}, u32[]{:S(2)}, u32[]{:S(2)}) collective-permute-start(f32[1,128,128]{2,1,0:T(8,128)S(1)} %get-tuple-element.34), channel_id=1, source_target_pairs={{0,4},{1,5},{2,6},{3,7},{4,0},{5,1},{6,2},{7,3},{8,12},{9,13},{10,... | collective-permute-start | bytes 196616 | tf_op jit(solution)/shard_map/ppermute | solution.py:34
  67.3 6.1 %collective-permute-start.10 = (f32[1,128,128]{2,1,0:T(8,128)S(1)}, f32[1,128,128]{2,1,0:T(8,128)S(1)}, u32[]{:S(2)}, u32[]{:S(2)}) collective-permute-start(f32[1,128,128]{2,1,0:T(8,128)S(1)} %get-tuple-element.35), channel_id=1, source_target_pairs={{0,12},{1,13},{2,14},{3,15},{4,8},{5,9},{6,10},{7,11},{8,4},{9,5},... | collective-permute-start | bytes 196616 | tf_op jit(solution)/shard_map/ppermute | solution.py:34
  68.1 7.5 %collective-permute-start.9 = (f32[1,128,128]{2,1,0:T(8,128)S(1)}, f32[1,128,128]{2,1,0:T(8,128)S(1)}, u32[]{:S(2)}, u32[]{:S(2)}) collective-permute-start(f32[1,128,128]{2,1,0:T(8,128)S(1)} %get-tuple-element.36), channel_id=1, source_target_pairs={{0,8},{1,9},{2,10},{3,11},{4,12},{5,13},{6,14},{7,15},{8,0},{9,1},... | collective-permute-start | bytes 196616 | tf_op jit(solution)/shard_map/ppermute | solution.py:34
  83.0 4.3 %collective-permute-start.12 = (bf16[1,128,256]{2,1,0:T(8,128)(2,1)S(1)}, bf16[1,128,256]{2,1,0:T(8,128)(2,1)S(1)}, u32[]{:S(2)}, u32[]{:S(2)}) collective-permute-start(bf16[1,128,256]{2,1,0:T(8,128)(2,1)S(1)} %bitcast.32), channel_id=1, source_target_pairs={{0,2},{1,3},{2,0},{3,1},{4,6},{5,7},{6,4},{7,5},{8,10},{9,11},{10,... | collective-permute-start | bytes 196616 | tf_op jit(solution)/shard_map/ppermute | solution.py:34
  87.3 7.6 %collective-permute-start.13 = (bf16[2,128,256]{2,1,0:T(8,128)(2,1)S(1)}, bf16[2,128,256]{2,1,0:T(8,128)(2,1)S(1)}, u32[]{:S(2)}, u32[]{:S(2)}) collective-permute-start(bf16[2,128,256]{2,1,0:T(8,128)(2,1)S(1)} %pad_maximum_fusion.1), channel_id=1, source_target_pairs={{0,4},{1,5},{2,6},{3,7},{4,0},{5,1},{6,2},{7,3},{8,12},{9,13},{10,... | collective-permute-start | bytes 393224 | tf_op jit(solution)/shard_map/ppermute | solution.py:34
  87.4 14.1 %collective-permute-start.15 = (bf16[2,128,256]{2,1,0:T(8,128)(2,1)S(1)}, bf16[2,128,256]{2,1,0:T(8,128)(2,1)S(1)}, u32[]{:S(2)}, u32[]{:S(2)}) collective-permute-start(bf16[2,128,256]{2,1,0:T(8,128)(2,1)S(1)} %pad_maximum_fusion.1), channel_id=1, source_target_pairs={{0,12},{1,13},{2,14},{3,15},{4,8},{5,9},{6,10},{7,11},{8,4},{9,5},... | collective-permute-start | bytes 393224 | tf_op jit(solution)/shard_map/ppermute | solution.py:34
  88.9 12.6 %collective-permute-start.14 = (bf16[2,128,256]{2,1,0:T(8,128)(2,1)S(1)}, bf16[2,128,256]{2,1,0:T(8,128)(2,1)S(1)}, u32[]{:S(2)}, u32[]{:S(2)}) collective-permute-start(bf16[2,128,256]{2,1,0:T(8,128)(2,1)S(1)} %pad_maximum_fusion.1), channel_id=1, source_target_pairs={{0,8},{1,9},{2,10},{3,11},{4,12},{5,13},{6,14},{7,15},{8,0},{9,1},... | collective-permute-start | bytes 393224 | tf_op jit(solution)/shard_map/ppermute | solution.py:34
  114.8 3.8 %collective-permute-start.18 = (f32[3,16,128]{2,1,0:T(8,128)S(1)}, f32[3,16,128]{2,1,0:T(8,128)S(1)}, u32[]{:S(2)}, u32[]{:S(2)}) collective-permute-start(f32[3,16,128]{2,1,0:T(8,128)S(1)} %add.95), channel_id=1, source_target_pairs={{0,2},{1,3},{2,0},{3,1},{4,6},{5,7},{6,4},{7,5},{8,10},{9,11},{10,... | collective-permute-start | bytes 73736 | tf_op jit(solution)/shard_map/ppermute | solution.py:34
  118.6 3.8 %collective-permute-start.19 = (f32[3,16,128]{2,1,0:T(8,128)S(1)}, f32[3,16,128]{2,1,0:T(8,128)S(1)}, u32[]{:S(2)}, u32[]{:S(2)}) collective-permute-start(f32[3,16,128]{2,1,0:T(8,128)S(1)} %add.96), channel_id=1, source_target_pairs={{0,4},{1,5},{2,6},{3,7},{4,0},{5,1},{6,2},{7,3},{8,12},{9,13},{10,... | collective-permute-start | bytes 73736 | tf_op jit(solution)/shard_map/ppermute | solution.py:34
  122.4 7.4 %collective-permute-start.20 = (f32[3,16,128]{2,1,0:T(8,128)S(1)}, f32[3,16,128]{2,1,0:T(8,128)S(1)}, u32[]{:S(2)}, u32[]{:S(2)}) collective-permute-start(f32[3,16,128]{2,1,0:T(8,128)S(1)} %add.97), channel_id=1, source_target_pairs={{0,8},{1,9},{2,10},{3,11},{4,12},{5,13},{6,14},{7,15},{8,0},{9,1},... | collective-permute-start | bytes 73736 | tf_op jit(solution)/shard_map/ppermute | solution.py:34
  135.0 8.4 %collective-permute-start.22 = (f32[4,128,128]{2,1,0:T(8,128)S(1)}, f32[4,128,128]{2,1,0:T(8,128)S(1)}, u32[]{:S(2)}, u32[]{:S(2)}) collective-permute-start(f32[4,128,128]{2,1,0:T(8,128)S(1)} %dynamic-slice_bitcast_fusion), channel_id=1, source_target_pairs={{0,2},{1,3},{2,0},{3,1},{4,6},{5,7},{6,4},{7,5},{8,10},{9,11},{10,... | collective-permute-start | bytes 786440 | tf_op jit(solution)/shard_map/ppermute | solution.py:34
  143.5 4.4 %collective-permute-start.23 = (f32[1,128,128]{2,1,0:T(8,128)S(1)}, f32[1,128,128]{2,1,0:T(8,128)S(1)}, u32[]{:S(2)}, u32[]{:S(2)}) collective-permute-start(f32[1,128,128]{2,1,0:T(8,128)S(1)} %get-tuple-element.31), channel_id=1, source_target_pairs={{0,4},{1,5},{2,6},{3,7},{4,0},{5,1},{6,2},{7,3},{8,12},{9,13},{10,... | collective-permute-start | bytes 196616 | tf_op jit(solution)/shard_map/ppermute | solution.py:34
  145.6 6.2 %collective-permute-start.25 = (f32[1,128,128]{2,1,0:T(8,128)S(1)}, f32[1,128,128]{2,1,0:T(8,128)S(1)}, u32[]{:S(2)}, u32[]{:S(2)}) collective-permute-start(f32[1,128,128]{2,1,0:T(8,128)S(1)} %get-tuple-element.32), channel_id=1, source_target_pairs={{0,12},{1,13},{2,14},{3,15},{4,8},{5,9},{6,10},{7,11},{8,4},{9,5},... | collective-permute-start | bytes 196616 | tf_op jit(solution)/shard_map/ppermute | solution.py:34
  147.7 5.8 %collective-permute-start.24 = (f32[1,128,128]{2,1,0:T(8,128)S(1)}, f32[1,128,128]{2,1,0:T(8,128)S(1)}, u32[]{:S(2)}, u32[]{:S(2)}) collective-permute-start(f32[1,128,128]{2,1,0:T(8,128)S(1)} %get-tuple-element.33), channel_id=1, source_target_pairs={{0,8},{1,9},{2,10},{3,11},{4,12},{5,13},{6,14},{7,15},{8,0},{9,1},... | collective-permute-start | bytes 196616 | tf_op jit(solution)/shard_map/ppermute | solution.py:34
  163.3 4.3 %collective-permute-start.27 = (bf16[1,128,256]{2,1,0:T(8,128)(2,1)S(1)}, bf16[1,128,256]{2,1,0:T(8,128)(2,1)S(1)}, u32[]{:S(2)}, u32[]{:S(2)}) collective-permute-start(bf16[1,128,256]{2,1,0:T(8,128)(2,1)S(1)} %bitcast.34), channel_id=1, source_target_pairs={{0,2},{1,3},{2,0},{3,1},{4,6},{5,7},{6,4},{7,5},{8,10},{9,11},{10,... | collective-permute-start | bytes 196616 | tf_op jit(solution)/shard_map/ppermute | solution.py:34
  167.7 6.9 %collective-permute-start.28 = (bf16[2,128,256]{2,1,0:T(8,128)(2,1)S(1)}, bf16[2,128,256]{2,1,0:T(8,128)(2,1)S(1)}, u32[]{:S(2)}, u32[]{:S(2)}) collective-permute-start(bf16[2,128,256]{2,1,0:T(8,128)(2,1)S(1)} %pad_maximum_fusion.3), channel_id=1, source_target_pairs={{0,4},{1,5},{2,6},{3,7},{4,0},{5,1},{6,2},{7,3},{8,12},{9,13},{10,... | collective-permute-start | bytes 393224 | tf_op jit(solution)/shard_map/ppermute | solution.py:34
  167.8 14.1 %collective-permute-start.30 = (bf16[2,128,256]{2,1,0:T(8,128)(2,1)S(1)}, bf16[2,128,256]{2,1,0:T(8,128)(2,1)S(1)}, u32[]{:S(2)}, u32[]{:S(2)}) collective-permute-start(bf16[2,128,256]{2,1,0:T(8,128)(2,1)S(1)} %pad_maximum_fusion.3), channel_id=1, source_target_pairs={{0,12},{1,13},{2,14},{3,15},{4,8},{5,9},{6,10},{7,11},{8,4},{9,5},... | collective-permute-start | bytes 393224 | tf_op jit(solution)/shard_map/ppermute | solution.py:34
  170.0 11.8 %collective-permute-start.29 = (bf16[2,128,256]{2,1,0:T(8,128)(2,1)S(1)}, bf16[2,128,256]{2,1,0:T(8,128)(2,1)S(1)}, u32[]{:S(2)}, u32[]{:S(2)}) collective-permute-start(bf16[2,128,256]{2,1,0:T(8,128)(2,1)S(1)} %pad_maximum_fusion.3), channel_id=1, source_target_pairs={{0,8},{1,9},{2,10},{3,11},{4,12},{5,13},{6,14},{7,15},{8,0},{9,1},... | collective-permute-start | bytes 393224 | tf_op jit(solution)/shard_map/ppermute | solution.py:34
  (18 other events, 94.2 us)

commit v2 on v1

v2 whole, which is shorter than its diff:
```python
import functools

import jax
import jax.numpy as jnp
from jax import lax
from jax.experimental import pallas as pl
from jax.experimental.pallas import tpu as pltpu
from jax.sharding import PartitionSpec as P

HALF = 128
BLK = 128
ROUNDS = 2
PAIR = 2 * HALF
F32 = jnp.float32
BF16 = jnp.bfloat16
VMEM_LIMIT = 24 * 1024 * 1024
VMEM = pl.BlockSpec(memory_space=pltpu.VMEM)
SMEM = pl.BlockSpec(memory_space=pltpu.SMEM)
TILE = 512
SMALL = 3e-8
WIRE = BF16


def params():
    return pltpu.CompilerParams(vmem_limit_bytes=VMEM_LIMIT)


def bits_of(count):
    return count.bit_length() - 1


def bitrev(value, bits):
    return sum(((value >> j) & 1) << (bits - 1 - j) for j in range(bits))


def swap(block, distance):
    count = lax.axis_size("orb")
    return lax.ppermute(block, "orb", [(i, i ^ distance) for i in range(count)])


def put_diag(diag_ref, component, block, cols, image, first):
    total = jnp.sum(cols.astype(F32) * image.astype(F32), axis=0, keepdims=True)
    for half in range(total.shape[1] // HALF):
        spot = pl.ds(block + half, 1)
        piece = total[:, half * HALF : (half + 1) * HALF]
        if first:
            diag_ref[component, spot, :] = piece
        else:
            diag_ref[component, spot, :] += piece


def edge_rows_kernel(last_ref, first_ref, last_out_ref, first_out_ref):
    last_out_ref[...] = last_ref[...]
    first_out_ref[...] = first_ref[...]


def edge_rows(orbitals):
    row_count, orb_count = orbitals.shape
    shape = jax.ShapeDtypeStruct((BLK, orb_count), BF16)
    return pl.pallas_call(
        edge_rows_kernel,
        out_shape=(shape, shape),
        grid=(1,),
        in_specs=[
            pl.BlockSpec((BLK, orb_count), lambda i: (row_count // BLK - 1, 0)),
            pl.BlockSpec((BLK, orb_count), lambda i: (0, 0)),
        ],
        out_specs=(VMEM, VMEM),
        compiler_params=params(),
        name="edge_rows",
    )(orbitals, orbitals)


def inner_kernel(block_rows, blocks_ref, cols_ref, image_ref, diag_ref):
    for start in range(0, cols_ref.shape[1], TILE):
        tile = slice(start, start + TILE)
        for b in range(1, block_rows - 1):
            out = jnp.dot(
                blocks_ref[b],
                cols_ref[(b - 1) * BLK : (b + 2) * BLK, tile],
                preferred_element_type=F32,
            ).astype(BF16)
            own = cols_ref[b * BLK : (b + 1) * BLK, tile]
            for k in range(3):
                image = out[k * BLK : (k + 1) * BLK]
                image_ref[k, (b - 1) * BLK : b * BLK, tile] = image
                put_diag(diag_ref, k, start // HALF, own, image, b == 1)


def inner_images(blocks, orbitals):
    row_count, orb_count = orbitals.shape
    block_rows = row_count // BLK
    return pl.pallas_call(
        functools.partial(inner_kernel, block_rows),
        out_shape=(
            jax.ShapeDtypeStruct((3, row_count - 2 * BLK, orb_count), BF16),
            jax.ShapeDtypeStruct((3, orb_count // HALF, HALF), F32),
        ),
        in_specs=[VMEM, VMEM],
        out_specs=(VMEM, VMEM),
        compiler_params=params(),
        name="inner_images",
    )(blocks, orbitals)


def edge_kernel(block_rows, blocks_ref, cols_ref, low_ref, high_ref, start_ref, image_ref, diag_ref):
    diag_ref[...] = start_ref[...]
    for start in range(0, cols_ref.shape[1], TILE):
        tile = slice(start, start + TILE)
        for place, b in ((0, 0), (1, block_rows - 1)):
            if b == 0:
                window = jnp.concatenate([low_ref[:, tile], cols_ref[: 2 * BLK, tile]], axis=0)
            else:
                window = jnp.concatenate(
                    [cols_ref[(b - 1) * BLK :, tile], high_ref[:, tile]], axis=0
                )
            out = jnp.dot(blocks_ref[b], window, preferred_element_type=F32).astype(BF16)
            own = cols_ref[b * BLK : (b + 1) * BLK, tile]
            for k in range(3):
                image = out[k * BLK : (k + 1) * BLK]
                image_ref[k, place * BLK : (place + 1) * BLK, tile] = image
                put_diag(diag_ref, k, start // HALF, own, image, False)


def edge_images(blocks, orbitals, low, high, start):
    row_count, orb_count = orbitals.shape
    block_rows = row_count // BLK
    return pl.pallas_call(
        functools.partial(edge_kernel, block_rows),
        out_shape=(
            jax.ShapeDtypeStruct((3, 2 * BLK, orb_count), BF16),
            jax.ShapeDtypeStruct((3, orb_count // HALF, HALF), F32),
        ),
        in_specs=[VMEM] * 5,
        out_specs=(VMEM, VMEM),
        compiler_params=params(),
        name="edge_images",
    )(blocks, orbitals, low, high, start)


def lower_mask():
    rows = lax.broadcasted_iota(jnp.int32, (HALF, HALF), 0)
    cols = lax.broadcasted_iota(jnp.int32, (HALF, HALF), 1)
    return rows > cols


def pair_columns(ref, lead, places):
    return jnp.concatenate(
        [ref[lead + (slice(None), pl.ds(pl.multiple_of(at * HALF, HALF), HALF))] for at in places],
        axis=1,
    )


def pair_image(refs, component, places):
    pieces = [pair_columns(ref, (component,), places) for ref in refs]
    if len(pieces) == 1:
        return pieces[0]
    inner, edge = pieces
    return jnp.concatenate([edge[:BLK], inner, edge[BLK:]], axis=0)


def gram_kernel(first, place_ref, cols_ref, *refs):
    image_refs, mats_ref = refs[:-1], refs[-1]
    for i in range(mats_ref.shape[0]):
        places = [place_ref[2 * (first + i) + h] for h in (0, 1)]
        cols = pair_columns(cols_ref, (), places)
        images = jnp.concatenate([pair_image(image_refs, k, places) for k in range(3)], axis=1)
        mats_ref[i] = lax.dot_general(
            cols, images, (((0,), (0,)), ((), ())), preferred_element_type=F32
        )


def pair_products(place, cols, images, first, count):
    return pl.pallas_call(
        functools.partial(gram_kernel, first),
        out_shape=jax.ShapeDtypeStruct((count, PAIR, 3 * PAIR), F32),
        in_specs=[SMEM] + [VMEM] * (1 + len(images)),
        out_specs=VMEM,
        compiler_params=params(),
        name="pair_products",
    )(place, cols, *images)


def weight_kernel(first, place_ref, me_ref, diag_ref, *refs):
    mats_refs, keep_ref, send_ref = refs[:-2], refs[-2], refs[-1]
    mine = (me_ref[0] & 1) == 0
    low = lower_mask()
    p = 0
    for mats_ref in mats_refs:
        for i in range(mats_ref.shape[0]):
            halves = [
                [diag_ref[k, pl.ds(place_ref[2 * (first + p) + h], 1), :] for k in range(3)] for h in (0, 1)
            ]
            turned = jnp.concatenate(
                [jnp.concatenate(half + half + half[:2], axis=0).T for half in halves], axis=0
            )
            total = jnp.zeros((PAIR, PAIR), F32)
            for k in range(3):
                row = jnp.concatenate([half[k] for half in halves], axis=1)
                total += mats_ref[i, :, k * PAIR : (k + 1) * PAIR] * (turned[:, k : k + 1] - row)
            one, two = total[:HALF, :HALF], total[HALF:, HALF:]
            cross = total[:HALF, HALF:] - total[HALF:, :HALF].T
            within = jnp.where(low, one, two) - jnp.where(low, two, one).T
            keep_ref[p] = jnp.where(mine, cross, within)
            send_ref[p] = jnp.where(mine, within, cross)
            p += 1


def weigh(place, me, diag, mats, first):
    pair_count = sum(mat.shape[0] for mat in mats)
    shape = jax.ShapeDtypeStruct((pair_count, HALF, HALF), F32)
    return pl.pallas_call(
        functools.partial(weight_kernel, first),
        out_shape=(shape, shape),
        in_specs=[SMEM, SMEM] + [VMEM] * (1 + len(mats)),
        out_specs=(VMEM, VMEM),
        compiler_params=params(),
        name="weigh",
    )(place, me, diag, *mats)


def matmul(left, right):
    return jnp.dot(left, right, precision=lax.Precision.HIGHEST, preferred_element_type=F32)


def rotation_kernel(scale, subs, me_ref, packed_ref, out_ref, sum_ref, power_ref):
    sub = me_ref[0] & (subs - 1)
    pieces = [packed_ref[bitrev(i, bits_of(subs)) ^ sub] for i in range(subs)]
    packed = jnp.concatenate(pieces, axis=0) * scale
    cross, within = packed[:HALF], packed[HALF:]
    low = lower_mask()
    first = jnp.where(low, within, 0.0)
    second = jnp.where(low, 0.0, within)
    half_gen = jnp.concatenate(
        [
            jnp.concatenate([first - first.T, cross], axis=1),
            jnp.concatenate([-cross.T, second - second.T], axis=1),
        ],
        axis=0,
    )
    rows = lax.broadcasted_iota(jnp.int32, (PAIR, PAIR), 0)
    cols = lax.broadcasted_iota(jnp.int32, (PAIR, PAIR), 1)
    eye = jnp.where(rows == cols, 1.0, 0.0).astype(F32)
    square = -matmul(half_gen, half_gen)
    fourth = matmul(square, square)
    bound = 1.0001 * jnp.sqrt(jnp.max(jnp.sum(jnp.abs(fourth), axis=1)))
    factor = 2.0 / (2.0 + bound)
    rest = 1.0 - factor
    sum_ref[...] = factor * ((1.0 + rest) * eye - factor * square)
    power_ref[...] = rest * rest * eye - (2.0 * rest * factor) * square + factor * factor * fourth

    def going(state):
        step, left = state
        return jnp.logical_and(step < 24, left > SMALL)

    def body(state):
        step, left = state
        power = power_ref[...]
        sum_ref[...] += matmul(sum_ref[...], power)

        @pl.when(left * left > SMALL)
        def _():
            power_ref[...] = matmul(power, power)

        return step + 1, left * left

    reach = bound / (2.0 + bound)
    lax.while_loop(going, body, (jnp.int32(0), reach * reach))
    result = 2.0 * matmul(eye + half_gen, sum_ref[...]) - eye
    share = PAIR // subs
    for i in range(subs):

        @pl.when(sub == i)
        def _():
            out_ref[...] = result[i * share : (i + 1) * share].astype(BF16)


def rotation_share(scale, me, packed):
    subs = packed.shape[0]
    return pl.pallas_call(
        functools.partial(rotation_kernel, scale, subs),
        out_shape=jax.ShapeDtypeStruct((PAIR // subs, PAIR), BF16),
        in_specs=[SMEM, VMEM],
        out_specs=VMEM,
        scratch_shapes=[pltpu.VMEM((PAIR, PAIR), F32), pltpu.VMEM((PAIR, PAIR), F32)],
        compiler_params=params(),
        name="rotation",
    )(me, packed)


def assemble(gathered_ref, me, pair_count, pair):
    subs = PAIR // gathered_ref.shape[1]
    my_sub, my_pair = me & (subs - 1), me // subs
    return jnp.concatenate(
        [gathered_ref[(i ^ my_sub) * pair_count + (pair ^ my_pair)] for i in range(subs)], axis=0
    )


def rotate_kernel(pair_count, place_ref, me_ref, gathered_ref, cols_ref, *refs):
    image_refs, (out_ref, image_ref, diag_ref) = refs[:-3], refs[-3:]
    for p in range(pair_count):
        rotation = assemble(gathered_ref, me_ref[0], pair_count, p)
        places = [place_ref[2 * p + h] for h in (0, 1)]
        spot = slice(p * PAIR, (p + 1) * PAIR)
        cols = pair_columns(cols_ref, (), places)
        turned = jnp.dot(cols, rotation, preferred_element_type=F32).astype(BF16)
        out_ref[:, spot] = turned
        for k in range(3):
            image = pair_image(image_refs, k, places)
            moved = jnp.dot(image, rotation, preferred_element_type=F32).astype(BF16)
            image_ref[k, :, spot] = moved
            put_diag(diag_ref, k, 2 * p, turned, moved, True)


def rotate(place, me, gathered, cols, images):
    row_count, orb_count = cols.shape
    return pl.pallas_call(
        functools.partial(rotate_kernel, orb_count // PAIR),
        out_shape=(
            jax.ShapeDtypeStruct((row_count, orb_count), BF16),
            jax.ShapeDtypeStruct((3, row_count, orb_count), BF16),
            jax.ShapeDtypeStruct((3, orb_count // HALF, HALF), F32),
        ),
        in_specs=[SMEM, SMEM] + [VMEM] * (2 + len(images)),
        out_specs=(VMEM, VMEM, VMEM),
        compiler_params=params(),
        name="rotate",
    )(place, me, gathered, cols, *images)


def last_kernel(pair_count, place_ref, home_ref, me_ref, gathered_ref, cols_ref, out_ref):
    for p in range(pair_count):
        rotation = assemble(gathered_ref, me_ref[0], pair_count, p)
        places = [place_ref[2 * p + h] for h in (0, 1)]
        cols = pair_columns(cols_ref, (), places)
        turned = jnp.dot(cols, rotation, preferred_element_type=F32).astype(BF16)
        for h in (0, 1):
            home = pl.multiple_of(home_ref[2 * p + h] * HALF, HALF)
            out_ref[:, pl.ds(home, HALF)] = turned[:, h * HALF : (h + 1) * HALF]


def rotate_last(place, home, me, gathered, cols):
    row_count, orb_count = cols.shape
    rows = row_count // 2
    return pl.pallas_call(
        functools.partial(last_kernel, orb_count // PAIR),
        out_shape=jax.ShapeDtypeStruct((row_count, orb_count), BF16),
        grid=(row_count // rows,),
        in_specs=[
            SMEM,
            SMEM,
            SMEM,
            pl.BlockSpec(gathered.shape, lambda r: (0, 0, 0)),
            pl.BlockSpec((rows, orb_count), lambda r: (r, 0)),
        ],
        out_specs=pl.BlockSpec((rows, orb_count), lambda r: (r, 0)),
        compiler_params=params(),
        name="rotate_last",
    )(place, home, me, gathered, cols)


def sum_beside(diag, makers):
    made = []
    hops = bits_of(lax.axis_size("orb"))
    for bit in range(hops):
        arrived = swap(diag, 1 << bit)
        if bit < len(makers):
            diag, arrived, product = lax.optimization_barrier((diag, arrived, makers[bit](diag)))
            made.append(product)
        diag = diag + arrived
    return diag, made


def places_of(position, sub_bits, pair_bits):
    steps = [(bit, 1) for bit in range(1, sub_bits)] + [(sub_bits, 1), (sub_bits + 1, pair_bits - 1)]
    found = {}
    for low_bit, bits in steps:
        mine = (position >> low_bit) & ((1 << bits) - 1)
        found[low_bit] = [(mine ^ q).astype(jnp.uint32) for q in range(1 << bits)]
    return found


def pick(value, at):
    zero = jnp.uint32(0)
    start = (at,) + (zero,) * (value.ndim - 1)
    return lax.dynamic_slice(value, start, (1,) + value.shape[1:])[0]


def spread(value, places, low_bit, wire):
    ways = len(places)
    value = value.reshape((ways, -1) + value.shape[1:])
    pieces = [swap(pick(value, places[q]).astype(wire), q << low_bit) for q in range(1, ways)]
    own = pick(value, places[0])
    for piece in pieces:
        own = own + piece.astype(F32)
    return own


def reduce_pairs(value, places, sub_bits):
    pair_count = value.shape[0]
    for bit in range(1, sub_bits):
        rows = value.shape[1] // 2
        value = jnp.swapaxes(value.reshape(pair_count, 2, rows, HALF), 0, 1)
        value = spread(value.reshape(2 * pair_count, rows, HALF), places[bit], bit, F32)
    rows = value.shape[1]
    value = value.reshape(pair_count // 2, 2, rows, HALF)
    value = jnp.swapaxes(value, 0, 1).reshape(pair_count, rows, HALF)
    value = spread(value, places[sub_bits], sub_bits, BF16)
    return spread(value, places[sub_bits + 1], sub_bits + 1, WIRE)[0]


def gather_bits(value, bits, low_bit):
    return jnp.concatenate(
        [value] + [swap(value, q << low_bit) for q in range(1, 1 << bits)], axis=0
    )


def per_device(orbitals, dipole_blocks, coupling_mask, matchings):
    row_count, orb_count = orbitals.shape
    count = lax.axis_size("orb")
    block_count = orb_count // HALF
    pair_count = orb_count // PAIR
    pair_bits = bits_of(pair_count)
    sub_bits = bits_of(count) - pair_bits
    basis_count = row_count * count
    block_rows = row_count // BLK
    position = lax.axis_index("orb").astype(jnp.int32)
    places = places_of(position, sub_bits, pair_bits)
    ident = jnp.arange(block_count, dtype=jnp.int32)
    held = [ident] + [matchings[r] for r in range(ROUNDS - 1)]
    spots = []
    for r in range(ROUNDS):
        found = jnp.where(matchings[r][:, None] == held[r][None, :], ident[None, :], 0)
        spots.append(jnp.sum(found, axis=1).astype(jnp.int32))
    orbitals, places, spots, me = lax.optimization_barrier(
        (orbitals, places, spots, position.reshape(1))
    )

    forward = [(i, i + 1) for i in range(count - 1)]
    backward = [(i + 1, i) for i in range(count - 1)]
    last, first = edge_rows(orbitals)
    low = lax.ppermute(last, "orb", forward)
    high = lax.ppermute(first, "orb", backward)
    mask_full = jnp.stack(
        [coupling_mask[:, 0], jnp.ones((block_rows,), jnp.int32), coupling_mask[:, 1]], axis=1
    ).astype(BF16)
    blocks = jnp.transpose(
        dipole_blocks * mask_full[None, :, :, None, None], (1, 0, 3, 2, 4)
    ).reshape(block_rows, 3 * BLK, 3 * BLK)
    inner, diag = inner_images(blocks, orbitals)
    edge, diag = edge_images(blocks, orbitals, low, high, diag)

    cols, images = orbitals, (inner, edge)
    for round_index in range(ROUNDS):
        place = spots[round_index]
        splits = 4
        step = pair_count // splits

        def product(start, token):
            held_cols, _ = lax.optimization_barrier((cols, token))
            return pair_products(place, held_cols, images, start, step)

        makers = [functools.partial(product, i * step) for i in range(splits)]
        diag_sum, mats = sum_beside(diag, makers)
        half = splits // 2
        keep_a, send_a = weigh(place, me, diag_sum, mats[:half], 0)
        came_a = swap(send_a, 1)
        keep_b, send_b = weigh(place, me, diag_sum, mats[half:], half * step)
        came_a, keep_b, send_b = lax.optimization_barrier((came_a, keep_b, send_b))
        value = jnp.concatenate([keep_a + came_a, keep_b + swap(send_b, 1)], axis=0)
        own = reduce_pairs(value, places, sub_bits)
        packed = own[None]
        for bit in range(sub_bits):
            packed = gather_bits(packed, 1, bit)
        share = rotation_share(0.01 / basis_count, me, packed)
        gathered = gather_bits(share[None], 1, sub_bits)
        gathered = gather_bits(gathered, pair_bits - 1, sub_bits + 1)
        for bit in range(sub_bits):
            gathered = gather_bits(gathered, 1, bit)
        if round_index + 1 < ROUNDS:
            cols, moved, diag = rotate(place, me, gathered, cols, images)
            images = (moved,)
    return rotate_last(place, matchings[ROUNDS - 1], me, gathered, cols)


def solution(mesh):
    in_specs = (
        P("orb", "groups"),
        P("groups", "orb", None, None, None),
        P("orb", "groups"),
        P("groups", None),
    )
    out_specs = P("orb", "groups")
    return jax.shard_map(
        per_device, mesh=mesh, in_specs=in_specs, out_specs=out_specs, check_vma=False
    )
```

time: 193 us -> 161 us (0.83)
  Pallas kernels: 60.8 us -> 45.9 us
  waiting for transfers between devices: 74.9 us -> 62.4 us
  local copies, waits for them, and re-layouts: 17.4 us -> 8.54 us
  starting transfers between devices: 36.6 us -> 40.4 us
    ppermute x30 -> x32, waiting for transfers between devices: 74.9 us -> 62.4 us  [swap(): return lax.ppermute(block, 'orb', [(i, i ^ distance) for i in range(count)])]
    pallas_call x6 -> x15, Pallas kernels: 36.6 us -> 27 us  [the longest x8 10.8 us: pair_products(): pl.pallas_call(functools.partial(gram_kernel, first), out_shape=jax.Shape...]
    unnamed x28 -> x16, local copies, waits for them, and re-layouts: 9.06 us -> 1.71 us
    ppermute x30 -> x32, starting transfers between devices: 31.5 us -> 36 us  [swap(): return lax.ppermute(block, 'orb', [(i, i ^ distance) for i in range(count)])]
    pallas_call x1, Pallas kernels: 5.96 us -> 3.08 us  [edge_images(): pl.pallas_call(functools.partial(edge_kernel, block_rows), out_shape=(jax...]
    slice x1 -> x0, local copies, waits for them, and re-layouts: 2.37 us -> none  [per_device(): high = lax.ppermute(orbitals[:BLK], 'orb', backward)]
    pallas_call x1, Pallas kernels: 3.81 us -> 1.87 us  [inner_images(): pl.pallas_call(functools.partial(inner_kernel, block_rows), out_shape=(ja...]
  transfers between devices with their start and end apart: 32 -> 34, of which waited for: 26 -> 25; matrix products, arithmetic and copies ran while one was open for 3% -> 4% of each run, Pallas kernels for 10% -> 11%
where the time goes in v2:
time: 161 us; the launch traced here: 159 us
  waiting for transfers between devices  62.4 us (39%)
  Pallas kernels  45.9 us (29%)
  starting transfers between devices  40.4 us (25%)
  local copies, waits for them, and re-layouts  8.54 us (5%)
    ppermute x32, waiting for transfers between devices, swap(): return lax.ppermute(block, 'orb', [(i, i ^ distance) for i in range(count)])  62.4 us
    ppermute x32, starting transfers between devices, swap(): return lax.ppermute(block, 'orb', [(i, i ^ distance) for i in range(count)])  36 us
    pallas_call x2, Pallas kernels, rotation_share(): pl.pallas_call(functools.partial(rotation_kernel, scale, subs), out_shape...  14 us
    pallas_call x8, Pallas kernels, pair_products(): pl.pallas_call(functools.partial(gram_kernel, first), out_shape=jax.Shape...  10.8 us
    pallas_call x4, Pallas kernels, weigh(): pl.pallas_call(functools.partial(weight_kernel, first), out_shape=(shape,...  8.45 us
    pallas_call x1, Pallas kernels, rotate(): pl.pallas_call(functools.partial(rotate_kernel, orb_count // PAIR), out_s...  3.77 us
    reshape x1, local copies, waits for them, and re-layouts, per_device(): blocks = jnp.transpose(dipole_blocks * mask_full[None, :, :, None, None],...  3.51 us
  transfers between devices with their start and end apart: 34, of which 25 were waited for; matrix products, arithmetic and copies ran while one was open for 4% of the time, Pallas kernels for 11%

profile of v2, /device:TPU:0, one launch (start us, length us, event | category | flops | bytes accessed | tf_op | source)
XLA Modules:
  0.0 158.6 jit_solution(13465591366069092050)
XLA Ops:
  3.6 3.2 %collective-permute-start = (bf16[128,2048]{1,0:T(8,128)(2,1)}, bf16[128,2048]{1,0:T(8,128)(2,1)}, u32[]{:S(2)}, u32[]{:S(2)}) collective-permute-start(bf16[128,2048]{1,0:T(8,128)(2,1)} %get-tuple-element.74), channel_id=1, source_target_pairs={{0,1},{1,2},{2,3},{3,4},{4,5},{5,6},{6,7},{7,8},{8,9},{9,10},{10,1... | collective-permute-start | bytes 1572872 | tf_op jit(solution)/shard_map/ppermute | solution.py:442
  10.7 3.5 %reshape.74.blocks_ref = bf16[4,384,384]{2,1,0:T(8,128)(2,1)S(1)} reshape(bf16[4,3,128,3,128]{4,3,2,1,0:T(4,128)(2,1)} %copy.12) | data formatting | bytes 2359296 | tf_op jit(solution)/shard_map/reshape | solution.py:449
  16.1 3.1 %edge_images.1 = (bf16[3,256,2048]{2,1,0:T(8,128)(2,1)S(1)}, f32[3,16,128]{2,1,0:T(8,128)S(1)}) custom-call(bf16[4,384,384]{2,1,0:T(8,128)(2,1)S(1)} %reshape.74.blocks_ref, bf16[512,2048]{1,0:T(8,128)(2,1)S(1)} %copy-done.1, bf16[128,2048]{1,0:T(8,128)(2,1)} %collective-permute-done.low_ref, bf16[128,2048]{1,0:T(8,128)(2,1)} %collective-permute-done.1.high_ref, ...), custom_call_target="tpu_custom_call" | custom-call | tf_op jit(solution)/shard_map/edge_images/pallas_call | solution.py:128
  19.2 4.6 %collective-permute-start.2 = (f32[3,16,128]{2,1,0:T(8,128)S(1)}, f32[3,16,128]{2,1,0:T(8,128)S(1)}, u32[]{:S(2)}, u32[]{:S(2)}) collective-permute-start(f32[3,16,128]{2,1,0:T(8,128)S(1)} %get-tuple-element.81), channel_id=1, source_target_pairs={{0,1},{1,0},{2,3},{3,2},{4,5},{5,4},{6,7},{7,6},{8,9},{9,8},{10,11... | collective-permute-start | bytes 73736 | tf_op jit(solution)/shard_map/ppermute | solution.py:38
  25.2 2.4 %collective-permute-start.3 = (f32[3,16,128]{2,1,0:T(8,128)S(1)}, f32[3,16,128]{2,1,0:T(8,128)S(1)}, u32[]{:S(2)}, u32[]{:S(2)}) collective-permute-start(f32[3,16,128]{2,1,0:T(8,128)S(1)} %add.60), channel_id=1, source_target_pairs={{0,2},{1,3},{2,0},{3,1},{4,6},{5,7},{6,4},{7,5},{8,10},{9,11},{10,... | collective-permute-start | bytes 73736 | tf_op jit(solution)/shard_map/ppermute | solution.py:38
  29.5 2.7 %collective-permute-start.4 = (f32[3,16,128]{2,1,0:T(8,128)S(1)}, f32[3,16,128]{2,1,0:T(8,128)S(1)}, u32[]{:S(2)}, u32[]{:S(2)}) collective-permute-start(f32[3,16,128]{2,1,0:T(8,128)S(1)} %add.61), channel_id=1, source_target_pairs={{0,4},{1,5},{2,6},{3,7},{4,0},{5,1},{6,2},{7,3},{8,12},{9,13},{10,... | collective-permute-start | bytes 73736 | tf_op jit(solution)/shard_map/ppermute | solution.py:38
  34.0 3.0 %collective-permute-start.5 = (f32[3,16,128]{2,1,0:T(8,128)S(1)}, f32[3,16,128]{2,1,0:T(8,128)S(1)}, u32[]{:S(2)}, u32[]{:S(2)}) collective-permute-start(f32[3,16,128]{2,1,0:T(8,128)S(1)} %add.62), channel_id=1, source_target_pairs={{0,8},{1,9},{2,10},{3,11},{4,12},{5,13},{6,14},{7,15},{8,0},{9,1},... | collective-permute-start | bytes 73736 | tf_op jit(solution)/shard_map/ppermute | solution.py:38
  46.3 4.6 %collective-permute-done.8 = bf16[4,128,128]{2,1,0:T(8,128)(2,1)S(1)} collective-permute-done((bf16[4,128,128]{2,1,0:T(8,128)(2,1)S(1)}, bf16[4,128,128]{2,1,0:T(8,128)(2,1)S(1)}, u32[]{:S(2)}, u32[]{:S(2)}) %collective-permute-start.8) | collective-permute-done | bytes 131104 | tf_op jit(solution)/shard_map/ppermute | solution.py:38
  52.9 2.5 %collective-permute-start.11 = (bf16[1,128,128]{2,1,0:T(8,128)(2,1)S(1)}, bf16[1,128,128]{2,1,0:T(8,128)(2,1)S(1)}, u32[]{:S(2)}, u32[]{:S(2)}) collective-permute-start(bf16[1,128,128]{2,1,0:T(8,128)(2,1)S(1)} %get-tuple-element.141), channel_id=1, source_target_pairs={{0,12},{1,13},{2,14},{3,15},{4,8},{5,9},{6,10},{7,11},{8,4},{9,5},... | collective-permute-start | bytes 98312 | tf_op jit(solution)/shard_map/ppermute | solution.py:38
  55.6 3.3 %collective-permute-done.11 = bf16[1,128,128]{2,1,0:T(8,128)(2,1)S(1)} collective-permute-done((bf16[1,128,128]{2,1,0:T(8,128)(2,1)S(1)}, bf16[1,128,128]{2,1,0:T(8,128)(2,1)S(1)}, u32[]{:S(2)}, u32[]{:S(2)}) %collective-permute-start.11) | collective-permute-done | bytes 32800 | tf_op jit(solution)/shard_map/ppermute | solution.py:38
  61.6 6.3 %rotation.2 = bf16[128,256]{1,0:T(8,128)(2,1)S(1)} custom-call(s32[1]{0:T(128)} %bitcast.2.me_ref, f32[2,128,128]{2,1,0:T(8,128)S(1)} %pad_maximum_fusion.2.packed_ref), custom_call_target="tpu_custom_call" | custom-call | tf_op jit(solution)/shard_map/rotation/pallas_call | solution.py:280
  68.1 4.1 %collective-permute-done.13 = bf16[1,128,256]{2,1,0:T(8,128)(2,1)S(1)} collective-permute-done((bf16[1,128,256]{2,1,0:T(8,128)(2,1)S(1)}, bf16[1,128,256]{2,1,0:T(8,128)(2,1)S(1)}, u32[]{:S(2)}, u32[]{:S(2)}) %collective-permute-start.13) | collective-permute-done | bytes 65568 | tf_op jit(solution)/shard_map/ppermute | solution.py:38
  75.9 3.8 %collective-permute-done.14 = bf16[2,128,256]{2,1,0:T(8,128)(2,1)S(1)} collective-permute-done((bf16[2,128,256]{2,1,0:T(8,128)(2,1)S(1)}, bf16[2,128,256]{2,1,0:T(8,128)(2,1)S(1)}, u32[]{:S(2)}, u32[]{:S(2)}) %collective-permute-start.14) | collective-permute-done | bytes 131104 | tf_op jit(solution)/shard_map/ppermute | solution.py:38
  79.7 6.7 %collective-permute-done.15 = bf16[2,128,256]{2,1,0:T(8,128)(2,1)S(1)} collective-permute-done((bf16[2,128,256]{2,1,0:T(8,128)(2,1)S(1)}, bf16[2,128,256]{2,1,0:T(8,128)(2,1)S(1)}, u32[]{:S(2)}, u32[]{:S(2)}) %collective-permute-start.15) | collective-permute-done | bytes 131104 | tf_op jit(solution)/shard_map/ppermute | solution.py:38
  88.5 3.8 %rotate.1 = (bf16[512,2048]{1,0:T(8,128)(2,1)S(1)}, bf16[3,512,2048]{2,1,0:T(8,128)(2,1)S(1)}, f32[3,16,128]{2,1,0:T(8,128)S(1)}) custom-call(s32[16]{0:T(128)S(1)} %get-tuple-element.72.place_ref, s32[1]{0:T(128)} %bitcast.2.me_ref, bf16[16,128,256]{2,1,0:T(8,128)(2,1)S(1)} %constant_dynamic-update-slice_fusion.5.gathered_ref, ...), custom_call_target="tpu_custom_call" | custom-call | tf_op jit(solution)/shard_map/rotate/pallas_call | solution.py:317
  99.1 2.5 %collective-permute-done.20 = f32[3,16,128]{2,1,0:T(8,128)S(1)} collective-permute-done((f32[3,16,128]{2,1,0:T(8,128)S(1)}, f32[3,16,128]{2,1,0:T(8,128)S(1)}, u32[]{:S(2)}, u32[]{:S(2)}) %collective-permute-start.20) | collective-permute-done | bytes 24608 | tf_op jit(solution)/shard_map/ppermute | solution.py:38
  103.1 3.2 %collective-permute-done.21 = f32[3,16,128]{2,1,0:T(8,128)S(1)} collective-permute-done((f32[3,16,128]{2,1,0:T(8,128)S(1)}, f32[3,16,128]{2,1,0:T(8,128)S(1)}, u32[]{:S(2)}, u32[]{:S(2)}) %collective-permute-start.21) | collective-permute-done | bytes 24608 | tf_op jit(solution)/shard_map/ppermute | solution.py:38
  113.2 5.1 %collective-permute-done.24 = bf16[4,128,128]{2,1,0:T(8,128)(2,1)S(1)} collective-permute-done((bf16[4,128,128]{2,1,0:T(8,128)(2,1)S(1)}, bf16[4,128,128]{2,1,0:T(8,128)(2,1)S(1)}, u32[]{:S(2)}, u32[]{:S(2)}) %collective-permute-start.24) | collective-permute-done | bytes 131104 | tf_op jit(solution)/shard_map/ppermute | solution.py:38
  126.3 7.7 %rotation.3 = bf16[128,256]{1,0:T(8,128)(2,1)S(1)} custom-call(s32[1]{0:T(128)} %bitcast.2.me_ref, f32[2,128,128]{2,1,0:T(8,128)S(1)} %pad_maximum_fusion.4.packed_ref), custom_call_target="tpu_custom_call" | custom-call | tf_op jit(solution)/shard_map/rotation/pallas_call | solution.py:280
  135.5 2.8 %collective-permute-done.29 = bf16[1,128,256]{2,1,0:T(8,128)(2,1)S(1)} collective-permute-done((bf16[1,128,256]{2,1,0:T(8,128)(2,1)S(1)}, bf16[1,128,256]{2,1,0:T(8,128)(2,1)S(1)}, u32[]{:S(2)}, u32[]{:S(2)}) %collective-permute-start.29) | collective-permute-done | bytes 65568 | tf_op jit(solution)/shard_map/ppermute | solution.py:38
  138.3 2.3 %collective-permute-start.30 = (bf16[2,128,256]{2,1,0:T(8,128)(2,1)S(1)}, bf16[2,128,256]{2,1,0:T(8,128)(2,1)S(1)}, u32[]{:S(2)}, u32[]{:S(2)}) collective-permute-start(bf16[2,128,256]{2,1,0:T(8,128)(2,1)S(1)} %pad_maximum_fusion.5), channel_id=1, source_target_pairs={{0,4},{1,5},{2,6},{3,7},{4,0},{5,1},{6,2},{7,3},{8,12},{9,13},{10,... | collective-permute-start | bytes 393224 | tf_op jit(solution)/shard_map/ppermute | solution.py:38
  140.6 2.6 %collective-permute-start.32 = (bf16[2,128,256]{2,1,0:T(8,128)(2,1)S(1)}, bf16[2,128,256]{2,1,0:T(8,128)(2,1)S(1)}, u32[]{:S(2)}, u32[]{:S(2)}) collective-permute-start(bf16[2,128,256]{2,1,0:T(8,128)(2,1)S(1)} %pad_maximum_fusion.5), channel_id=1, source_target_pairs={{0,12},{1,13},{2,14},{3,15},{4,8},{5,9},{6,10},{7,11},{8,4},{9,5},... | collective-permute-start | bytes 393224 | tf_op jit(solution)/shard_map/ppermute | solution.py:38
  144.2 9.4 %collective-permute-done.31 = bf16[2,128,256]{2,1,0:T(8,128)(2,1)S(1)} collective-permute-done((bf16[2,128,256]{2,1,0:T(8,128)(2,1)S(1)}, bf16[2,128,256]{2,1,0:T(8,128)(2,1)S(1)}, u32[]{:S(2)}, u32[]{:S(2)}) %collective-permute-start.31) | collective-permute-done | bytes 131104 | tf_op jit(solution)/shard_map/ppermute | solution.py:38
  155.7 2.9 %rotate_last.1 = bf16[512,2048]{1,0:T(8,128)(2,1)} custom-call(s32[16]{0:T(128)S(1)} %get-tuple-element.70.place_ref, s32[16]{0:T(128)S(1)} %get-tuple-element.163.home_ref, s32[1]{0:T(128)} %bitcast.2.me_ref, bf16[16,128,256]{2,1,0:T(8,128)(2,1)S(1)} %constant_dynamic-update-slice_fusion.16.gathered_ref, bf16[512,2048]{1,0:T(8,128)(2,1)S(1)} %get-tuple-element.121.cols_ref), custom_call_target="tpu_custom_call" | custom-call | tf_op jit(solution)/shard_map/rotate_last/pallas_call | solution.py:345
  (119 shorter events, 62.1 us)
Async XLA Ops:
  3.6 12.5 %collective-permute-start = (bf16[128,2048]{1,0:T(8,128)(2,1)}, bf16[128,2048]{1,0:T(8,128)(2,1)}, u32[]{:S(2)}, u32[]{:S(2)}) collective-permute-start(bf16[128,2048]{1,0:T(8,128)(2,1)} %get-tuple-element.74), channel_id=1, source_target_pairs={{0,1},{1,2},{2,3},{3,4},{4,5},{5,6},{6,7},{7,8},{8,9},{9,10},{10,1... | collective-permute-start | bytes 1572872 | tf_op jit(solution)/shard_map/ppermute | solution.py:442
  6.8 9.3 %collective-permute-start.1 = (bf16[128,2048]{1,0:T(8,128)(2,1)}, bf16[128,2048]{1,0:T(8,128)(2,1)}, u32[]{:S(2)}, u32[]{:S(2)}) collective-permute-start(bf16[128,2048]{1,0:T(8,128)(2,1)} %get-tuple-element.75), channel_id=1, source_target_pairs={{1,0},{2,1},{3,2},{4,3},{5,4},{6,5},{7,6},{8,7},{9,8},{10,9},{11,1... | collective-permute-start | bytes 1572872 | tf_op jit(solution)/shard_map/ppermute | solution.py:443
  19.2 6.0 %collective-permute-start.2 = (f32[3,16,128]{2,1,0:T(8,128)S(1)}, f32[3,16,128]{2,1,0:T(8,128)S(1)}, u32[]{:S(2)}, u32[]{:S(2)}) collective-permute-start(f32[3,16,128]{2,1,0:T(8,128)S(1)} %get-tuple-element.81), channel_id=1, source_target_pairs={{0,1},{1,0},{2,3},{3,2},{4,5},{5,4},{6,7},{7,6},{8,9},{9,8},{10,11... | collective-permute-start | bytes 73736 | tf_op jit(solution)/shard_map/ppermute | solution.py:38
  25.2 4.3 %collective-permute-start.3 = (f32[3,16,128]{2,1,0:T(8,128)S(1)}, f32[3,16,128]{2,1,0:T(8,128)S(1)}, u32[]{:S(2)}, u32[]{:S(2)}) collective-permute-start(f32[3,16,128]{2,1,0:T(8,128)S(1)} %add.60), channel_id=1, source_target_pairs={{0,2},{1,3},{2,0},{3,1},{4,6},{5,7},{6,4},{7,5},{8,10},{9,11},{10,... | collective-permute-start | bytes 73736 | tf_op jit(solution)/shard_map/ppermute | solution.py:38
  29.5 4.5 %collective-permute-start.4 = (f32[3,16,128]{2,1,0:T(8,128)S(1)}, f32[3,16,128]{2,1,0:T(8,128)S(1)}, u32[]{:S(2)}, u32[]{:S(2)}) collective-permute-start(f32[3,16,128]{2,1,0:T(8,128)S(1)} %add.61), channel_id=1, source_target_pairs={{0,4},{1,5},{2,6},{3,7},{4,0},{5,1},{6,2},{7,3},{8,12},{9,13},{10,... | collective-permute-start | bytes 73736 | tf_op jit(solution)/shard_map/ppermute | solution.py:38
  34.0 4.8 %collective-permute-start.5 = (f32[3,16,128]{2,1,0:T(8,128)S(1)}, f32[3,16,128]{2,1,0:T(8,128)S(1)}, u32[]{:S(2)}, u32[]{:S(2)}) collective-permute-start(f32[3,16,128]{2,1,0:T(8,128)S(1)} %add.62), channel_id=1, source_target_pairs={{0,8},{1,9},{2,10},{3,11},{4,12},{5,13},{6,14},{7,15},{8,0},{9,1},... | collective-permute-start | bytes 73736 | tf_op jit(solution)/shard_map/ppermute | solution.py:38
  45.0 5.8 %collective-permute-start.8 = (bf16[4,128,128]{2,1,0:T(8,128)(2,1)S(1)}, bf16[4,128,128]{2,1,0:T(8,128)(2,1)S(1)}, u32[]{:S(2)}, u32[]{:S(2)}) collective-permute-start(bf16[4,128,128]{2,1,0:T(8,128)(2,1)S(1)} %fusion), channel_id=1, source_target_pairs={{0,2},{1,3},{2,0},{3,1},{4,6},{5,7},{6,4},{7,5},{8,10},{9,11},{10,... | collective-permute-start | bytes 393224 | tf_op jit(solution)/shard_map/ppermute | solution.py:38
  50.9 4.7 %collective-permute-start.9 = (bf16[1,128,128]{2,1,0:T(8,128)(2,1)S(1)}, bf16[1,128,128]{2,1,0:T(8,128)(2,1)S(1)}, u32[]{:S(2)}, u32[]{:S(2)}) collective-permute-start(bf16[1,128,128]{2,1,0:T(8,128)(2,1)S(1)} %get-tuple-element.140), channel_id=1, source_target_pairs={{0,4},{1,5},{2,6},{3,7},{4,0},{5,1},{6,2},{7,3},{8,12},{9,13},{10,... | collective-permute-start | bytes 98312 | tf_op jit(solution)/shard_map/ppermute | solution.py:38
  52.9 6.0 %collective-permute-start.11 = (bf16[1,128,128]{2,1,0:T(8,128)(2,1)S(1)}, bf16[1,128,128]{2,1,0:T(8,128)(2,1)S(1)}, u32[]{:S(2)}, u32[]{:S(2)}) collective-permute-start(bf16[1,128,128]{2,1,0:T(8,128)(2,1)S(1)} %get-tuple-element.141), channel_id=1, source_target_pairs={{0,12},{1,13},{2,14},{3,15},{4,8},{5,9},{6,10},{7,11},{8,4},{9,5},... | collective-permute-start | bytes 98312 | tf_op jit(solution)/shard_map/ppermute | solution.py:38
  55.4 4.8 %collective-permute-start.10 = (bf16[1,128,128]{2,1,0:T(8,128)(2,1)S(1)}, bf16[1,128,128]{2,1,0:T(8,128)(2,1)S(1)}, u32[]{:S(2)}, u32[]{:S(2)}) collective-permute-start(bf16[1,128,128]{2,1,0:T(8,128)(2,1)S(1)} %get-tuple-element.142), channel_id=1, source_target_pairs={{0,8},{1,9},{2,10},{3,11},{4,12},{5,13},{6,14},{7,15},{8,0},{9,1},... | collective-permute-start | bytes 98312 | tf_op jit(solution)/shard_map/ppermute | solution.py:38
  67.9 4.3 %collective-permute-start.13 = (bf16[1,128,256]{2,1,0:T(8,128)(2,1)S(1)}, bf16[1,128,256]{2,1,0:T(8,128)(2,1)S(1)}, u32[]{:S(2)}, u32[]{:S(2)}) collective-permute-start(bf16[1,128,256]{2,1,0:T(8,128)(2,1)S(1)} %bitcast.32), channel_id=1, source_target_pairs={{0,2},{1,3},{2,0},{3,1},{4,6},{5,7},{6,4},{7,5},{8,10},{9,11},{10,... | collective-permute-start | bytes 196616 | tf_op jit(solution)/shard_map/ppermute | solution.py:38
  72.2 7.4 %collective-permute-start.14 = (bf16[2,128,256]{2,1,0:T(8,128)(2,1)S(1)}, bf16[2,128,256]{2,1,0:T(8,128)(2,1)S(1)}, u32[]{:S(2)}, u32[]{:S(2)}) collective-permute-start(bf16[2,128,256]{2,1,0:T(8,128)(2,1)S(1)} %pad_maximum_fusion.3), channel_id=1, source_target_pairs={{0,4},{1,5},{2,6},{3,7},{4,0},{5,1},{6,2},{7,3},{8,12},{9,13},{10,... | collective-permute-start | bytes 393224 | tf_op jit(solution)/shard_map/ppermute | solution.py:38
  72.5 14.0 %collective-permute-start.16 = (bf16[2,128,256]{2,1,0:T(8,128)(2,1)S(1)}, bf16[2,128,256]{2,1,0:T(8,128)(2,1)S(1)}, u32[]{:S(2)}, u32[]{:S(2)}) collective-permute-start(bf16[2,128,256]{2,1,0:T(8,128)(2,1)S(1)} %pad_maximum_fusion.3), channel_id=1, source_target_pairs={{0,12},{1,13},{2,14},{3,15},{4,8},{5,9},{6,10},{7,11},{8,4},{9,5},... | collective-permute-start | bytes 393224 | tf_op jit(solution)/shard_map/ppermute | solution.py:38
  74.0 12.4 %collective-permute-start.15 = (bf16[2,128,256]{2,1,0:T(8,128)(2,1)S(1)}, bf16[2,128,256]{2,1,0:T(8,128)(2,1)S(1)}, u32[]{:S(2)}, u32[]{:S(2)}) collective-permute-start(bf16[2,128,256]{2,1,0:T(8,128)(2,1)S(1)} %pad_maximum_fusion.3), channel_id=1, source_target_pairs={{0,8},{1,9},{2,10},{3,11},{4,12},{5,13},{6,14},{7,15},{8,0},{9,1},... | collective-permute-start | bytes 393224 | tf_op jit(solution)/shard_map/ppermute | solution.py:38
  93.8 3.9 %collective-permute-start.19 = (f32[3,16,128]{2,1,0:T(8,128)S(1)}, f32[3,16,128]{2,1,0:T(8,128)S(1)}, u32[]{:S(2)}, u32[]{:S(2)}) collective-permute-start(f32[3,16,128]{2,1,0:T(8,128)S(1)} %add.70), channel_id=1, source_target_pairs={{0,2},{1,3},{2,0},{3,1},{4,6},{5,7},{6,4},{7,5},{8,10},{9,11},{10,... | collective-permute-start | bytes 73736 | tf_op jit(solution)/shard_map/ppermute | solution.py:38
  101.6 4.7 %collective-permute-start.21 = (f32[3,16,128]{2,1,0:T(8,128)S(1)}, f32[3,16,128]{2,1,0:T(8,128)S(1)}, u32[]{:S(2)}, u32[]{:S(2)}) collective-permute-start(f32[3,16,128]{2,1,0:T(8,128)S(1)} %add.72), channel_id=1, source_target_pairs={{0,8},{1,9},{2,10},{3,11},{4,12},{5,13},{6,14},{7,15},{8,0},{9,1},... | collective-permute-start | bytes 73736 | tf_op jit(solution)/shard_map/ppermute | solution.py:38
  112.5 5.8 %collective-permute-start.24 = (bf16[4,128,128]{2,1,0:T(8,128)(2,1)S(1)}, bf16[4,128,128]{2,1,0:T(8,128)(2,1)S(1)}, u32[]{:S(2)}, u32[]{:S(2)}) collective-permute-start(bf16[4,128,128]{2,1,0:T(8,128)(2,1)S(1)} %fusion.1), channel_id=1, source_target_pairs={{0,2},{1,3},{2,0},{3,1},{4,6},{5,7},{6,4},{7,5},{8,10},{9,11},{10,... | collective-permute-start | bytes 393224 | tf_op jit(solution)/shard_map/ppermute | solution.py:38
  118.4 4.0 %collective-permute-start.25 = (bf16[1,128,128]{2,1,0:T(8,128)(2,1)S(1)}, bf16[1,128,128]{2,1,0:T(8,128)(2,1)S(1)}, u32[]{:S(2)}, u32[]{:S(2)}) collective-permute-start(bf16[1,128,128]{2,1,0:T(8,128)(2,1)S(1)} %get-tuple-element.137), channel_id=1, source_target_pairs={{0,4},{1,5},{2,6},{3,7},{4,0},{5,1},{6,2},{7,3},{8,12},{9,13},{10,... | collective-permute-start | bytes 98312 | tf_op jit(solution)/shard_map/ppermute | solution.py:38
  118.5 5.8 %collective-permute-start.27 = (bf16[1,128,128]{2,1,0:T(8,128)(2,1)S(1)}, bf16[1,128,128]{2,1,0:T(8,128)(2,1)S(1)}, u32[]{:S(2)}, u32[]{:S(2)}) collective-permute-start(bf16[1,128,128]{2,1,0:T(8,128)(2,1)S(1)} %get-tuple-element.138), channel_id=1, source_target_pairs={{0,12},{1,13},{2,14},{3,15},{4,8},{5,9},{6,10},{7,11},{8,4},{9,5},... | collective-permute-start | bytes 98312 | tf_op jit(solution)/shard_map/ppermute | solution.py:38
  120.1 4.8 %collective-permute-start.26 = (bf16[1,128,128]{2,1,0:T(8,128)(2,1)S(1)}, bf16[1,128,128]{2,1,0:T(8,128)(2,1)S(1)}, u32[]{:S(2)}, u32[]{:S(2)}) collective-permute-start(bf16[1,128,128]{2,1,0:T(8,128)(2,1)S(1)} %get-tuple-element.139), channel_id=1, source_target_pairs={{0,8},{1,9},{2,10},{3,11},{4,12},{5,13},{6,14},{7,15},{8,0},{9,1},... | collective-permute-start | bytes 98312 | tf_op jit(solution)/shard_map/ppermute | solution.py:38
  134.0 4.3 %collective-permute-start.29 = (bf16[1,128,256]{2,1,0:T(8,128)(2,1)S(1)}, bf16[1,128,256]{2,1,0:T(8,128)(2,1)S(1)}, u32[]{:S(2)}, u32[]{:S(2)}) collective-permute-start(bf16[1,128,256]{2,1,0:T(8,128)(2,1)S(1)} %bitcast.34), channel_id=1, source_target_pairs={{0,2},{1,3},{2,0},{3,1},{4,6},{5,7},{6,4},{7,5},{8,10},{9,11},{10,... | collective-permute-start | bytes 196616 | tf_op jit(solution)/shard_map/ppermute | solution.py:38
  138.3 5.9 %collective-permute-start.30 = (bf16[2,128,256]{2,1,0:T(8,128)(2,1)S(1)}, bf16[2,128,256]{2,1,0:T(8,128)(2,1)S(1)}, u32[]{:S(2)}, u32[]{:S(2)}) collective-permute-start(bf16[2,128,256]{2,1,0:T(8,128)(2,1)S(1)} %pad_maximum_fusion.5), channel_id=1, source_target_pairs={{0,4},{1,5},{2,6},{3,7},{4,0},{5,1},{6,2},{7,3},{8,12},{9,13},{10,... | collective-permute-start | bytes 393224 | tf_op jit(solution)/shard_map/ppermute | solution.py:38
  140.6 13.0 %collective-permute-start.32 = (bf16[2,128,256]{2,1,0:T(8,128)(2,1)S(1)}, bf16[2,128,256]{2,1,0:T(8,128)(2,1)S(1)}, u32[]{:S(2)}, u32[]{:S(2)}) collective-permute-start(bf16[2,128,256]{2,1,0:T(8,128)(2,1)S(1)} %pad_maximum_fusion.5), channel_id=1, source_target_pairs={{0,12},{1,13},{2,14},{3,15},{4,8},{5,9},{6,10},{7,11},{8,4},{9,5},... | collective-permute-start | bytes 393224 | tf_op jit(solution)/shard_map/ppermute | solution.py:38
  143.2 10.4 %collective-permute-start.31 = (bf16[2,128,256]{2,1,0:T(8,128)(2,1)S(1)}, bf16[2,128,256]{2,1,0:T(8,128)(2,1)S(1)}, u32[]{:S(2)}, u32[]{:S(2)}) collective-permute-start(bf16[2,128,256]{2,1,0:T(8,128)(2,1)S(1)} %pad_maximum_fusion.5), channel_id=1, source_target_pairs={{0,8},{1,9},{2,10},{3,11},{4,12},{5,13},{6,14},{7,15},{8,0},{9,1},... | collective-permute-start | bytes 393224 | tf_op jit(solution)/shard_map/ppermute | solution.py:38
  (14 other events, 36.3 us)

commit v3 on v2

--- a/solution.py
+++ b/solution.py
@@ -17,12 +17,12 @@
 VMEM = pl.BlockSpec(memory_space=pltpu.VMEM)
 SMEM = pl.BlockSpec(memory_space=pltpu.SMEM)
 TILE = 512
-SMALL = 3e-8
+SMALL = 1e-6
 WIRE = BF16
 
 
-def params():
-    return pltpu.CompilerParams(vmem_limit_bytes=VMEM_LIMIT)
+def params(limit=VMEM_LIMIT):
+    return pltpu.CompilerParams(vmem_limit_bytes=limit)
 
 
 def bits_of(count):
@@ -49,26 +49,38 @@
             diag_ref[component, spot, :] += piece
 
 
-def edge_rows_kernel(last_ref, first_ref, last_out_ref, first_out_ref):
-    last_out_ref[...] = last_ref[...]
-    first_out_ref[...] = first_ref[...]
+def edge_rows_kernel(orbitals_ref, last_ref, first_ref, held_ref, sems):
+    row_count = orbitals_ref.shape[0]
+    spots = (orbitals_ref.at[row_count - BLK :], orbitals_ref.at[:BLK])
+    loads = [pltpu.make_async_copy(spots[i], held_ref.at[i], sems.at[i]) for i in (0, 1)]
+    stores = [
+        pltpu.make_async_copy(held_ref.at[i], (last_ref, first_ref)[i], sems.at[2 + i])
+        for i in (0, 1)
+    ]
+    for load in loads:
+        load.start()
+    for load, store in zip(loads, stores):
+        load.wait()
+        store.start()
+    for store in stores:
+        store.wait()
 
 
 def edge_rows(orbitals):
-    row_count, orb_count = orbitals.shape
-    shape = jax.ShapeDtypeStruct((BLK, orb_count), BF16)
+    shape = jax.ShapeDtypeStruct((BLK, orbitals.shape[1]), BF16)
+    hbm = pl.BlockSpec(memory_space=pltpu.HBM)
     return pl.pallas_call(
         edge_rows_kernel,
         out_shape=(shape, shape),
-        grid=(1,),
-        in_specs=[
-            pl.BlockSpec((BLK, orb_count), lambda i: (row_count // BLK - 1, 0)),
-            pl.BlockSpec((BLK, orb_count), lambda i: (0, 0)),
+        in_specs=[hbm],
+        out_specs=(hbm, hbm),
+        scratch_shapes=[
+            pltpu.VMEM((2, BLK, orbitals.shape[1]), BF16),
+            pltpu.SemaphoreType.DMA((4,)),
         ],
-        out_specs=(VMEM, VMEM),
-        compiler_params=params(),
+        compiler_params=params(56 * 1024 * 1024),
         name="edge_rows",
-    )(orbitals, orbitals)
+    )(orbitals)
 
 
 def inner_kernel(block_rows, blocks_ref, cols_ref, image_ref, diag_ref):
@@ -159,68 +171,105 @@
     return jnp.concatenate([edge[:BLK], inner, edge[BLK:]], axis=0)
 
 
-def gram_kernel(first, place_ref, cols_ref, *refs):
-    image_refs, mats_ref = refs[:-1], refs[-1]
-    for i in range(mats_ref.shape[0]):
+def gram_kernel(first, place_ref, me_ref, cols_ref, *refs):
+    image_refs, keep_ref, send_ref = refs[:-2], refs[-2], refs[-1]
+    mine = (me_ref[0] & 1) == 0
+    low = lower_mask()
+    for i in range(keep_ref.shape[0]):
         places = [place_ref[2 * (first + i) + h] for h in (0, 1)]
         cols = pair_columns(cols_ref, (), places)
         images = jnp.concatenate([pair_image(image_refs, k, places) for k in range(3)], axis=1)
-        mats_ref[i] = lax.dot_general(
-            cols, images, (((0,), (0,)), ((), ())), preferred_element_type=F32
-        )
-
-
-def pair_products(place, cols, images, first, count):
+        mats = lax.dot_general(cols, images, (((0,), (0,)), ((), ())), preferred_element_type=F32)
+        for k in range(3):
+            mat = mats[:, k * PAIR : (k + 1) * PAIR]
+            one, two = mat[:HALF, :HALF], mat[HALF:, HALF:]
+            cross = mat[:HALF, HALF:] + mat[HALF:, :HALF].T
+            within = jnp.where(low, one, two) + jnp.where(low, two, one).T
+            keep_ref[i, k] = jnp.where(mine, cross, within)
+            send_ref[i, k] = jnp.where(mine, within, cross)
+
+
+def pair_products(place, me, cols, images, first, count):
+    shape = jax.ShapeDtypeStruct((count, 3, HALF, HALF), F32)
     return pl.pallas_call(
         functools.partial(gram_kernel, first),
-        out_shape=jax.ShapeDtypeStruct((count, PAIR, 3 * PAIR), F32),
-        in_specs=[SMEM] + [VMEM] * (1 + len(images)),
-        out_specs=VMEM,
+        out_shape=(shape, shape),
+        in_specs=[SMEM, SMEM] + [VMEM] * (1 + len(images)),
+        out_specs=(VMEM, VMEM),
         compiler_params=params(),
         name="pair_products",
-    )(place, cols, *images)
-
-
-def weight_kernel(first, place_ref, me_ref, diag_ref, *refs):
-    mats_refs, keep_ref, send_ref = refs[:-2], refs[-2], refs[-1]
-    mine = (me_ref[0] & 1) == 0
-    low = lower_mask()
-    p = 0
-    for mats_ref in mats_refs:
-        for i in range(mats_ref.shape[0]):
+    )(place, me, cols, *images)
+
+
+def weight_kernel(sub_bits, place_ref, me_ref, diag_ref, *refs):
+    sums_refs, keep_ref, send_ref = refs[:-2], refs[-2], refs[-1]
+    kept_refs, came_refs = sums_refs[: len(sums_refs) // 2], sums_refs[len(sums_refs) // 2 :]
+    core = me_ref[0] & 1
+    bit = (me_ref[0] >> sub_bits) & 1
+    rows = lax.broadcasted_iota(jnp.int32, (HALF, HALF), 0)
+    cols = lax.broadcasted_iota(jnp.int32, (HALF, HALF), 1)
+    low = jnp.where(rows > cols, 1, 0)
+    col_first = jnp.maximum(low, 1 - core) > 0
+    row_first = jnp.minimum(low, core) > 0
+    step = kept_refs[0].shape[0]
+    for j in range(keep_ref.shape[0]):
+        for stays in (True, False):
+            odd = bit if stays else 1 - bit
+            pair = 2 * j + odd
+            i = 2 * j % step + odd
+            kept_ref, came_ref = kept_refs[2 * j // step], came_refs[2 * j // step]
             halves = [
-                [diag_ref[k, pl.ds(place_ref[2 * (first + p) + h], 1), :] for k in range(3)] for h in (0, 1)
+                [diag_ref[k, pl.ds(place_ref[2 * pair + h], 1), :] for k in range(3)]
+                for h in (0, 1)
             ]
-            turned = jnp.concatenate(
-                [jnp.concatenate(half + half + half[:2], axis=0).T for half in halves], axis=0
-            )
-            total = jnp.zeros((PAIR, PAIR), F32)
+            first, second = [
+                jnp.concatenate(half + half + half[:2], axis=0).T for half in halves
+            ]
+            total = jnp.zeros((HALF, HALF), F32)
             for k in range(3):
-                row = jnp.concatenate([half[k] for half in halves], axis=1)
-                total += mats_ref[i, :, k * PAIR : (k + 1) * PAIR] * (turned[:, k : k + 1] - row)
-            one, two = total[:HALF, :HALF], total[HALF:, HALF:]
-            cross = total[:HALF, HALF:] - total[HALF:, :HALF].T
-            within = jnp.where(low, one, two) - jnp.where(low, two, one).T
-            keep_ref[p] = jnp.where(mine, cross, within)
-            send_ref[p] = jnp.where(mine, within, cross)
-            p += 1
-
-
-def weigh(place, me, diag, mats, first):
-    pair_count = sum(mat.shape[0] for mat in mats)
-    shape = jax.ShapeDtypeStruct((pair_count, HALF, HALF), F32)
-    return pl.pallas_call(
-        functools.partial(weight_kernel, first),
-        out_shape=(shape, shape),
-        in_specs=[SMEM, SMEM] + [VMEM] * (1 + len(mats)),
+                col = jnp.where(col_first, first[:, k : k + 1], second[:, k : k + 1])
+                row = jnp.where(row_first, halves[0][k], halves[1][k])
+                total += (kept_ref[i, k] + came_ref[i, k]) * (col - row)
+            if stays:
+                keep_ref[j] = total
+            else:
+                send_ref[j] = total.astype(BF16)
+
+
+def weigh(place, me, diag, kept, came, sub_bits):
+    high = sum(part.shape[0] for part in kept) // 2
+    return pl.pallas_call(
+        functools.partial(weight_kernel, sub_bits),
+        out_shape=(
+            jax.ShapeDtypeStruct((high, HALF, HALF), F32),
+            jax.ShapeDtypeStruct((high, HALF, HALF), BF16),
+        ),
+        in_specs=[SMEM, SMEM] + [VMEM] * (1 + 2 * len(kept)),
         out_specs=(VMEM, VMEM),
         compiler_params=params(),
         name="weigh",
-    )(place, me, diag, *mats)
+    )(place, me, diag, *kept, *came)
 
 
 def matmul(left, right):
     return jnp.dot(left, right, precision=lax.Precision.HIGHEST, preferred_element_type=F32)
+
+
+def parts_of(value):
+    high = value.astype(BF16)
+    return high, (value - high.astype(F32)).astype(BF16)
+
+
+def by_parts(left, right):
+    left_high, left_low = parts_of(left)
+    right_high, right_low = parts_of(right)
+    rows = left.shape[0]
+    both = jnp.dot(
+        jnp.concatenate([left_high, left_low], axis=0), right_high, preferred_element_type=F32
+    )
+    return both[:rows] + (
+        both[rows:] + jnp.dot(left_high, right_low, preferred_element_type=F32)
+    )
 
 
 def rotation_kernel(scale, subs, me_ref, packed_ref, out_ref, sum_ref, power_ref):
@@ -264,8 +313,20 @@
 
         return step + 1, left * left
 
+    def quick_going(state):
+        return jnp.logical_and(bound < 16.0, going(state))
+
+    def quick_body(state):
+        step, left = state
+        power = power_ref[...]
+        both = by_parts(jnp.concatenate([sum_ref[...], power], axis=0), power)
+        sum_ref[...] += both[:PAIR]
+        power_ref[...] = both[PAIR:]
+        return step + 1, left * left
+
     reach = bound / (2.0 + bound)
-    lax.while_loop(going, body, (jnp.int32(0), reach * reach))
+    state = lax.while_loop(quick_going, quick_body, (jnp.int32(0), reach * reach))
+    lax.while_loop(going, body, state)
     result = 2.0 * matmul(eye + half_gen, sum_ref[...]) - eye
     share = PAIR // subs
     for i in range(subs):
@@ -288,20 +349,24 @@
     )(me, packed)
 
 
-def assemble(gathered_ref, me, pair_count, pair):
+def assemble(gathered_ref, me, slot):
     subs = PAIR // gathered_ref.shape[1]
-    my_sub, my_pair = me & (subs - 1), me // subs
+    slots = gathered_ref.shape[0] // subs
+    my_sub = me & (subs - 1)
     return jnp.concatenate(
-        [gathered_ref[(i ^ my_sub) * pair_count + (pair ^ my_pair)] for i in range(subs)], axis=0
-    )
-
-
-def rotate_kernel(pair_count, place_ref, me_ref, gathered_ref, cols_ref, *refs):
-    image_refs, (out_ref, image_ref, diag_ref) = refs[:-3], refs[-3:]
-    for p in range(pair_count):
-        rotation = assemble(gathered_ref, me_ref[0], pair_count, p)
+        [gathered_ref[(i ^ my_sub) * slots + slot] for i in range(subs)], axis=0
+    )
+
+
+def rotate_kernel(first, earlier, place_ref, me_ref, gathered_ref, cols_ref, *refs):
+    subs = PAIR // gathered_ref.shape[1]
+    my_pair = me_ref[0] // subs
+    image_refs, (out_ref, image_ref, diag_ref) = refs[: -3 - earlier], refs[-3:]
+    for slot in range(gathered_ref.shape[0] // subs):
+        p = my_pair ^ (first + slot)
+        rotation = assemble(gathered_ref, me_ref[0], slot)
         places = [place_ref[2 * p + h] for h in (0, 1)]
-        spot = slice(p * PAIR, (p + 1) * PAIR)
+        spot = pl.ds(pl.multiple_of(p * PAIR, PAIR), PAIR)
         cols = pair_columns(cols_ref, (), places)
         turned = jnp.dot(cols, rotation, preferred_element_type=F32).astype(BF16)
         out_ref[:, spot] = turned
@@ -312,51 +377,61 @@
             put_diag(diag_ref, k, 2 * p, turned, moved, True)
 
 
-def rotate(place, me, gathered, cols, images):
+def rotate(place, me, gathered, cols, images, first, earlier):
     row_count, orb_count = cols.shape
-    return pl.pallas_call(
-        functools.partial(rotate_kernel, orb_count // PAIR),
+    operands = [place, me, gathered, cols, *images]
+    return pl.pallas_call(
+        functools.partial(rotate_kernel, first, len(earlier)),
         out_shape=(
             jax.ShapeDtypeStruct((row_count, orb_count), BF16),
             jax.ShapeDtypeStruct((3, row_count, orb_count), BF16),
             jax.ShapeDtypeStruct((3, orb_count // HALF, HALF), F32),
         ),
-        in_specs=[SMEM, SMEM] + [VMEM] * (2 + len(images)),
+        in_specs=[SMEM, SMEM] + [VMEM] * (2 + len(images) + len(earlier)),
         out_specs=(VMEM, VMEM, VMEM),
+        cost_estimate=pl.CostEstimate(
+            flops=8 * row_count * PAIR * PAIR * gathered.shape[0] * gathered.shape[1] // PAIR,
+            bytes_accessed=8 * row_count * orb_count,
+            transcendentals=0,
+        ),
+        input_output_aliases={len(operands) + i: i for i in range(len(earlier))},
         compiler_params=params(),
         name="rotate",
-    )(place, me, gathered, cols, *images)
-
-
-def last_kernel(pair_count, place_ref, home_ref, me_ref, gathered_ref, cols_ref, out_ref):
-    for p in range(pair_count):
-        rotation = assemble(gathered_ref, me_ref[0], pair_count, p)
-        places = [place_ref[2 * p + h] for h in (0, 1)]
-        cols = pair_columns(cols_ref, (), places)
-        turned = jnp.dot(cols, rotation, preferred_element_type=F32).astype(BF16)
-        for h in (0, 1):
-            home = pl.multiple_of(home_ref[2 * p + h] * HALF, HALF)
-            out_ref[:, pl.ds(home, HALF)] = turned[:, h * HALF : (h + 1) * HALF]
+    )(*operands, *earlier)
+
+
+def last_kernel(parts, place_ref, home_ref, me_ref, *refs):
+    gathered_refs, (cols_ref, out_ref) = refs[:parts], refs[parts:]
+    subs = PAIR // gathered_refs[0].shape[1]
+    my_pair = me_ref[0] // subs
+    done = 0
+    for gathered_ref in gathered_refs:
+        for slot in range(gathered_ref.shape[0] // subs):
+            p = my_pair ^ done
+            done += 1
+            rotation = assemble(gathered_ref, me_ref[0], slot)
+            places = [place_ref[2 * p + h] for h in (0, 1)]
+            cols = pair_columns(cols_ref, (), places)
+            turned = jnp.dot(cols, rotation, preferred_element_type=F32).astype(BF16)
+            for h in (0, 1):
+                home = pl.multiple_of(home_ref[2 * p + h] * HALF, HALF)
+                out_ref[:, pl.ds(home, HALF)] = turned[:, h * HALF : (h + 1) * HALF]
 
 
 def rotate_last(place, home, me, gathered, cols):
     row_count, orb_count = cols.shape
     rows = row_count // 2
     return pl.pallas_call(
-        functools.partial(last_kernel, orb_count // PAIR),
+        functools.partial(last_kernel, len(gathered)),
         out_shape=jax.ShapeDtypeStruct((row_count, orb_count), BF16),
         grid=(row_count // rows,),
-        in_specs=[
-            SMEM,
-            SMEM,
-            SMEM,
-            pl.BlockSpec(gathered.shape, lambda r: (0, 0, 0)),
-            pl.BlockSpec((rows, orb_count), lambda r: (r, 0)),
-        ],
+        in_specs=[SMEM, SMEM, SMEM]
+        + [pl.BlockSpec(part.shape, lambda r: (0, 0, 0)) for part in gathered]
+        + [pl.BlockSpec((rows, orb_count), lambda r: (r, 0))],
         out_specs=pl.BlockSpec((rows, orb_count), lambda r: (r, 0)),
         compiler_params=params(),
         name="rotate_last",
-    )(place, home, me, gathered, cols)
+    )(place, home, me, *gathered, cols)
 
 
 def sum_beside(diag, makers):
@@ -364,15 +439,15 @@
     hops = bits_of(lax.axis_size("orb"))
     for bit in range(hops):
         arrived = swap(diag, 1 << bit)
-        if bit < len(makers):
-            diag, arrived, product = lax.optimization_barrier((diag, arrived, makers[bit](diag)))
+        for maker in makers.get(bit, ()):
+            diag, arrived, product = lax.optimization_barrier((diag, arrived, maker(diag)))
             made.append(product)
         diag = diag + arrived
     return diag, made
 
 
 def places_of(position, sub_bits, pair_bits):
-    steps = [(bit, 1) for bit in range(1, sub_bits)] + [(sub_bits, 1), (sub_bits + 1, pair_bits - 1)]
+    steps = [(bit, 1) for bit in range(1, sub_bits)] + [(sub_bits + 1, pair_bits - 1)]
     found = {}
     for low_bit, bits in steps:
         mine = (position >> low_bit) & ((1 << bits) - 1)
@@ -396,16 +471,13 @@
     return own
 
 
-def reduce_pairs(value, places, sub_bits):
-    pair_count = value.shape[0]
+def reduce_pairs(keep, send, places, sub_bits):
+    value = keep + swap(send, 1 << sub_bits).astype(F32)
+    high = value.shape[0]
     for bit in range(1, sub_bits):
         rows = value.shape[1] // 2
-        value = jnp.swapaxes(value.reshape(pair_count, 2, rows, HALF), 0, 1)
-        value = spread(value.reshape(2 * pair_count, rows, HALF), places[bit], bit, F32)
-    rows = value.shape[1]
-    value = value.reshape(pair_count // 2, 2, rows, HALF)
-    value = jnp.swapaxes(value, 0, 1).reshape(pair_count, rows, HALF)
-    value = spread(value, places[sub_bits], sub_bits, BF16)
+        value = jnp.swapaxes(value.reshape(high, 2, rows, HALF), 0, 1)
+        value = spread(value.reshape(2 * high, rows, HALF), places[bit], bit, F32)
     return spread(value, places[sub_bits + 1], sub_bits + 1, WIRE)[0]
 
 
@@ -413,6 +485,24 @@
     return jnp.concatenate(
         [value] + [swap(value, q << low_bit) for q in range(1, 1 << bits)], axis=0
     )
+
+
+def gather_pairs(share, sub_bits, pair_bits):
+    beside = 1 << sub_bits
+    ways = 1 << (pair_bits - 1)
+    away = {q: swap(share, q * 2 * beside) for q in range(ways - 1, 0, -1)}
+    away[0] = share
+    across = {q: swap(away[q], beside) for q in range(ways // 2)}
+    across, away = lax.optimization_barrier((across, away))
+    later = swap(jnp.concatenate([away[q] for q in range(ways // 2, ways)], axis=0), beside)
+    near = jnp.concatenate([part[q] for q in range(ways // 2) for part in (away, across)], axis=0)
+    for bit in range(sub_bits):
+        near = gather_bits(near, 1, bit)
+    later, near = lax.optimization_barrier((later, near))
+    far = []
+    for q in range(ways // 2, ways):
+        far += [away[q], later[q - ways // 2 : q - ways // 2 + 1]]
+    return near, jnp.concatenate(far, axis=0)
 
 
 def per_device(orbitals, dipole_blocks, coupling_mask, matchings):
@@ -424,6 +514,10 @@
     sub_bits = bits_of(count) - pair_bits
     basis_count = row_count * count
     block_rows = row_count // BLK
+    last, first = edge_rows(orbitals)
+    orbitals, matchings, last, first = lax.optimization_barrier(
+        (orbitals, matchings, last, first)
+    )
     position = lax.axis_index("orb").astype(jnp.int32)
     places = places_of(position, sub_bits, pair_bits)
     ident = jnp.arange(block_count, dtype=jnp.int32)
@@ -432,13 +526,11 @@
     for r in range(ROUNDS):
         found = jnp.where(matchings[r][:, None] == held[r][None, :], ident[None, :], 0)
         spots.append(jnp.sum(found, axis=1).astype(jnp.int32))
+    forward = [(i, i + 1) for i in range(count - 1)]
+    backward = [(i + 1, i) for i in range(count - 1)]
     orbitals, places, spots, me = lax.optimization_barrier(
         (orbitals, places, spots, position.reshape(1))
     )
-
-    forward = [(i, i + 1) for i in range(count - 1)]
-    backward = [(i + 1, i) for i in range(count - 1)]
-    last, first = edge_rows(orbitals)
     low = lax.ppermute(last, "orb", forward)
     high = lax.ppermute(first, "orb", backward)
     mask_full = jnp.stack(
@@ -458,29 +550,29 @@
 
         def product(start, token):
             held_cols, _ = lax.optimization_barrier((cols, token))
-            return pair_products(place, held_cols, images, start, step)
-
-        makers = [functools.partial(product, i * step) for i in range(splits)]
-        diag_sum, mats = sum_beside(diag, makers)
-        half = splits // 2
-        keep_a, send_a = weigh(place, me, diag_sum, mats[:half], 0)
-        came_a = swap(send_a, 1)
-        keep_b, send_b = weigh(place, me, diag_sum, mats[half:], half * step)
-        came_a, keep_b, send_b = lax.optimization_barrier((came_a, keep_b, send_b))
-        value = jnp.concatenate([keep_a + came_a, keep_b + swap(send_b, 1)], axis=0)
-        own = reduce_pairs(value, places, sub_bits)
+            return pair_products(place, me, held_cols, images, start, step)
+
+        made = [functools.partial(product, i * step) for i in range(splits)]
+        makers = {0: made[:1], 1: made[1:3], 2: made[3:]}
+        diag_sum, made = sum_beside(diag, makers)
+        kept = [keep for keep, _ in made]
+        came = [swap(send, 1) for _, send in made]
+        keep, send = weigh(place, me, diag_sum, kept, came, sub_bits)
+        own = reduce_pairs(keep, send, places, sub_bits)
         packed = own[None]
         for bit in range(sub_bits):
             packed = gather_bits(packed, 1, bit)
         share = rotation_share(0.01 / basis_count, me, packed)
-        gathered = gather_bits(share[None], 1, sub_bits)
-        gathered = gather_bits(gathered, pair_bits - 1, sub_bits + 1)
+        near, far = gather_pairs(share[None], sub_bits, pair_bits)
+        if round_index + 1 < ROUNDS:
+            earlier = rotate(place, me, near, cols, images, 0, ())
         for bit in range(sub_bits):
-            gathered = gather_bits(gathered, 1, bit)
+            far = gather_bits(far, 1, bit)
         if round_index + 1 < ROUNDS:
-            cols, moved, diag = rotate(place, me, gathered, cols, images)
+            half = pair_count // 2
+            cols, moved, diag = rotate(place, me, far, cols, images, half, earlier)
             images = (moved,)
-    return rotate_last(place, matchings[ROUNDS - 1], me, gathered, cols)
+    return rotate_last(place, matchings[ROUNDS - 1], me, (near, far), cols)
 
 
 def solution(mesh):

time: 161 us -> 144 us (0.89); the launches traced: 159 us -> 146 us
  waiting for transfers between devices: 62.4 us -> 50.3 us
  local copies, waits for them, and re-layouts: 8.54 us -> 5.98 us
    ppermute x32 -> x42, waiting for transfers between devices: 62.4 us -> 50.3 us  [swap(): return lax.ppermute(block, 'orb', [(i, i ^ distance) for i in range(count)])]
    pallas_call x2, Pallas kernels: 14 us -> 16.4 us  [rotation_share(): pl.pallas_call(functools.partial(rotation_kernel, scale, subs), out_shape...]
    pallas_call x15 -> x14, Pallas kernels: 27 us -> 25.4 us  [the longest x8 12 us: pair_products(): pl.pallas_call(functools.partial(gram_kernel, first), out_shape=(shape, s...]
    ppermute x32 -> x42, starting transfers between devices: 36 us -> 36.9 us  [swap(): return lax.ppermute(block, 'orb', [(i, i ^ distance) for i in range(count)])]
  transfers between devices with their start and end apart: 34 -> 44, of which waited for: 25 -> 25; matrix products, arithmetic and copies ran while one was open for 4% -> 4% of each run, Pallas kernels for 11% -> 9%
where the time goes in v3:
time: 144 us; the launch traced here: 146 us
  waiting for transfers between devices  50.3 us (35%)
  Pallas kernels  46.8 us (32%)
  starting transfers between devices  41.3 us (29%)
  local copies, waits for them, and re-layouts  5.98 us (4%)
    ppermute x42, waiting for transfers between devices, swap(): return lax.ppermute(block, 'orb', [(i, i ^ distance) for i in range(count)])  50.3 us
    ppermute x42, starting transfers between devices, swap(): return lax.ppermute(block, 'orb', [(i, i ^ distance) for i in range(count)])  36.9 us
    pallas_call x2, Pallas kernels, rotation_share(): pl.pallas_call(functools.partial(rotation_kernel, scale, subs), out_shape...  16.4 us
    pallas_call x8, Pallas kernels, pair_products(): pl.pallas_call(functools.partial(gram_kernel, first), out_shape=(shape, s...  12 us
    pallas_call x2, Pallas kernels, rotate(): pl.pallas_call(functools.partial(rotate_kernel, first, len(earlier)), out...  4.38 us
    pallas_call x2, Pallas kernels, weigh(): pl.pallas_call(functools.partial(weight_kernel, sub_bits), out_shape=(jax...  3.97 us
    reshape x1, local copies, waits for them, and re-layouts, per_device(): blocks = jnp.transpose(dipole_blocks * mask_full[None, :, :, None, None],...  3.36 us
    ppermute x1, starting transfers between devices, per_device(): low = lax.ppermute(last, 'orb', forward)  3.16 us
  transfers between devices with their start and end apart: 44, of which 25 were waited for; matrix products, arithmetic and copies ran while one was open for 4% of the time, Pallas kernels for 9%

profile of v3, /device:TPU:0, one launch (start us, length us, event | category | flops | bytes accessed | tf_op | source)
XLA Modules:
  0.0 145.8 jit_solution(12179675352249139970)
XLA Ops:
  0.0 2.2 %edge_rows.1 = (bf16[128,2048]{1,0:T(8,128)(2,1)}, bf16[128,2048]{1,0:T(8,128)(2,1)}) custom-call(bf16[512,2048]{1,0:T(8,128)(2,1)} %cols_ref.7), custom_call_target="tpu_custom_call" | custom-call | tf_op jit(solution)/shard_map/edge_rows/pallas_call | solution.py:72
  2.2 3.2 %collective-permute-start = (bf16[128,2048]{1,0:T(8,128)(2,1)}, bf16[128,2048]{1,0:T(8,128)(2,1)}, u32[]{:S(2)}, u32[]{:S(2)}) collective-permute-start(bf16[128,2048]{1,0:T(8,128)(2,1)} %get-tuple-element.113), channel_id=1, source_target_pairs={{0,1},{1,2},{2,3},{3,4},{4,5},{5,6},{6,7},{7,8},{8,9},{9,10},{10,1... | collective-permute-start | bytes 1572872 | tf_op jit(solution)/shard_map/ppermute | solution.py:534
  9.5 3.4 %reshape.58.blocks_ref = bf16[4,384,384]{2,1,0:T(8,128)(2,1)S(1)} reshape(bf16[4,3,128,3,128]{4,3,2,1,0:T(4,128)(2,1)} %copy.13) | data formatting | bytes 2359296 | tf_op jit(solution)/shard_map/reshape | solution.py:541
  14.8 3.1 %edge_images.1 = (bf16[3,256,2048]{2,1,0:T(8,128)(2,1)S(1)}, f32[3,16,128]{2,1,0:T(8,128)S(1)}) custom-call(bf16[4,384,384]{2,1,0:T(8,128)(2,1)S(1)} %reshape.58.blocks_ref, bf16[512,2048]{1,0:T(8,128)(2,1)S(1)} %copy-done, bf16[128,2048]{1,0:T(8,128)(2,1)} %collective-permute-done.low_ref, bf16[128,2048]{1,0:T(8,128)(2,1)} %collective-permute-done.1.high_ref, ...), custom_call_target="tpu_custom_call" | custom-call | tf_op jit(solution)/shard_map/edge_images/pallas_call | solution.py:140
  17.9 4.5 %collective-permute-start.2 = (f32[3,16,128]{2,1,0:T(8,128)S(1)}, f32[3,16,128]{2,1,0:T(8,128)S(1)}, u32[]{:S(2)}, u32[]{:S(2)}) collective-permute-start(f32[3,16,128]{2,1,0:T(8,128)S(1)} %get-tuple-element.122), channel_id=1, source_target_pairs={{0,1},{1,0},{2,3},{3,2},{4,5},{5,4},{6,7},{7,6},{8,9},{9,8},{10,11... | collective-permute-start | bytes 73736 | tf_op jit(solution)/shard_map/ppermute | solution.py:38
  23.9 2.5 %collective-permute-start.3 = (f32[3,16,128]{2,1,0:T(8,128)S(1)}, f32[3,16,128]{2,1,0:T(8,128)S(1)}, u32[]{:S(2)}, u32[]{:S(2)}) collective-permute-start(f32[3,16,128]{2,1,0:T(8,128)S(1)} %add.48), channel_id=1, source_target_pairs={{0,2},{1,3},{2,0},{3,1},{4,6},{5,7},{6,4},{7,5},{8,10},{9,11},{10,... | collective-permute-start | bytes 73736 | tf_op jit(solution)/shard_map/ppermute | solution.py:38
  29.8 2.8 %collective-permute-start.4 = (f32[3,16,128]{2,1,0:T(8,128)S(1)}, f32[3,16,128]{2,1,0:T(8,128)S(1)}, u32[]{:S(2)}, u32[]{:S(2)}) collective-permute-start(f32[3,16,128]{2,1,0:T(8,128)S(1)} %add.49), channel_id=1, source_target_pairs={{0,4},{1,5},{2,6},{3,7},{4,0},{5,1},{6,2},{7,3},{8,12},{9,13},{10,... | collective-permute-start | bytes 73736 | tf_op jit(solution)/shard_map/ppermute | solution.py:38
  35.1 2.6 %collective-permute-start.5 = (f32[3,16,128]{2,1,0:T(8,128)S(1)}, f32[3,16,128]{2,1,0:T(8,128)S(1)}, u32[]{:S(2)}, u32[]{:S(2)}) collective-permute-start(f32[3,16,128]{2,1,0:T(8,128)S(1)} %add.50), channel_id=1, source_target_pairs={{0,8},{1,9},{2,10},{3,11},{4,12},{5,13},{6,14},{7,15},{8,0},{9,1},... | collective-permute-start | bytes 73736 | tf_op jit(solution)/shard_map/ppermute | solution.py:38
  42.8 4.2 %collective-permute-done.10 = bf16[4,128,128]{2,1,0:T(8,128)(2,1)S(1)} collective-permute-done((bf16[4,128,128]{2,1,0:T(8,128)(2,1)S(1)}, bf16[4,128,128]{2,1,0:T(8,128)(2,1)S(1)}, u32[]{:S(2)}, u32[]{:S(2)}) %collective-permute-start.10) | collective-permute-done | bytes 131104 | tf_op jit(solution)/shard_map/ppermute | solution.py:38
  48.4 2.8 %collective-permute-start.13 = (bf16[1,128,128]{2,1,0:T(8,128)(2,1)S(1)}, bf16[1,128,128]{2,1,0:T(8,128)(2,1)S(1)}, u32[]{:S(2)}, u32[]{:S(2)}) collective-permute-start(bf16[1,128,128]{2,1,0:T(8,128)(2,1)S(1)} %get-tuple-element.211), channel_id=1, source_target_pairs={{0,12},{1,13},{2,14},{3,15},{4,8},{5,9},{6,10},{7,11},{8,4},{9,5},... | collective-permute-start | bytes 98312 | tf_op jit(solution)/shard_map/ppermute | solution.py:38
  51.3 2.7 %collective-permute-done.13 = bf16[1,128,128]{2,1,0:T(8,128)(2,1)S(1)} collective-permute-done((bf16[1,128,128]{2,1,0:T(8,128)(2,1)S(1)}, bf16[1,128,128]{2,1,0:T(8,128)(2,1)S(1)}, u32[]{:S(2)}, u32[]{:S(2)}) %collective-permute-start.13) | collective-permute-done | bytes 32800 | tf_op jit(solution)/shard_map/ppermute | solution.py:38
  54.1 2.3 %collective-permute-done.12 = bf16[1,128,128]{2,1,0:T(8,128)(2,1)S(1)} collective-permute-done((bf16[1,128,128]{2,1,0:T(8,128)(2,1)S(1)}, bf16[1,128,128]{2,1,0:T(8,128)(2,1)S(1)}, u32[]{:S(2)}, u32[]{:S(2)}) %collective-permute-start.12) | collective-permute-done | bytes 32800 | tf_op jit(solution)/shard_map/ppermute | solution.py:38
  57.7 7.1 %rotation.2 = bf16[128,256]{1,0:T(8,128)(2,1)S(1)} custom-call(s32[1]{0:T(128)} %bitcast.2.me_ref, f32[2,128,128]{2,1,0:T(8,128)S(1)} %pad_maximum_fusion.4.packed_ref), custom_call_target="tpu_custom_call" | custom-call | tf_op jit(solution)/shard_map/rotation/pallas_call | solution.py:341
  71.7 2.7 %collective-permute-done.18 = bf16[1,128,256]{2,1,0:T(8,128)(2,1)S(1)} collective-permute-done((bf16[1,128,256]{2,1,0:T(8,128)(2,1)S(1)}, bf16[1,128,256]{2,1,0:T(8,128)(2,1)S(1)}, u32[]{:S(2)}, u32[]{:S(2)}) %collective-permute-start.18) | collective-permute-done | bytes 65568 | tf_op jit(solution)/shard_map/ppermute | solution.py:38
  76.4 3.1 %collective-permute-done.20 = bf16[2,128,256]{2,1,0:T(8,128)(2,1)S(1)} collective-permute-done((bf16[2,128,256]{2,1,0:T(8,128)(2,1)S(1)}, bf16[2,128,256]{2,1,0:T(8,128)(2,1)S(1)}, u32[]{:S(2)}, u32[]{:S(2)}) %collective-permute-start.20) | collective-permute-done | bytes 131104 | tf_op jit(solution)/shard_map/ppermute | solution.py:38
  79.6 2.2 %rotate.2 = (bf16[512,2048]{1,0:T(8,128)(2,1)S(1)}, bf16[3,512,2048]{2,1,0:T(8,128)(2,1)S(1)}, f32[3,16,128]{2,1,0:T(8,128)S(1)}) custom-call(s32[16]{0:T(128)S(1)} %get-tuple-element.111.place_ref, s32[1]{0:T(128)} %bitcast.2.me_ref, bf16[8,128,256]{2,1,0:T(8,128)(2,1)S(1)} %constant_dynamic-update-slice_fusion.gathered_ref, bf16[512,2048]{1,0:T(8,128)(2,1)S(1)} %copy-done, ...), custom_call_target="tpu_custom_call" | custom-call | flops 1073741824 | bytes 8388608 | tf_op jit(solution)/shard_map/rotate/pallas_call | solution.py:383
  81.9 2.2 %rotate.3 = (bf16[512,2048]{1,0:T(8,128)(2,1)S(1)}, bf16[3,512,2048]{2,1,0:T(8,128)(2,1)S(1)}, f32[3,16,128]{2,1,0:T(8,128)S(1)}) custom-call(s32[16]{0:T(128)S(1)} %get-tuple-element.111.place_ref, s32[1]{0:T(128)} %bitcast.2.me_ref, ...), custom_call_target="tpu_custom_call", output_to_operand_aliasing={{0}: (6, {}), {1}: (7, {}), {2}: (8, {})} | custom-call | flops 1073741824 | bytes 8388608 | tf_op jit(solution)/shard_map/rotate/pallas_call | solution.py:383
  96.5 4.0 %collective-permute-done.26 = f32[3,16,128]{2,1,0:T(8,128)S(1)} collective-permute-done((f32[3,16,128]{2,1,0:T(8,128)S(1)}, f32[3,16,128]{2,1,0:T(8,128)S(1)}, u32[]{:S(2)}, u32[]{:S(2)}) %collective-permute-start.26) | collective-permute-done | bytes 24608 | tf_op jit(solution)/shard_map/ppermute | solution.py:38
  102.9 4.7 %collective-permute-done.31 = bf16[4,128,128]{2,1,0:T(8,128)(2,1)S(1)} collective-permute-done((bf16[4,128,128]{2,1,0:T(8,128)(2,1)S(1)}, bf16[4,128,128]{2,1,0:T(8,128)(2,1)S(1)}, u32[]{:S(2)}, u32[]{:S(2)}) %collective-permute-start.31) | collective-permute-done | bytes 131104 | tf_op jit(solution)/shard_map/ppermute | solution.py:38
  111.7 2.3 %collective-permute-done.34 = bf16[1,128,128]{2,1,0:T(8,128)(2,1)S(1)} collective-permute-done((bf16[1,128,128]{2,1,0:T(8,128)(2,1)S(1)}, bf16[1,128,128]{2,1,0:T(8,128)(2,1)S(1)}, u32[]{:S(2)}, u32[]{:S(2)}) %collective-permute-start.34) | collective-permute-done | bytes 32800 | tf_op jit(solution)/shard_map/ppermute | solution.py:38
  116.5 9.4 %rotation.3 = bf16[128,256]{1,0:T(8,128)(2,1)S(1)} custom-call(s32[1]{0:T(128)} %bitcast.2.me_ref, f32[2,128,128]{2,1,0:T(8,128)S(1)} %pad_maximum_fusion.6.packed_ref), custom_call_target="tpu_custom_call" | custom-call | tf_op jit(solution)/shard_map/rotation/pallas_call | solution.py:341
  133.6 2.4 %collective-permute-done.39 = bf16[1,128,256]{2,1,0:T(8,128)(2,1)S(1)} collective-permute-done((bf16[1,128,256]{2,1,0:T(8,128)(2,1)S(1)}, bf16[1,128,256]{2,1,0:T(8,128)(2,1)S(1)}, u32[]{:S(2)}, u32[]{:S(2)}) %collective-permute-start.39) | collective-permute-done | bytes 65568 | tf_op jit(solution)/shard_map/ppermute | solution.py:38
  138.3 2.9 %collective-permute-done.41 = bf16[2,128,256]{2,1,0:T(8,128)(2,1)S(1)} collective-permute-done((bf16[2,128,256]{2,1,0:T(8,128)(2,1)S(1)}, bf16[2,128,256]{2,1,0:T(8,128)(2,1)S(1)}, u32[]{:S(2)}, u32[]{:S(2)}) %collective-permute-start.41) | collective-permute-done | bytes 131104 | tf_op jit(solution)/shard_map/ppermute | solution.py:38
  142.9 2.9 %rotate_last.1 = bf16[512,2048]{1,0:T(8,128)(2,1)} custom-call(s32[16]{0:T(128)S(1)} %get-tuple-element.109.place_ref, s32[16]{0:T(128)S(1)} %get-tuple-element.219.home_ref, s32[1]{0:T(128)} %bitcast.2.me_ref, bf16[8,128,256]{2,1,0:T(8,128)(2,1)S(1)} %constant_dynamic-update-slice_fusion.10.refs_0_, ...), custom_call_target="tpu_custom_call" | custom-call | tf_op jit(solution)/shard_map/rotate_last/pallas_call | solution.py:424
  (141 shorter events, 63.1 us)
Async XLA Ops:
  2.2 12.5 %collective-permute-start = (bf16[128,2048]{1,0:T(8,128)(2,1)}, bf16[128,2048]{1,0:T(8,128)(2,1)}, u32[]{:S(2)}, u32[]{:S(2)}) collective-permute-start(bf16[128,2048]{1,0:T(8,128)(2,1)} %get-tuple-element.113), channel_id=1, source_target_pairs={{0,1},{1,2},{2,3},{3,4},{4,5},{5,6},{6,7},{7,8},{8,9},{9,10},{10,1... | collective-permute-start | bytes 1572872 | tf_op jit(solution)/shard_map/ppermute | solution.py:534
  5.4 9.4 %collective-permute-start.1 = (bf16[128,2048]{1,0:T(8,128)(2,1)}, bf16[128,2048]{1,0:T(8,128)(2,1)}, u32[]{:S(2)}, u32[]{:S(2)}) collective-permute-start(bf16[128,2048]{1,0:T(8,128)(2,1)} %get-tuple-element.114), channel_id=1, source_target_pairs={{1,0},{2,1},{3,2},{4,3},{5,4},{6,5},{7,6},{8,7},{9,8},{10,9},{11,1... | collective-permute-start | bytes 1572872 | tf_op jit(solution)/shard_map/ppermute | solution.py:535
  17.9 6.0 %collective-permute-start.2 = (f32[3,16,128]{2,1,0:T(8,128)S(1)}, f32[3,16,128]{2,1,0:T(8,128)S(1)}, u32[]{:S(2)}, u32[]{:S(2)}) collective-permute-start(f32[3,16,128]{2,1,0:T(8,128)S(1)} %get-tuple-element.122), channel_id=1, source_target_pairs={{0,1},{1,0},{2,3},{3,2},{4,5},{5,4},{6,7},{7,6},{8,9},{9,8},{10,11... | collective-permute-start | bytes 73736 | tf_op jit(solution)/shard_map/ppermute | solution.py:38
  32.5 7.3 %collective-permute-start.6 = (f32[2,3,128,128]{3,2,1,0:T(8,128)S(1)}, f32[2,3,128,128]{3,2,1,0:T(8,128)S(1)}, u32[]{:S(2)}, u32[]{:S(2)}) collective-permute-start(f32[2,3,128,128]{3,2,1,0:T(8,128)S(1)} %get-tuple-element.143), channel_id=1, source_target_pairs={{0,1},{1,0},{2,3},{3,2},{4,5},{5,4},{6,7},{7,6},{8,9},{9,8},{10,11... | collective-permute-start | bytes 1179656 | tf_op jit(solution)/shard_map/ppermute | solution.py:38
  32.5 7.3 %collective-permute-start.7 = (f32[2,3,128,128]{3,2,1,0:T(8,128)S(1)}, f32[2,3,128,128]{3,2,1,0:T(8,128)S(1)}, u32[]{:S(2)}, u32[]{:S(2)}) collective-permute-start(f32[2,3,128,128]{3,2,1,0:T(8,128)S(1)} %get-tuple-element.144), channel_id=1, source_target_pairs={{0,1},{1,0},{2,3},{3,2},{4,5},{5,4},{6,7},{7,6},{8,9},{9,8},{10,11... | collective-permute-start | bytes 1179656 | tf_op jit(solution)/shard_map/ppermute | solution.py:38
  33.1 6.8 %collective-permute-start.8 = (f32[2,3,128,128]{3,2,1,0:T(8,128)S(1)}, f32[2,3,128,128]{3,2,1,0:T(8,128)S(1)}, u32[]{:S(2)}, u32[]{:S(2)}) collective-permute-start(f32[2,3,128,128]{3,2,1,0:T(8,128)S(1)} %get-tuple-element.145), channel_id=1, source_target_pairs={{0,1},{1,0},{2,3},{3,2},{4,5},{5,4},{6,7},{7,6},{8,9},{9,8},{10,11... | collective-permute-start | bytes 1179656 | tf_op jit(solution)/shard_map/ppermute | solution.py:38
  34.6 5.4 %collective-permute-start.9 = (f32[2,3,128,128]{3,2,1,0:T(8,128)S(1)}, f32[2,3,128,128]{3,2,1,0:T(8,128)S(1)}, u32[]{:S(2)}, u32[]{:S(2)}) collective-permute-start(f32[2,3,128,128]{3,2,1,0:T(8,128)S(1)} %get-tuple-element.146), channel_id=1, source_target_pairs={{0,1},{1,0},{2,3},{3,2},{4,5},{5,4},{6,7},{7,6},{8,9},{9,8},{10,11... | collective-permute-start | bytes 1179656 | tf_op jit(solution)/shard_map/ppermute | solution.py:38
  48.4 5.7 %collective-permute-start.13 = (bf16[1,128,128]{2,1,0:T(8,128)(2,1)S(1)}, bf16[1,128,128]{2,1,0:T(8,128)(2,1)S(1)}, u32[]{:S(2)}, u32[]{:S(2)}) collective-permute-start(bf16[1,128,128]{2,1,0:T(8,128)(2,1)S(1)} %get-tuple-element.211), channel_id=1, source_target_pairs={{0,12},{1,13},{2,14},{3,15},{4,8},{5,9},{6,10},{7,11},{8,4},{9,5},... | collective-permute-start | bytes 98312 | tf_op jit(solution)/shard_map/ppermute | solution.py:38
  51.2 5.2 %collective-permute-start.12 = (bf16[1,128,128]{2,1,0:T(8,128)(2,1)S(1)}, bf16[1,128,128]{2,1,0:T(8,128)(2,1)S(1)}, u32[]{:S(2)}, u32[]{:S(2)}) collective-permute-start(bf16[1,128,128]{2,1,0:T(8,128)(2,1)S(1)} %get-tuple-element.212), channel_id=1, source_target_pairs={{0,8},{1,9},{2,10},{3,11},{4,12},{5,13},{6,14},{7,15},{8,0},{9,1},... | collective-permute-start | bytes 98312 | tf_op jit(solution)/shard_map/ppermute | solution.py:38
  65.2 6.5 %collective-permute-start.19 = (bf16[1,128,256]{2,1,0:T(8,128)(2,1)S(1)}, bf16[1,128,256]{2,1,0:T(8,128)(2,1)S(1)}, u32[]{:S(2)}, u32[]{:S(2)}) collective-permute-start(bf16[1,128,256]{2,1,0:T(8,128)(2,1)S(1)} %bitcast.17), channel_id=1, source_target_pairs={{0,12},{1,13},{2,14},{3,15},{4,8},{5,9},{6,10},{7,11},{8,4},{9,5},... | collective-permute-start | bytes 196616 | tf_op jit(solution)/shard_map/ppermute | solution.py:38
  66.4 8.0 %collective-permute-start.18 = (bf16[1,128,256]{2,1,0:T(8,128)(2,1)S(1)}, bf16[1,128,256]{2,1,0:T(8,128)(2,1)S(1)}, u32[]{:S(2)}, u32[]{:S(2)}) collective-permute-start(bf16[1,128,256]{2,1,0:T(8,128)(2,1)S(1)} %bitcast.18), channel_id=1, source_target_pairs={{0,8},{1,9},{2,10},{3,11},{4,12},{5,13},{6,14},{7,15},{8,0},{9,1},... | collective-permute-start | bytes 196616 | tf_op jit(solution)/shard_map/ppermute | solution.py:38
  68.4 6.1 %collective-permute-start.15 = (bf16[1,128,256]{2,1,0:T(8,128)(2,1)S(1)}, bf16[1,128,256]{2,1,0:T(8,128)(2,1)S(1)}, u32[]{:S(2)}, u32[]{:S(2)}) collective-permute-start(bf16[1,128,256]{2,1,0:T(8,128)(2,1)S(1)} %bitcast.19), channel_id=1, source_target_pairs={{0,2},{1,3},{2,0},{3,1},{4,6},{5,7},{6,4},{7,5},{8,10},{9,11},{10,... | collective-permute-start | bytes 196616 | tf_op jit(solution)/shard_map/ppermute | solution.py:38
  69.1 5.3 %collective-permute-start.17 = (bf16[1,128,256]{2,1,0:T(8,128)(2,1)S(1)}, bf16[1,128,256]{2,1,0:T(8,128)(2,1)S(1)}, u32[]{:S(2)}, u32[]{:S(2)}) collective-permute-start(bf16[1,128,256]{2,1,0:T(8,128)(2,1)S(1)} %collective-permute-done.16), channel_id=1, source_target_pairs={{0,2},{1,3},{2,0},{3,1},{4,6},{5,7},{6,4},{7,5},{8,10},{9,11},{10,... | collective-permute-start | bytes 196616 | tf_op jit(solution)/shard_map/ppermute | solution.py:38
  91.8 8.8 %collective-permute-start.27 = (f32[2,3,128,128]{3,2,1,0:T(8,128)S(1)}, f32[2,3,128,128]{3,2,1,0:T(8,128)S(1)}, u32[]{:S(2)}, u32[]{:S(2)}) collective-permute-start(f32[2,3,128,128]{3,2,1,0:T(8,128)S(1)} %get-tuple-element.191), channel_id=1, source_target_pairs={{0,1},{1,0},{2,3},{3,2},{4,5},{5,4},{6,7},{7,6},{8,9},{9,8},{10,11... | collective-permute-start | bytes 1179656 | tf_op jit(solution)/shard_map/ppermute | solution.py:38
  91.8 8.8 %collective-permute-start.28 = (f32[2,3,128,128]{3,2,1,0:T(8,128)S(1)}, f32[2,3,128,128]{3,2,1,0:T(8,128)S(1)}, u32[]{:S(2)}, u32[]{:S(2)}) collective-permute-start(f32[2,3,128,128]{3,2,1,0:T(8,128)S(1)} %get-tuple-element.192), channel_id=1, source_target_pairs={{0,1},{1,0},{2,3},{3,2},{4,5},{5,4},{6,7},{7,6},{8,9},{9,8},{10,11... | collective-permute-start | bytes 1179656 | tf_op jit(solution)/shard_map/ppermute | solution.py:38
  93.8 6.8 %collective-permute-start.29 = (f32[2,3,128,128]{3,2,1,0:T(8,128)S(1)}, f32[2,3,128,128]{3,2,1,0:T(8,128)S(1)}, u32[]{:S(2)}, u32[]{:S(2)}) collective-permute-start(f32[2,3,128,128]{3,2,1,0:T(8,128)S(1)} %get-tuple-element.193), channel_id=1, source_target_pairs={{0,1},{1,0},{2,3},{3,2},{4,5},{5,4},{6,7},{7,6},{8,9},{9,8},{10,11... | collective-permute-start | bytes 1179656 | tf_op jit(solution)/shard_map/ppermute | solution.py:38
  95.5 5.1 %collective-permute-start.30 = (f32[2,3,128,128]{3,2,1,0:T(8,128)S(1)}, f32[2,3,128,128]{3,2,1,0:T(8,128)S(1)}, u32[]{:S(2)}, u32[]{:S(2)}) collective-permute-start(f32[2,3,128,128]{3,2,1,0:T(8,128)S(1)} %get-tuple-element.194), channel_id=1, source_target_pairs={{0,1},{1,0},{2,3},{3,2},{4,5},{5,4},{6,7},{7,6},{8,9},{9,8},{10,11... | collective-permute-start | bytes 1179656 | tf_op jit(solution)/shard_map/ppermute | solution.py:38
  108.3 5.7 %collective-permute-start.34 = (bf16[1,128,128]{2,1,0:T(8,128)(2,1)S(1)}, bf16[1,128,128]{2,1,0:T(8,128)(2,1)S(1)}, u32[]{:S(2)}, u32[]{:S(2)}) collective-permute-start(bf16[1,128,128]{2,1,0:T(8,128)(2,1)S(1)} %get-tuple-element.208), channel_id=1, source_target_pairs={{0,12},{1,13},{2,14},{3,15},{4,8},{5,9},{6,10},{7,11},{8,4},{9,5},... | collective-permute-start | bytes 98312 | tf_op jit(solution)/shard_map/ppermute | solution.py:38
  110.0 5.2 %collective-permute-start.33 = (bf16[1,128,128]{2,1,0:T(8,128)(2,1)S(1)}, bf16[1,128,128]{2,1,0:T(8,128)(2,1)S(1)}, u32[]{:S(2)}, u32[]{:S(2)}) collective-permute-start(bf16[1,128,128]{2,1,0:T(8,128)(2,1)S(1)} %get-tuple-element.209), channel_id=1, source_target_pairs={{0,8},{1,9},{2,10},{3,11},{4,12},{5,13},{6,14},{7,15},{8,0},{9,1},... | collective-permute-start | bytes 98312 | tf_op jit(solution)/shard_map/ppermute | solution.py:38
  127.1 6.5 %collective-permute-start.40 = (bf16[1,128,256]{2,1,0:T(8,128)(2,1)S(1)}, bf16[1,128,256]{2,1,0:T(8,128)(2,1)S(1)}, u32[]{:S(2)}, u32[]{:S(2)}) collective-permute-start(bf16[1,128,256]{2,1,0:T(8,128)(2,1)S(1)} %bitcast.11), channel_id=1, source_target_pairs={{0,12},{1,13},{2,14},{3,15},{4,8},{5,9},{6,10},{7,11},{8,4},{9,5},... | collective-permute-start | bytes 196616 | tf_op jit(solution)/shard_map/ppermute | solution.py:38
  128.2 7.8 %collective-permute-start.39 = (bf16[1,128,256]{2,1,0:T(8,128)(2,1)S(1)}, bf16[1,128,256]{2,1,0:T(8,128)(2,1)S(1)}, u32[]{:S(2)}, u32[]{:S(2)}) collective-permute-start(bf16[1,128,256]{2,1,0:T(8,128)(2,1)S(1)} %bitcast.12), channel_id=1, source_target_pairs={{0,8},{1,9},{2,10},{3,11},{4,12},{5,13},{6,14},{7,15},{8,0},{9,1},... | collective-permute-start | bytes 196616 | tf_op jit(solution)/shard_map/ppermute | solution.py:38
  129.5 6.5 %collective-permute-start.36 = (bf16[1,128,256]{2,1,0:T(8,128)(2,1)S(1)}, bf16[1,128,256]{2,1,0:T(8,128)(2,1)S(1)}, u32[]{:S(2)}, u32[]{:S(2)}) collective-permute-start(bf16[1,128,256]{2,1,0:T(8,128)(2,1)S(1)} %bitcast.13), channel_id=1, source_target_pairs={{0,2},{1,3},{2,0},{3,1},{4,6},{5,7},{6,4},{7,5},{8,10},{9,11},{10,... | collective-permute-start | bytes 196616 | tf_op jit(solution)/shard_map/ppermute | solution.py:38
  130.4 5.5 %collective-permute-start.38 = (bf16[1,128,256]{2,1,0:T(8,128)(2,1)S(1)}, bf16[1,128,256]{2,1,0:T(8,128)(2,1)S(1)}, u32[]{:S(2)}, u32[]{:S(2)}) collective-permute-start(bf16[1,128,256]{2,1,0:T(8,128)(2,1)S(1)} %collective-permute-done.37), channel_id=1, source_target_pairs={{0,2},{1,3},{2,0},{3,1},{4,6},{5,7},{6,4},{7,5},{8,10},{9,11},{10,... | collective-permute-start | bytes 196616 | tf_op jit(solution)/shard_map/ppermute | solution.py:38
  136.0 5.2 %collective-permute-start.41 = (bf16[2,128,256]{2,1,0:T(8,128)(2,1)S(1)}, bf16[2,128,256]{2,1,0:T(8,128)(2,1)S(1)}, u32[]{:S(2)}, u32[]{:S(2)}) collective-permute-start(bf16[2,128,256]{2,1,0:T(8,128)(2,1)S(1)} %pad_maximum_fusion.7), channel_id=1, source_target_pairs={{0,2},{1,3},{2,0},{3,1},{4,6},{5,7},{6,4},{7,5},{8,10},{9,11},{10,... | collective-permute-start | bytes 393224 | tf_op jit(solution)/shard_map/ppermute | solution.py:38
  (24 other events, 97.1 us)

commit v4 on v3

--- a/solution.py
+++ b/solution.py
@@ -201,51 +201,41 @@
     )(place, me, cols, *images)
 
 
-def weight_kernel(sub_bits, place_ref, me_ref, diag_ref, *refs):
-    sums_refs, keep_ref, send_ref = refs[:-2], refs[-2], refs[-1]
+def weight_kernel(sub_bits, stays, place_ref, me_ref, diag_ref, *refs):
+    sums_refs, out_ref = refs[:-1], refs[-1]
     kept_refs, came_refs = sums_refs[: len(sums_refs) // 2], sums_refs[len(sums_refs) // 2 :]
     core = me_ref[0] & 1
     bit = (me_ref[0] >> sub_bits) & 1
+    odd = bit if stays else 1 - bit
     rows = lax.broadcasted_iota(jnp.int32, (HALF, HALF), 0)
     cols = lax.broadcasted_iota(jnp.int32, (HALF, HALF), 1)
     low = jnp.where(rows > cols, 1, 0)
     col_first = jnp.maximum(low, 1 - core) > 0
     row_first = jnp.minimum(low, core) > 0
     step = kept_refs[0].shape[0]
-    for j in range(keep_ref.shape[0]):
-        for stays in (True, False):
-            odd = bit if stays else 1 - bit
-            pair = 2 * j + odd
-            i = 2 * j % step + odd
-            kept_ref, came_ref = kept_refs[2 * j // step], came_refs[2 * j // step]
-            halves = [
-                [diag_ref[k, pl.ds(place_ref[2 * pair + h], 1), :] for k in range(3)]
-                for h in (0, 1)
-            ]
-            first, second = [
-                jnp.concatenate(half + half + half[:2], axis=0).T for half in halves
-            ]
-            total = jnp.zeros((HALF, HALF), F32)
-            for k in range(3):
-                col = jnp.where(col_first, first[:, k : k + 1], second[:, k : k + 1])
-                row = jnp.where(row_first, halves[0][k], halves[1][k])
-                total += (kept_ref[i, k] + came_ref[i, k]) * (col - row)
-            if stays:
-                keep_ref[j] = total
-            else:
-                send_ref[j] = total.astype(BF16)
-
-
-def weigh(place, me, diag, kept, came, sub_bits):
+    for j in range(out_ref.shape[0]):
+        pair = 2 * j + odd
+        i = 2 * j % step + odd
+        kept_ref, came_ref = kept_refs[2 * j // step], came_refs[2 * j // step]
+        halves = [
+            [diag_ref[k, pl.ds(place_ref[2 * pair + h], 1), :] for k in range(3)] for h in (0, 1)
+        ]
+        first, second = [jnp.concatenate(half + half + half[:2], axis=0).T for half in halves]
+        total = jnp.zeros((HALF, HALF), F32)
+        for k in range(3):
+            col = jnp.where(col_first, first[:, k : k + 1], second[:, k : k + 1])
+            row = jnp.where(row_first, halves[0][k], halves[1][k])
+            total += (kept_ref[i, k] + came_ref[i, k]) * (col - row)
+        out_ref[j] = total.astype(out_ref.dtype)
+
+
+def weigh(place, me, diag, kept, came, sub_bits, stays):
     high = sum(part.shape[0] for part in kept) // 2
     return pl.pallas_call(
-        functools.partial(weight_kernel, sub_bits),
-        out_shape=(
-            jax.ShapeDtypeStruct((high, HALF, HALF), F32),
-            jax.ShapeDtypeStruct((high, HALF, HALF), BF16),
-        ),
+        functools.partial(weight_kernel, sub_bits, stays),
+        out_shape=jax.ShapeDtypeStruct((high, HALF, HALF), F32 if stays else BF16),
         in_specs=[SMEM, SMEM] + [VMEM] * (1 + 2 * len(kept)),
-        out_specs=(VMEM, VMEM),
+        out_specs=VMEM,
         compiler_params=params(),
         name="weigh",
     )(place, me, diag, *kept, *came)
@@ -439,9 +429,12 @@
     hops = bits_of(lax.axis_size("orb"))
     for bit in range(hops):
         arrived = swap(diag, 1 << bit)
+        products, token = [], diag
         for maker in makers.get(bit, ()):
-            diag, arrived, product = lax.optimization_barrier((diag, arrived, maker(diag)))
-            made.append(product)
+            products.append(maker(token))
+            token = products[-1][0]
+        diag, arrived, products = lax.optimization_barrier((diag, arrived, products))
+        made += products
         diag = diag + arrived
     return diag, made
 
@@ -471,8 +464,7 @@
     return own
 
 
-def reduce_pairs(keep, send, places, sub_bits):
-    value = keep + swap(send, 1 << sub_bits).astype(F32)
+def reduce_pairs(value, places, sub_bits):
     high = value.shape[0]
     for bit in range(1, sub_bits):
         rows = value.shape[1] // 2
@@ -557,8 +549,11 @@
         diag_sum, made = sum_beside(diag, makers)
         kept = [keep for keep, _ in made]
         came = [swap(send, 1) for _, send in made]
-        keep, send = weigh(place, me, diag_sum, kept, came, sub_bits)
-        own = reduce_pairs(keep, send, places, sub_bits)
+        send = weigh(place, me, diag_sum, kept, came, sub_bits, False)
+        across = swap(send, 1 << sub_bits)
+        keep = weigh(place, me, diag_sum, kept, came, sub_bits, True)
+        across, keep = lax.optimization_barrier((across, keep))
+        own = reduce_pairs(keep + across.astype(F32), places, sub_bits)
         packed = own[None]
         for bit in range(sub_bits):
             packed = gather_bits(packed, 1, bit)

time: 144 us -> 141 us (0.979); the launches traced: 146 us -> 141 us
  waiting for transfers between devices: 50.3 us -> 42.7 us
  starting transfers between devices: 41.3 us -> 46.4 us
  Pallas kernels: 46.8 us -> 44.7 us
    ppermute x42, waiting for transfers between devices: 50.3 us -> 42.7 us  [swap(): return lax.ppermute(block, 'orb', [(i, i ^ distance) for i in range(count)])]
    ppermute x42, starting transfers between devices: 36.9 us -> 42 us  [swap(): return lax.ppermute(block, 'orb', [(i, i ^ distance) for i in range(count)])]
    pallas_call x2, Pallas kernels: 16.4 us -> 13 us  [rotation_share(): pl.pallas_call(functools.partial(rotation_kernel, scale, subs), out_shape...]
    pallas_call x2 -> x4, Pallas kernels: 3.97 us -> 5.3 us  [weigh(): pl.pallas_call(functools.partial(weight_kernel, sub_bits, stays), out_sha...]
  transfers between devices with their start and end apart: 44 -> 44, of which waited for: 25 -> 23; matrix products, arithmetic and copies ran while one was open for 4% -> 4% of each run, Pallas kernels for 9% -> 13%
where the time goes in v4:
time: 141 us
  starting transfers between devices  46.4 us (33%)
  Pallas kernels  44.7 us (32%)
  waiting for transfers between devices  42.7 us (30%)
  local copies, waits for them, and re-layouts  5.98 us (4%)
    ppermute x42, waiting for transfers between devices, swap(): return lax.ppermute(block, 'orb', [(i, i ^ distance) for i in range(count)])  42.7 us
    ppermute x42, starting transfers between devices, swap(): return lax.ppermute(block, 'orb', [(i, i ^ distance) for i in range(count)])  42 us
    pallas_call x2, Pallas kernels, rotation_share(): pl.pallas_call(functools.partial(rotation_kernel, scale, subs), out_shape...  13 us
    pallas_call x8, Pallas kernels, pair_products(): pl.pallas_call(functools.partial(gram_kernel, first), out_shape=(shape, s...  12 us
    pallas_call x4, Pallas kernels, weigh(): pl.pallas_call(functools.partial(weight_kernel, sub_bits, stays), out_sha...  5.3 us
    pallas_call x2, Pallas kernels, rotate(): pl.pallas_call(functools.partial(rotate_kernel, first, len(earlier)), out...  4.38 us
    reshape x1, local copies, waits for them, and re-layouts, per_device(): blocks = jnp.transpose(dipole_blocks * mask_full[None, :, :, None, None],...  3.36 us
    ppermute x1, starting transfers between devices, per_device(): low = lax.ppermute(last, 'orb', forward)  3.17 us
  transfers between devices with their start and end apart: 44, of which 23 were waited for; matrix products, arithmetic and copies ran while one was open for 4% of the time, Pallas kernels for 13%

profile of v4, /device:TPU:0, one launch (start us, length us, event | category | flops | bytes accessed | tf_op | source)
XLA Modules:
  0.0 141.2 jit_solution(2635067232878613655)
XLA Ops:
  0.0 2.2 %edge_rows.1 = (bf16[128,2048]{1,0:T(8,128)(2,1)}, bf16[128,2048]{1,0:T(8,128)(2,1)}) custom-call(bf16[512,2048]{1,0:T(8,128)(2,1)} %cols_ref.7), custom_call_target="tpu_custom_call" | custom-call | tf_op jit(solution)/shard_map/edge_rows/pallas_call | solution.py:72
  2.2 3.2 %collective-permute-start = (bf16[128,2048]{1,0:T(8,128)(2,1)}, bf16[128,2048]{1,0:T(8,128)(2,1)}, u32[]{:S(2)}, u32[]{:S(2)}) collective-permute-start(bf16[128,2048]{1,0:T(8,128)(2,1)} %get-tuple-element.113), channel_id=1, source_target_pairs={{0,1},{1,2},{2,3},{3,4},{4,5},{5,6},{6,7},{7,8},{8,9},{9,10},{10,1... | collective-permute-start | bytes 1572872 | tf_op jit(solution)/shard_map/ppermute | solution.py:526
  9.5 3.4 %reshape.58.blocks_ref = bf16[4,384,384]{2,1,0:T(8,128)(2,1)S(1)} reshape(bf16[4,3,128,3,128]{4,3,2,1,0:T(4,128)(2,1)} %copy.13) | data formatting | bytes 2359296 | tf_op jit(solution)/shard_map/reshape | solution.py:533
  14.8 3.1 %edge_images.1 = (bf16[3,256,2048]{2,1,0:T(8,128)(2,1)S(1)}, f32[3,16,128]{2,1,0:T(8,128)S(1)}) custom-call(bf16[4,384,384]{2,1,0:T(8,128)(2,1)S(1)} %reshape.58.blocks_ref, bf16[512,2048]{1,0:T(8,128)(2,1)S(1)} %copy-done, bf16[128,2048]{1,0:T(8,128)(2,1)} %collective-permute-done.low_ref, bf16[128,2048]{1,0:T(8,128)(2,1)} %collective-permute-done.1.high_ref, ...), custom_call_target="tpu_custom_call" | custom-call | tf_op jit(solution)/shard_map/edge_images/pallas_call | solution.py:140
  17.9 4.5 %collective-permute-start.2 = (f32[3,16,128]{2,1,0:T(8,128)S(1)}, f32[3,16,128]{2,1,0:T(8,128)S(1)}, u32[]{:S(2)}, u32[]{:S(2)}) collective-permute-start(f32[3,16,128]{2,1,0:T(8,128)S(1)} %get-tuple-element.122), channel_id=1, source_target_pairs={{0,1},{1,0},{2,3},{3,2},{4,5},{5,4},{6,7},{7,6},{8,9},{9,8},{10,11... | collective-permute-start | bytes 73736 | tf_op jit(solution)/shard_map/ppermute | solution.py:38
  23.9 2.4 %collective-permute-start.3 = (f32[3,16,128]{2,1,0:T(8,128)S(1)}, f32[3,16,128]{2,1,0:T(8,128)S(1)}, u32[]{:S(2)}, u32[]{:S(2)}) collective-permute-start(f32[3,16,128]{2,1,0:T(8,128)S(1)} %add.48), channel_id=1, source_target_pairs={{0,2},{1,3},{2,0},{3,1},{4,6},{5,7},{6,4},{7,5},{8,10},{9,11},{10,... | collective-permute-start | bytes 73736 | tf_op jit(solution)/shard_map/ppermute | solution.py:38
  33.7 2.5 %collective-permute-start.5 = (f32[3,16,128]{2,1,0:T(8,128)S(1)}, f32[3,16,128]{2,1,0:T(8,128)S(1)}, u32[]{:S(2)}, u32[]{:S(2)}) collective-permute-start(f32[3,16,128]{2,1,0:T(8,128)S(1)} %add.50), channel_id=1, source_target_pairs={{0,8},{1,9},{2,10},{3,11},{4,12},{5,13},{6,14},{7,15},{8,0},{9,1},... | collective-permute-start | bytes 73736 | tf_op jit(solution)/shard_map/ppermute | solution.py:38
  36.2 2.2 %collective-permute-done.5 = f32[3,16,128]{2,1,0:T(8,128)S(1)} collective-permute-done((f32[3,16,128]{2,1,0:T(8,128)S(1)}, f32[3,16,128]{2,1,0:T(8,128)S(1)}, u32[]{:S(2)}, u32[]{:S(2)}) %collective-permute-start.5) | collective-permute-done | bytes 24608 | tf_op jit(solution)/shard_map/ppermute | solution.py:38
  42.4 2.4 %collective-permute-done.10 = bf16[4,128,128]{2,1,0:T(8,128)(2,1)S(1)} collective-permute-done((bf16[4,128,128]{2,1,0:T(8,128)(2,1)S(1)}, bf16[4,128,128]{2,1,0:T(8,128)(2,1)S(1)}, u32[]{:S(2)}, u32[]{:S(2)}) %collective-permute-start.10) | collective-permute-done | bytes 131104 | tf_op jit(solution)/shard_map/ppermute | solution.py:38
  46.2 2.8 %collective-permute-start.13 = (bf16[1,128,128]{2,1,0:T(8,128)(2,1)S(1)}, bf16[1,128,128]{2,1,0:T(8,128)(2,1)S(1)}, u32[]{:S(2)}, u32[]{:S(2)}) collective-permute-start(bf16[1,128,128]{2,1,0:T(8,128)(2,1)S(1)} %get-tuple-element.211), channel_id=1, source_target_pairs={{0,12},{1,13},{2,14},{3,15},{4,8},{5,9},{6,10},{7,11},{8,4},{9,5},... | collective-permute-start | bytes 98312 | tf_op jit(solution)/shard_map/ppermute | solution.py:38
  49.2 2.7 %collective-permute-done.13 = bf16[1,128,128]{2,1,0:T(8,128)(2,1)S(1)} collective-permute-done((bf16[1,128,128]{2,1,0:T(8,128)(2,1)S(1)}, bf16[1,128,128]{2,1,0:T(8,128)(2,1)S(1)}, u32[]{:S(2)}, u32[]{:S(2)}) %collective-permute-start.13) | collective-permute-done | bytes 32800 | tf_op jit(solution)/shard_map/ppermute | solution.py:38
  55.2 4.4 %rotation.2 = bf16[128,256]{1,0:T(8,128)(2,1)S(1)} custom-call(s32[1]{0:T(128)} %bitcast.2.me_ref, f32[2,128,128]{2,1,0:T(8,128)S(1)} %pad_maximum_fusion.4.packed_ref), custom_call_target="tpu_custom_call" | custom-call | tf_op jit(solution)/shard_map/rotation/pallas_call | solution.py:331
  59.9 4.1 %collective-permute-start.19 = (bf16[1,128,256]{2,1,0:T(8,128)(2,1)S(1)}, bf16[1,128,256]{2,1,0:T(8,128)(2,1)S(1)}, u32[]{:S(2)}, u32[]{:S(2)}) collective-permute-start(bf16[1,128,256]{2,1,0:T(8,128)(2,1)S(1)} %bitcast.17), channel_id=1, source_target_pairs={{0,12},{1,13},{2,14},{3,15},{4,8},{5,9},{6,10},{7,11},{8,4},{9,5},... | collective-permute-start | bytes 196616 | tf_op jit(solution)/shard_map/ppermute | solution.py:38
  67.9 2.9 %collective-permute-done.18 = bf16[1,128,256]{2,1,0:T(8,128)(2,1)S(1)} collective-permute-done((bf16[1,128,256]{2,1,0:T(8,128)(2,1)S(1)}, bf16[1,128,256]{2,1,0:T(8,128)(2,1)S(1)}, u32[]{:S(2)}, u32[]{:S(2)}) %collective-permute-start.18) | collective-permute-done | bytes 65568 | tf_op jit(solution)/shard_map/ppermute | solution.py:38
  76.4 2.2 %rotate.2 = (bf16[512,2048]{1,0:T(8,128)(2,1)S(1)}, bf16[3,512,2048]{2,1,0:T(8,128)(2,1)S(1)}, f32[3,16,128]{2,1,0:T(8,128)S(1)}) custom-call(s32[16]{0:T(128)S(1)} %get-tuple-element.111.place_ref, s32[1]{0:T(128)} %bitcast.2.me_ref, bf16[8,128,256]{2,1,0:T(8,128)(2,1)S(1)} %constant_dynamic-update-slice_fusion.gathered_ref, bf16[512,2048]{1,0:T(8,128)(2,1)S(1)} %copy-done, ...), custom_call_target="tpu_custom_call" | custom-call | flops 1073741824 | bytes 8388608 | tf_op jit(solution)/shard_map/rotate/pallas_call | solution.py:373
  78.7 2.2 %rotate.3 = (bf16[512,2048]{1,0:T(8,128)(2,1)S(1)}, bf16[3,512,2048]{2,1,0:T(8,128)(2,1)S(1)}, f32[3,16,128]{2,1,0:T(8,128)S(1)}) custom-call(s32[16]{0:T(128)S(1)} %get-tuple-element.111.place_ref, s32[1]{0:T(128)} %bitcast.2.me_ref, ...), custom_call_target="tpu_custom_call", output_to_operand_aliasing={{0}: (6, {}), {1}: (7, {}), {2}: (8, {})} | custom-call | flops 1073741824 | bytes 8388608 | tf_op jit(solution)/shard_map/rotate/pallas_call | solution.py:373
  93.0 3.7 %collective-permute-done.26 = f32[3,16,128]{2,1,0:T(8,128)S(1)} collective-permute-done((f32[3,16,128]{2,1,0:T(8,128)S(1)}, f32[3,16,128]{2,1,0:T(8,128)S(1)}, u32[]{:S(2)}, u32[]{:S(2)}) %collective-permute-start.26) | collective-permute-done | bytes 24608 | tf_op jit(solution)/shard_map/ppermute | solution.py:38
  100.1 3.0 %collective-permute-done.31 = bf16[4,128,128]{2,1,0:T(8,128)(2,1)S(1)} collective-permute-done((bf16[4,128,128]{2,1,0:T(8,128)(2,1)S(1)}, bf16[4,128,128]{2,1,0:T(8,128)(2,1)S(1)}, u32[]{:S(2)}, u32[]{:S(2)}) %collective-permute-start.31) | collective-permute-done | bytes 131104 | tf_op jit(solution)/shard_map/ppermute | solution.py:38
  107.2 2.3 %collective-permute-done.34 = bf16[1,128,128]{2,1,0:T(8,128)(2,1)S(1)} collective-permute-done((bf16[1,128,128]{2,1,0:T(8,128)(2,1)S(1)}, bf16[1,128,128]{2,1,0:T(8,128)(2,1)S(1)}, u32[]{:S(2)}, u32[]{:S(2)}) %collective-permute-start.34) | collective-permute-done | bytes 32800 | tf_op jit(solution)/shard_map/ppermute | solution.py:38
  112.3 8.6 %rotation.3 = bf16[128,256]{1,0:T(8,128)(2,1)S(1)} custom-call(s32[1]{0:T(128)} %bitcast.2.me_ref, f32[2,128,128]{2,1,0:T(8,128)S(1)} %pad_maximum_fusion.6.packed_ref), custom_call_target="tpu_custom_call" | custom-call | tf_op jit(solution)/shard_map/rotation/pallas_call | solution.py:331
  122.1 2.5 %collective-permute-start.40 = (bf16[1,128,256]{2,1,0:T(8,128)(2,1)S(1)}, bf16[1,128,256]{2,1,0:T(8,128)(2,1)S(1)}, u32[]{:S(2)}, u32[]{:S(2)}) collective-permute-start(bf16[1,128,256]{2,1,0:T(8,128)(2,1)S(1)} %bitcast.11), channel_id=1, source_target_pairs={{0,12},{1,13},{2,14},{3,15},{4,8},{5,9},{6,10},{7,11},{8,4},{9,5},... | collective-permute-start | bytes 196616 | tf_op jit(solution)/shard_map/ppermute | solution.py:38
  126.6 2.3 %collective-permute-done.40 = bf16[1,128,256]{2,1,0:T(8,128)(2,1)S(1)} collective-permute-done((bf16[1,128,256]{2,1,0:T(8,128)(2,1)S(1)}, bf16[1,128,256]{2,1,0:T(8,128)(2,1)S(1)}, u32[]{:S(2)}, u32[]{:S(2)}) %collective-permute-start.40) | collective-permute-done | bytes 65568 | tf_op jit(solution)/shard_map/ppermute | solution.py:38
  133.7 2.9 %collective-permute-done.41 = bf16[2,128,256]{2,1,0:T(8,128)(2,1)S(1)} collective-permute-done((bf16[2,128,256]{2,1,0:T(8,128)(2,1)S(1)}, bf16[2,128,256]{2,1,0:T(8,128)(2,1)S(1)}, u32[]{:S(2)}, u32[]{:S(2)}) %collective-permute-start.41) | collective-permute-done | bytes 131104 | tf_op jit(solution)/shard_map/ppermute | solution.py:38
  138.3 2.9 %rotate_last.1 = bf16[512,2048]{1,0:T(8,128)(2,1)} custom-call(s32[16]{0:T(128)S(1)} %get-tuple-element.109.place_ref, s32[16]{0:T(128)S(1)} %get-tuple-element.219.home_ref, s32[1]{0:T(128)} %bitcast.2.me_ref, bf16[8,128,256]{2,1,0:T(8,128)(2,1)S(1)} %constant_dynamic-update-slice_fusion.10.refs_0_, ...), custom_call_target="tpu_custom_call" | custom-call | tf_op jit(solution)/shard_map/rotate_last/pallas_call | solution.py:414
  (143 shorter events, 65.2 us)
Async XLA Ops:
  2.2 12.6 %collective-permute-start = (bf16[128,2048]{1,0:T(8,128)(2,1)}, bf16[128,2048]{1,0:T(8,128)(2,1)}, u32[]{:S(2)}, u32[]{:S(2)}) collective-permute-start(bf16[128,2048]{1,0:T(8,128)(2,1)} %get-tuple-element.113), channel_id=1, source_target_pairs={{0,1},{1,2},{2,3},{3,4},{4,5},{5,6},{6,7},{7,8},{8,9},{9,10},{10,1... | collective-permute-start | bytes 1572872 | tf_op jit(solution)/shard_map/ppermute | solution.py:526
  5.4 9.4 %collective-permute-start.1 = (bf16[128,2048]{1,0:T(8,128)(2,1)}, bf16[128,2048]{1,0:T(8,128)(2,1)}, u32[]{:S(2)}, u32[]{:S(2)}) collective-permute-start(bf16[128,2048]{1,0:T(8,128)(2,1)} %get-tuple-element.114), channel_id=1, source_target_pairs={{1,0},{2,1},{3,2},{4,3},{5,4},{6,5},{7,6},{8,7},{9,8},{10,9},{11,1... | collective-permute-start | bytes 1572872 | tf_op jit(solution)/shard_map/ppermute | solution.py:527
  17.9 6.0 %collective-permute-start.2 = (f32[3,16,128]{2,1,0:T(8,128)S(1)}, f32[3,16,128]{2,1,0:T(8,128)S(1)}, u32[]{:S(2)}, u32[]{:S(2)}) collective-permute-start(f32[3,16,128]{2,1,0:T(8,128)S(1)} %get-tuple-element.122), channel_id=1, source_target_pairs={{0,1},{1,0},{2,3},{3,2},{4,5},{5,4},{6,7},{7,6},{8,9},{9,8},{10,11... | collective-permute-start | bytes 73736 | tf_op jit(solution)/shard_map/ppermute | solution.py:38
  23.9 5.5 %collective-permute-start.3 = (f32[3,16,128]{2,1,0:T(8,128)S(1)}, f32[3,16,128]{2,1,0:T(8,128)S(1)}, u32[]{:S(2)}, u32[]{:S(2)}) collective-permute-start(f32[3,16,128]{2,1,0:T(8,128)S(1)} %add.48), channel_id=1, source_target_pairs={{0,2},{1,3},{2,0},{3,1},{4,6},{5,7},{6,4},{7,5},{8,10},{9,11},{10,... | collective-permute-start | bytes 73736 | tf_op jit(solution)/shard_map/ppermute | solution.py:38
  31.0 7.4 %collective-permute-start.6 = (f32[2,3,128,128]{3,2,1,0:T(8,128)S(1)}, f32[2,3,128,128]{3,2,1,0:T(8,128)S(1)}, u32[]{:S(2)}, u32[]{:S(2)}) collective-permute-start(f32[2,3,128,128]{3,2,1,0:T(8,128)S(1)} %get-tuple-element.143), channel_id=1, source_target_pairs={{0,1},{1,0},{2,3},{3,2},{4,5},{5,4},{6,7},{7,6},{8,9},{9,8},{10,11... | collective-permute-start | bytes 1179656 | tf_op jit(solution)/shard_map/ppermute | solution.py:38
  31.1 7.4 %collective-permute-start.7 = (f32[2,3,128,128]{3,2,1,0:T(8,128)S(1)}, f32[2,3,128,128]{3,2,1,0:T(8,128)S(1)}, u32[]{:S(2)}, u32[]{:S(2)}) collective-permute-start(f32[2,3,128,128]{3,2,1,0:T(8,128)S(1)} %get-tuple-element.144), channel_id=1, source_target_pairs={{0,1},{1,0},{2,3},{3,2},{4,5},{5,4},{6,7},{7,6},{8,9},{9,8},{10,11... | collective-permute-start | bytes 1179656 | tf_op jit(solution)/shard_map/ppermute | solution.py:38
  31.6 6.9 %collective-permute-start.8 = (f32[2,3,128,128]{3,2,1,0:T(8,128)S(1)}, f32[2,3,128,128]{3,2,1,0:T(8,128)S(1)}, u32[]{:S(2)}, u32[]{:S(2)}) collective-permute-start(f32[2,3,128,128]{3,2,1,0:T(8,128)S(1)} %get-tuple-element.145), channel_id=1, source_target_pairs={{0,1},{1,0},{2,3},{3,2},{4,5},{5,4},{6,7},{7,6},{8,9},{9,8},{10,11... | collective-permute-start | bytes 1179656 | tf_op jit(solution)/shard_map/ppermute | solution.py:38
  33.3 5.1 %collective-permute-start.9 = (f32[2,3,128,128]{3,2,1,0:T(8,128)S(1)}, f32[2,3,128,128]{3,2,1,0:T(8,128)S(1)}, u32[]{:S(2)}, u32[]{:S(2)}) collective-permute-start(f32[2,3,128,128]{3,2,1,0:T(8,128)S(1)} %get-tuple-element.146), channel_id=1, source_target_pairs={{0,1},{1,0},{2,3},{3,2},{4,5},{5,4},{6,7},{7,6},{8,9},{9,8},{10,11... | collective-permute-start | bytes 1179656 | tf_op jit(solution)/shard_map/ppermute | solution.py:38
  46.2 5.7 %collective-permute-start.13 = (bf16[1,128,128]{2,1,0:T(8,128)(2,1)S(1)}, bf16[1,128,128]{2,1,0:T(8,128)(2,1)S(1)}, u32[]{:S(2)}, u32[]{:S(2)}) collective-permute-start(bf16[1,128,128]{2,1,0:T(8,128)(2,1)S(1)} %get-tuple-element.211), channel_id=1, source_target_pairs={{0,12},{1,13},{2,14},{3,15},{4,8},{5,9},{6,10},{7,11},{8,4},{9,5},... | collective-permute-start | bytes 98312 | tf_op jit(solution)/shard_map/ppermute | solution.py:38
  59.6 6.1 %collective-permute-start.16 = (bf16[1,128,256]{2,1,0:T(8,128)(2,1)S(1)}, bf16[1,128,256]{2,1,0:T(8,128)(2,1)S(1)}, u32[]{:S(2)}, u32[]{:S(2)}) collective-permute-start(bf16[1,128,256]{2,1,0:T(8,128)(2,1)S(1)} %bitcast.16), channel_id=1, source_target_pairs={{0,4},{1,5},{2,6},{3,7},{4,0},{5,1},{6,2},{7,3},{8,12},{9,13},{10,... | collective-permute-start | bytes 196616 | tf_op jit(solution)/shard_map/ppermute | solution.py:38
  59.9 8.0 %collective-permute-start.19 = (bf16[1,128,256]{2,1,0:T(8,128)(2,1)S(1)}, bf16[1,128,256]{2,1,0:T(8,128)(2,1)S(1)}, u32[]{:S(2)}, u32[]{:S(2)}) collective-permute-start(bf16[1,128,256]{2,1,0:T(8,128)(2,1)S(1)} %bitcast.17), channel_id=1, source_target_pairs={{0,12},{1,13},{2,14},{3,15},{4,8},{5,9},{6,10},{7,11},{8,4},{9,5},... | collective-permute-start | bytes 196616 | tf_op jit(solution)/shard_map/ppermute | solution.py:38
  64.0 6.9 %collective-permute-start.18 = (bf16[1,128,256]{2,1,0:T(8,128)(2,1)S(1)}, bf16[1,128,256]{2,1,0:T(8,128)(2,1)S(1)}, u32[]{:S(2)}, u32[]{:S(2)}) collective-permute-start(bf16[1,128,256]{2,1,0:T(8,128)(2,1)S(1)} %bitcast.18), channel_id=1, source_target_pairs={{0,8},{1,9},{2,10},{3,11},{4,12},{5,13},{6,14},{7,15},{8,0},{9,1},... | collective-permute-start | bytes 196616 | tf_op jit(solution)/shard_map/ppermute | solution.py:38
  64.5 6.4 %collective-permute-start.15 = (bf16[1,128,256]{2,1,0:T(8,128)(2,1)S(1)}, bf16[1,128,256]{2,1,0:T(8,128)(2,1)S(1)}, u32[]{:S(2)}, u32[]{:S(2)}) collective-permute-start(bf16[1,128,256]{2,1,0:T(8,128)(2,1)S(1)} %bitcast.19), channel_id=1, source_target_pairs={{0,2},{1,3},{2,0},{3,1},{4,6},{5,7},{6,4},{7,5},{8,10},{9,11},{10,... | collective-permute-start | bytes 196616 | tf_op jit(solution)/shard_map/ppermute | solution.py:38
  70.9 5.4 %collective-permute-start.20 = (bf16[2,128,256]{2,1,0:T(8,128)(2,1)S(1)}, bf16[2,128,256]{2,1,0:T(8,128)(2,1)S(1)}, u32[]{:S(2)}, u32[]{:S(2)}) collective-permute-start(bf16[2,128,256]{2,1,0:T(8,128)(2,1)S(1)} %pad_maximum_fusion.5), channel_id=1, source_target_pairs={{0,2},{1,3},{2,0},{3,1},{4,6},{5,7},{6,4},{7,5},{8,10},{9,11},{10,... | collective-permute-start | bytes 393224 | tf_op jit(solution)/shard_map/ppermute | solution.py:38
  88.2 8.4 %collective-permute-start.27 = (f32[2,3,128,128]{3,2,1,0:T(8,128)S(1)}, f32[2,3,128,128]{3,2,1,0:T(8,128)S(1)}, u32[]{:S(2)}, u32[]{:S(2)}) collective-permute-start(f32[2,3,128,128]{3,2,1,0:T(8,128)S(1)} %get-tuple-element.191), channel_id=1, source_target_pairs={{0,1},{1,0},{2,3},{3,2},{4,5},{5,4},{6,7},{7,6},{8,9},{9,8},{10,11... | collective-permute-start | bytes 1179656 | tf_op jit(solution)/shard_map/ppermute | solution.py:38
  89.7 7.0 %collective-permute-start.28 = (f32[2,3,128,128]{3,2,1,0:T(8,128)S(1)}, f32[2,3,128,128]{3,2,1,0:T(8,128)S(1)}, u32[]{:S(2)}, u32[]{:S(2)}) collective-permute-start(f32[2,3,128,128]{3,2,1,0:T(8,128)S(1)} %get-tuple-element.192), channel_id=1, source_target_pairs={{0,1},{1,0},{2,3},{3,2},{4,5},{5,4},{6,7},{7,6},{8,9},{9,8},{10,11... | collective-permute-start | bytes 1179656 | tf_op jit(solution)/shard_map/ppermute | solution.py:38
  90.3 6.4 %collective-permute-start.29 = (f32[2,3,128,128]{3,2,1,0:T(8,128)S(1)}, f32[2,3,128,128]{3,2,1,0:T(8,128)S(1)}, u32[]{:S(2)}, u32[]{:S(2)}) collective-permute-start(f32[2,3,128,128]{3,2,1,0:T(8,128)S(1)} %get-tuple-element.193), channel_id=1, source_target_pairs={{0,1},{1,0},{2,3},{3,2},{4,5},{5,4},{6,7},{7,6},{8,9},{9,8},{10,11... | collective-permute-start | bytes 1179656 | tf_op jit(solution)/shard_map/ppermute | solution.py:38
  103.7 5.7 %collective-permute-start.34 = (bf16[1,128,128]{2,1,0:T(8,128)(2,1)S(1)}, bf16[1,128,128]{2,1,0:T(8,128)(2,1)S(1)}, u32[]{:S(2)}, u32[]{:S(2)}) collective-permute-start(bf16[1,128,128]{2,1,0:T(8,128)(2,1)S(1)} %get-tuple-element.208), channel_id=1, source_target_pairs={{0,12},{1,13},{2,14},{3,15},{4,8},{5,9},{6,10},{7,11},{8,4},{9,5},... | collective-permute-start | bytes 98312 | tf_op jit(solution)/shard_map/ppermute | solution.py:38
  105.8 5.2 %collective-permute-start.33 = (bf16[1,128,128]{2,1,0:T(8,128)(2,1)S(1)}, bf16[1,128,128]{2,1,0:T(8,128)(2,1)S(1)}, u32[]{:S(2)}, u32[]{:S(2)}) collective-permute-start(bf16[1,128,128]{2,1,0:T(8,128)(2,1)S(1)} %get-tuple-element.209), channel_id=1, source_target_pairs={{0,8},{1,9},{2,10},{3,11},{4,12},{5,13},{6,14},{7,15},{8,0},{9,1},... | collective-permute-start | bytes 98312 | tf_op jit(solution)/shard_map/ppermute | solution.py:38
  122.1 6.9 %collective-permute-start.40 = (bf16[1,128,256]{2,1,0:T(8,128)(2,1)S(1)}, bf16[1,128,256]{2,1,0:T(8,128)(2,1)S(1)}, u32[]{:S(2)}, u32[]{:S(2)}) collective-permute-start(bf16[1,128,256]{2,1,0:T(8,128)(2,1)S(1)} %bitcast.11), channel_id=1, source_target_pairs={{0,12},{1,13},{2,14},{3,15},{4,8},{5,9},{6,10},{7,11},{8,4},{9,5},... | collective-permute-start | bytes 196616 | tf_op jit(solution)/shard_map/ppermute | solution.py:38
  124.6 6.5 %collective-permute-start.39 = (bf16[1,128,256]{2,1,0:T(8,128)(2,1)S(1)}, bf16[1,128,256]{2,1,0:T(8,128)(2,1)S(1)}, u32[]{:S(2)}, u32[]{:S(2)}) collective-permute-start(bf16[1,128,256]{2,1,0:T(8,128)(2,1)S(1)} %bitcast.12), channel_id=1, source_target_pairs={{0,8},{1,9},{2,10},{3,11},{4,12},{5,13},{6,14},{7,15},{8,0},{9,1},... | collective-permute-start | bytes 196616 | tf_op jit(solution)/shard_map/ppermute | solution.py:38
  124.6 6.5 %collective-permute-start.36 = (bf16[1,128,256]{2,1,0:T(8,128)(2,1)S(1)}, bf16[1,128,256]{2,1,0:T(8,128)(2,1)S(1)}, u32[]{:S(2)}, u32[]{:S(2)}) collective-permute-start(bf16[1,128,256]{2,1,0:T(8,128)(2,1)S(1)} %bitcast.13), channel_id=1, source_target_pairs={{0,2},{1,3},{2,0},{3,1},{4,6},{5,7},{6,4},{7,5},{8,10},{9,11},{10,... | collective-permute-start | bytes 196616 | tf_op jit(solution)/shard_map/ppermute | solution.py:38
  125.9 5.2 %collective-permute-start.38 = (bf16[1,128,256]{2,1,0:T(8,128)(2,1)S(1)}, bf16[1,128,256]{2,1,0:T(8,128)(2,1)S(1)}, u32[]{:S(2)}, u32[]{:S(2)}) collective-permute-start(bf16[1,128,256]{2,1,0:T(8,128)(2,1)S(1)} %collective-permute-done.37), channel_id=1, source_target_pairs={{0,2},{1,3},{2,0},{3,1},{4,6},{5,7},{6,4},{7,5},{8,10},{9,11},{10,... | collective-permute-start | bytes 196616 | tf_op jit(solution)/shard_map/ppermute | solution.py:38
  131.1 5.5 %collective-permute-start.41 = (bf16[2,128,256]{2,1,0:T(8,128)(2,1)S(1)}, bf16[2,128,256]{2,1,0:T(8,128)(2,1)S(1)}, u32[]{:S(2)}, u32[]{:S(2)}) collective-permute-start(bf16[2,128,256]{2,1,0:T(8,128)(2,1)S(1)} %pad_maximum_fusion.7), channel_id=1, source_target_pairs={{0,2},{1,3},{2,0},{3,1},{4,6},{5,7},{6,4},{7,5},{8,10},{9,11},{10,... | collective-permute-start | bytes 393224 | tf_op jit(solution)/shard_map/ppermute | solution.py:38
  (24 other events, 98.9 us)

commit v5 on v4

--- a/solution.py
+++ b/solution.py
@@ -49,12 +49,18 @@
             diag_ref[component, spot, :] += piece
 
 
-def edge_rows_kernel(orbitals_ref, last_ref, first_ref, held_ref, sems):
-    row_count = orbitals_ref.shape[0]
-    spots = (orbitals_ref.at[row_count - BLK :], orbitals_ref.at[:BLK])
-    loads = [pltpu.make_async_copy(spots[i], held_ref.at[i], sems.at[i]) for i in (0, 1)]
+def edge_rows_kernel(me_ref, orbitals_ref, chip_ref, next_ref, held_ref, sems):
+    span = orbitals_ref.shape[0] - BLK
+    even = 1 - (me_ref[0] & 1)
+    starts = (even * span, (1 - even) * span)
+    loads = [
+        pltpu.make_async_copy(
+            orbitals_ref.at[pl.ds(pl.multiple_of(starts[i], BLK), BLK)], held_ref.at[i], sems.at[i]
+        )
+        for i in (0, 1)
+    ]
     stores = [
-        pltpu.make_async_copy(held_ref.at[i], (last_ref, first_ref)[i], sems.at[2 + i])
+        pltpu.make_async_copy(held_ref.at[i], (chip_ref, next_ref)[i], sems.at[2 + i])
         for i in (0, 1)
     ]
     for load in loads:
@@ -66,13 +72,13 @@
         store.wait()
 
 
-def edge_rows(orbitals):
+def edge_rows(me, orbitals):
     shape = jax.ShapeDtypeStruct((BLK, orbitals.shape[1]), BF16)
     hbm = pl.BlockSpec(memory_space=pltpu.HBM)
     return pl.pallas_call(
         edge_rows_kernel,
         out_shape=(shape, shape),
-        in_specs=[hbm],
+        in_specs=[SMEM, hbm],
         out_specs=(hbm, hbm),
         scratch_shapes=[
             pltpu.VMEM((2, BLK, orbitals.shape[1]), BF16),
@@ -80,34 +86,38 @@
         ],
         compiler_params=params(56 * 1024 * 1024),
         name="edge_rows",
-    )(orbitals)
+    )(me, orbitals)
+
+
+def put_images(blocks_ref, cols_ref, window, b, tile, image_ref, diag_ref, first):
+    out = jnp.dot(blocks_ref[b], window, preferred_element_type=F32).astype(BF16)
+    own = cols_ref[b * BLK : (b + 1) * BLK, tile]
+    for k in range(3):
+        image = out[k * BLK : (k + 1) * BLK]
+        image_ref[k, b * BLK : (b + 1) * BLK, tile] = image
+        put_diag(diag_ref, k, tile.start // HALF, own, image, first)
 
 
 def inner_kernel(block_rows, blocks_ref, cols_ref, image_ref, diag_ref):
     for start in range(0, cols_ref.shape[1], TILE):
         tile = slice(start, start + TILE)
         for b in range(1, block_rows - 1):
-            out = jnp.dot(
-                blocks_ref[b],
-                cols_ref[(b - 1) * BLK : (b + 2) * BLK, tile],
-                preferred_element_type=F32,
-            ).astype(BF16)
-            own = cols_ref[b * BLK : (b + 1) * BLK, tile]
-            for k in range(3):
-                image = out[k * BLK : (k + 1) * BLK]
-                image_ref[k, (b - 1) * BLK : b * BLK, tile] = image
-                put_diag(diag_ref, k, start // HALF, own, image, b == 1)
+            window = cols_ref[(b - 1) * BLK : (b + 2) * BLK, tile]
+            put_images(blocks_ref, cols_ref, window, b, tile, image_ref, diag_ref, b == 1)
+
+
+def image_shapes(orbitals):
+    row_count, orb_count = orbitals.shape
+    return (
+        jax.ShapeDtypeStruct((3, row_count, orb_count), BF16),
+        jax.ShapeDtypeStruct((3, orb_count // HALF, HALF), F32),
+    )
 
 
 def inner_images(blocks, orbitals):
-    row_count, orb_count = orbitals.shape
-    block_rows = row_count // BLK
-    return pl.pallas_call(
-        functools.partial(inner_kernel, block_rows),
-        out_shape=(
-            jax.ShapeDtypeStruct((3, row_count - 2 * BLK, orb_count), BF16),
-            jax.ShapeDtypeStruct((3, orb_count // HALF, HALF), F32),
-        ),
+    return pl.pallas_call(
+        functools.partial(inner_kernel, orbitals.shape[0] // BLK),
+        out_shape=image_shapes(orbitals),
         in_specs=[VMEM, VMEM],
         out_specs=(VMEM, VMEM),
         compiler_params=params(),
@@ -115,39 +125,43 @@
     )(blocks, orbitals)
 
 
-def edge_kernel(block_rows, blocks_ref, cols_ref, low_ref, high_ref, start_ref, image_ref, diag_ref):
-    diag_ref[...] = start_ref[...]
-    for start in range(0, cols_ref.shape[1], TILE):
-        tile = slice(start, start + TILE)
-        for place, b in ((0, 0), (1, block_rows - 1)):
+def edge_kernel(
+    block_rows, on_chip, me_ref, blocks_ref, cols_ref, came_ref, *refs
+):
+    old_diag_ref, image_ref, diag_ref = refs[1:]
+    even = (me_ref[0] & 1) == 0
+    last = even if on_chip else jnp.logical_not(even)
+    diag_ref[...] = old_diag_ref[...]
+
+    def put(b):
+        for start in range(0, cols_ref.shape[1], TILE):
+            tile = slice(start, start + TILE)
             if b == 0:
-                window = jnp.concatenate([low_ref[:, tile], cols_ref[: 2 * BLK, tile]], axis=0)
+                pieces = [came_ref[:, tile], cols_ref[: 2 * BLK, tile]]
             else:
-                window = jnp.concatenate(
-                    [cols_ref[(b - 1) * BLK :, tile], high_ref[:, tile]], axis=0
-                )
-            out = jnp.dot(blocks_ref[b], window, preferred_element_type=F32).astype(BF16)
-            own = cols_ref[b * BLK : (b + 1) * BLK, tile]
-            for k in range(3):
-                image = out[k * BLK : (k + 1) * BLK]
-                image_ref[k, place * BLK : (place + 1) * BLK, tile] = image
-                put_diag(diag_ref, k, start // HALF, own, image, False)
-
-
-def edge_images(blocks, orbitals, low, high, start):
-    row_count, orb_count = orbitals.shape
-    block_rows = row_count // BLK
-    return pl.pallas_call(
-        functools.partial(edge_kernel, block_rows),
-        out_shape=(
-            jax.ShapeDtypeStruct((3, 2 * BLK, orb_count), BF16),
-            jax.ShapeDtypeStruct((3, orb_count // HALF, HALF), F32),
-        ),
-        in_specs=[VMEM] * 5,
+                pieces = [cols_ref[(b - 1) * BLK :, tile], came_ref[:, tile]]
+            window = jnp.concatenate(pieces, axis=0)
+            put_images(blocks_ref, cols_ref, window, b, tile, image_ref, diag_ref, False)
+
+    @pl.when(last)
+    def _():
+        put(block_rows - 1)
+
+    @pl.when(jnp.logical_not(last))
+    def _():
+        put(0)
+
+
+def edge_images(me, blocks, orbitals, came, images, diag, on_chip):
+    return pl.pallas_call(
+        functools.partial(edge_kernel, orbitals.shape[0] // BLK, on_chip),
+        out_shape=image_shapes(orbitals),
+        in_specs=[SMEM] + [VMEM] * 5,
         out_specs=(VMEM, VMEM),
+        input_output_aliases={4: 0, 5: 1},
         compiler_params=params(),
         name="edge_images",
-    )(blocks, orbitals, low, high, start)
+    )(me, blocks, orbitals, came, images, diag)
 
 
 def lower_mask():
@@ -163,22 +177,13 @@
     )
 
 
-def pair_image(refs, component, places):
-    pieces = [pair_columns(ref, (component,), places) for ref in refs]
-    if len(pieces) == 1:
-        return pieces[0]
-    inner, edge = pieces
-    return jnp.concatenate([edge[:BLK], inner, edge[BLK:]], axis=0)
-
-
-def gram_kernel(first, place_ref, me_ref, cols_ref, *refs):
-    image_refs, keep_ref, send_ref = refs[:-2], refs[-2], refs[-1]
+def gram_kernel(first, place_ref, me_ref, cols_ref, image_ref, keep_ref, send_ref):
     mine = (me_ref[0] & 1) == 0
     low = lower_mask()
     for i in range(keep_ref.shape[0]):
         places = [place_ref[2 * (first + i) + h] for h in (0, 1)]
         cols = pair_columns(cols_ref, (), places)
-        images = jnp.concatenate([pair_image(image_refs, k, places) for k in range(3)], axis=1)
+        images = jnp.concatenate([pair_columns(image_ref, (k,), places) for k in range(3)], axis=1)
         mats = lax.dot_general(cols, images, (((0,), (0,)), ((), ())), preferred_element_type=F32)
         for k in range(3):
             mat = mats[:, k * PAIR : (k + 1) * PAIR]
@@ -194,11 +199,11 @@
     return pl.pallas_call(
         functools.partial(gram_kernel, first),
         out_shape=(shape, shape),
-        in_specs=[SMEM, SMEM] + [VMEM] * (1 + len(images)),
+        in_specs=[SMEM, SMEM, VMEM, VMEM],
         out_specs=(VMEM, VMEM),
         compiler_params=params(),
         name="pair_products",
-    )(place, me, cols, *images)
+    )(place, me, cols, images)
 
 
 def weight_kernel(sub_bits, stays, place_ref, me_ref, diag_ref, *refs):
@@ -348,10 +353,10 @@
     )
 
 
-def rotate_kernel(first, earlier, place_ref, me_ref, gathered_ref, cols_ref, *refs):
+def rotate_kernel(first, place_ref, me_ref, gathered_ref, cols_ref, old_ref, *refs):
     subs = PAIR // gathered_ref.shape[1]
     my_pair = me_ref[0] // subs
-    image_refs, (out_ref, image_ref, diag_ref) = refs[: -3 - earlier], refs[-3:]
+    out_ref, image_ref, diag_ref = refs[-3:]
     for slot in range(gathered_ref.shape[0] // subs):
         p = my_pair ^ (first + slot)
         rotation = assemble(gathered_ref, me_ref[0], slot)
@@ -361,7 +366,7 @@
         turned = jnp.dot(cols, rotation, preferred_element_type=F32).astype(BF16)
         out_ref[:, spot] = turned
         for k in range(3):
-            image = pair_image(image_refs, k, places)
+            image = pair_columns(old_ref, (k,), places)
             moved = jnp.dot(image, rotation, preferred_element_type=F32).astype(BF16)
             image_ref[k, :, spot] = moved
             put_diag(diag_ref, k, 2 * p, turned, moved, True)
@@ -369,15 +374,15 @@
 
 def rotate(place, me, gathered, cols, images, first, earlier):
     row_count, orb_count = cols.shape
-    operands = [place, me, gathered, cols, *images]
-    return pl.pallas_call(
-        functools.partial(rotate_kernel, first, len(earlier)),
+    operands = [place, me, gathered, cols, images]
+    return pl.pallas_call(
+        functools.partial(rotate_kernel, first),
         out_shape=(
             jax.ShapeDtypeStruct((row_count, orb_count), BF16),
             jax.ShapeDtypeStruct((3, row_count, orb_count), BF16),
             jax.ShapeDtypeStruct((3, orb_count // HALF, HALF), F32),
         ),
-        in_specs=[SMEM, SMEM] + [VMEM] * (2 + len(images) + len(earlier)),
+        in_specs=[SMEM, SMEM] + [VMEM] * (3 + len(earlier)),
         out_specs=(VMEM, VMEM, VMEM),
         cost_estimate=pl.CostEstimate(
             flops=8 * row_count * PAIR * PAIR * gathered.shape[0] * gathered.shape[1] // PAIR,
@@ -390,38 +395,74 @@
     )(*operands, *earlier)
 
 
-def last_kernel(parts, place_ref, home_ref, me_ref, *refs):
-    gathered_refs, (cols_ref, out_ref) = refs[:parts], refs[parts:]
-    subs = PAIR // gathered_refs[0].shape[1]
-    my_pair = me_ref[0] // subs
-    done = 0
-    for gathered_ref in gathered_refs:
-        for slot in range(gathered_ref.shape[0] // subs):
-            p = my_pair ^ done
-            done += 1
-            rotation = assemble(gathered_ref, me_ref[0], slot)
-            places = [place_ref[2 * p + h] for h in (0, 1)]
-            cols = pair_columns(cols_ref, (), places)
+def turn_kernel(place_ref, me_ref, gathered_ref, cols_ref, out_ref):
+    subs = PAIR // gathered_ref.shape[1]
+    for slot in range(gathered_ref.shape[0] // subs):
+        p = (me_ref[0] // subs) ^ slot
+        rotation = assemble(gathered_ref, me_ref[0], slot)
+        cols = pair_columns(cols_ref, (), [place_ref[2 * p + h] for h in (0, 1)])
+        turned = jnp.dot(cols, rotation, preferred_element_type=F32).astype(BF16)
+        out_ref[:, slot * PAIR : (slot + 1) * PAIR] = turned
+
+
+def turn_near(place, me, gathered, cols):
+    row_count = cols.shape[0]
+    subs = PAIR // gathered.shape[1]
+    slots = gathered.shape[0] // subs
+    return pl.pallas_call(
+        turn_kernel,
+        out_shape=jax.ShapeDtypeStruct((row_count, slots * PAIR), BF16),
+        in_specs=[SMEM, SMEM, VMEM, VMEM],
+        out_specs=VMEM,
+        compiler_params=params(),
+        name="turn_near",
+    )(place, me, gathered, cols)
+
+
+def last_kernel(
+    place_ref, home_ref, me_ref, turned_ref, gathered_ref, cols_ref, out_ref, held_ref, sems
+):
+    subs = PAIR // gathered_ref.shape[1]
+    near = turned_ref.shape[1] // PAIR
+    copies = []
+    for slot in range(near + gathered_ref.shape[0] // subs):
+        p = (me_ref[0] // subs) ^ slot
+        if slot < near:
+            source_ref, start = turned_ref, slot * PAIR
+        else:
+            source_ref, start = held_ref, (slot - near) * PAIR
+            rotation = assemble(gathered_ref, me_ref[0], slot - near)
+            cols = pair_columns(cols_ref, (), [place_ref[2 * p + h] for h in (0, 1)])
             turned = jnp.dot(cols, rotation, preferred_element_type=F32).astype(BF16)
-            for h in (0, 1):
-                home = pl.multiple_of(home_ref[2 * p + h] * HALF, HALF)
-                out_ref[:, pl.ds(home, HALF)] = turned[:, h * HALF : (h + 1) * HALF]
-
-
-def rotate_last(place, home, me, gathered, cols):
+            held_ref[:, start : start + PAIR] = turned
+        for h in (0, 1):
+            home = pl.multiple_of(home_ref[2 * p + h] * HALF, HALF)
+            copies.append(
+                pltpu.make_async_copy(
+                    source_ref.at[:, pl.ds(start + h * HALF, HALF)],
+                    out_ref.at[:, pl.ds(home, HALF)],
+                    sems.at[2 * slot + h],
+                )
+            )
+            copies[-1].start()
+    for copy in copies:
+        copy.wait()
+
+
+def rotate_last(place, home, me, turned, gathered, cols):
     row_count, orb_count = cols.shape
-    rows = row_count // 2
-    return pl.pallas_call(
-        functools.partial(last_kernel, len(gathered)),
+    return pl.pallas_call(
+        last_kernel,
         out_shape=jax.ShapeDtypeStruct((row_count, orb_count), BF16),
-        grid=(row_count // rows,),
-        in_specs=[SMEM, SMEM, SMEM]
-        + [pl.BlockSpec(part.shape, lambda r: (0, 0, 0)) for part in gathered]
-        + [pl.BlockSpec((rows, orb_count), lambda r: (r, 0))],
-        out_specs=pl.BlockSpec((rows, orb_count), lambda r: (r, 0)),
+        in_specs=[SMEM, SMEM, SMEM, VMEM, VMEM, VMEM],
+        out_specs=pl.BlockSpec(memory_space=pltpu.HBM),
+        scratch_shapes=[
+            pltpu.VMEM((row_count, orb_count - turned.shape[1]), BF16),
+            pltpu.SemaphoreType.DMA((orb_count // HALF,)),
+        ],
         compiler_params=params(),
         name="rotate_last",
-    )(place, home, me, *gathered, cols)
+    )(place, home, me, turned, gathered, cols)
 
 
 def sum_beside(diag, makers):
@@ -457,7 +498,9 @@
 def spread(value, places, low_bit, wire):
     ways = len(places)
     value = value.reshape((ways, -1) + value.shape[1:])
-    pieces = [swap(pick(value, places[q]).astype(wire), q << low_bit) for q in range(1, ways)]
+    pieces = [
+        swap(pick(value, places[q]).astype(wire), q << low_bit) for q in range(ways - 1, 0, -1)
+    ]
     own = pick(value, places[0])
     for piece in pieces:
         own = own + piece.astype(F32)
@@ -506,11 +549,12 @@
     sub_bits = bits_of(count) - pair_bits
     basis_count = row_count * count
     block_rows = row_count // BLK
-    last, first = edge_rows(orbitals)
-    orbitals, matchings, last, first = lax.optimization_barrier(
-        (orbitals, matchings, last, first)
-    )
     position = lax.axis_index("orb").astype(jnp.int32)
+    for_chip, for_next = edge_rows(position.reshape(1), orbitals)
+    from_chip = swap(for_chip, 1)
+    joints = [(i, i + 1) for i in range(1, count - 1, 2)]
+    from_next = lax.ppermute(for_next, "orb", joints + [(j, i) for i, j in joints])
+    orbitals, matchings, for_next = lax.optimization_barrier((orbitals, matchings, for_next))
     places = places_of(position, sub_bits, pair_bits)
     ident = jnp.arange(block_count, dtype=jnp.int32)
     held = [ident] + [matchings[r] for r in range(ROUNDS - 1)]
@@ -518,23 +562,21 @@
     for r in range(ROUNDS):
         found = jnp.where(matchings[r][:, None] == held[r][None, :], ident[None, :], 0)
         spots.append(jnp.sum(found, axis=1).astype(jnp.int32))
-    forward = [(i, i + 1) for i in range(count - 1)]
-    backward = [(i + 1, i) for i in range(count - 1)]
     orbitals, places, spots, me = lax.optimization_barrier(
         (orbitals, places, spots, position.reshape(1))
     )
-    low = lax.ppermute(last, "orb", forward)
-    high = lax.ppermute(first, "orb", backward)
+
     mask_full = jnp.stack(
         [coupling_mask[:, 0], jnp.ones((block_rows,), jnp.int32), coupling_mask[:, 1]], axis=1
     ).astype(BF16)
     blocks = jnp.transpose(
         dipole_blocks * mask_full[None, :, :, None, None], (1, 0, 3, 2, 4)
     ).reshape(block_rows, 3 * BLK, 3 * BLK)
-    inner, diag = inner_images(blocks, orbitals)
-    edge, diag = edge_images(blocks, orbitals, low, high, diag)
-
-    cols, images = orbitals, (inner, edge)
+    images, diag = inner_images(blocks, orbitals)
+    images, diag = edge_images(me, blocks, orbitals, from_chip, images, diag, True)
+    from_next, images, diag = lax.optimization_barrier((from_next, images, diag))
+    images, diag = edge_images(me, blocks, orbitals, from_next, images, diag, False)
+    cols = orbitals
     for round_index in range(ROUNDS):
         place = spots[round_index]
         splits = 4
@@ -561,13 +603,14 @@
         near, far = gather_pairs(share[None], sub_bits, pair_bits)
         if round_index + 1 < ROUNDS:
             earlier = rotate(place, me, near, cols, images, 0, ())
+        else:
+            turned = turn_near(place, me, near, cols)
         for bit in range(sub_bits):
             far = gather_bits(far, 1, bit)
         if round_index + 1 < ROUNDS:
             half = pair_count // 2
-            cols, moved, diag = rotate(place, me, far, cols, images, half, earlier)
-            images = (moved,)
-    return rotate_last(place, matchings[ROUNDS - 1], me, (near, far), cols)
+            cols, images, diag = rotate(place, me, far, cols, images, half, earlier)
+    return rotate_last(place, matchings[ROUNDS - 1], me, turned, far, cols)
 
 
 def solution(mesh):

time: 141 us -> 140 us (level)
  waiting for transfers between devices: 42.7 us -> 37.6 us
  Pallas kernels: 44.7 us -> 46.8 us
  starting transfers between devices: 46.4 us -> 48.4 us
    ppermute x42 -> x43, waiting for transfers between devices: 42.7 us -> 37.6 us  [swap(): return lax.ppermute(block, 'orb', [(i, i ^ distance) for i in range(count)])]
    ppermute x42 -> x43, starting transfers between devices: 42 us -> 47 us  [swap(): return lax.ppermute(block, 'orb', [(i, i ^ distance) for i in range(count)])]
    ppermute x2 -> x1, starting transfers between devices: 4.45 us -> 1.45 us  [per_device(): lax.ppermute(for_next, 'orb', joints + [(j, i) for i, j in joints])]
    pallas_call x6 -> x8, Pallas kernels: 14.4 us -> 16 us  [the longest x2 4.38 us: rotate(): pl.pallas_call(functools.partial(rotate_kernel, first), out_shape=(jax.Sh...]
  transfers between devices with their start and end apart: 44 -> 44, of which waited for: 23 -> 24; matrix products, arithmetic and copies ran while one was open for 4% -> 5% of each run, Pallas kernels for 13% -> 15%
where the time goes in v5:
time: 140 us
  starting transfers between devices  48.4 us (35%)
  Pallas kernels  46.8 us (33%)
  waiting for transfers between devices  37.6 us (27%)
  local copies, waits for them, and re-layouts  5.98 us (4%)
    ppermute x43, starting transfers between devices, swap(): return lax.ppermute(block, 'orb', [(i, i ^ distance) for i in range(count)])  47 us
    ppermute x43, waiting for transfers between devices, swap(): return lax.ppermute(block, 'orb', [(i, i ^ distance) for i in range(count)])  37.6 us
    pallas_call x2, Pallas kernels, rotation_share(): pl.pallas_call(functools.partial(rotation_kernel, scale, subs), out_shape...  13.6 us
    pallas_call x8, Pallas kernels, pair_products(): pl.pallas_call(functools.partial(gram_kernel, first), out_shape=(shape, s...  11.9 us
    pallas_call x4, Pallas kernels, weigh(): pl.pallas_call(functools.partial(weight_kernel, sub_bits, stays), out_sha...  5.29 us
    pallas_call x2, Pallas kernels, rotate(): pl.pallas_call(functools.partial(rotate_kernel, first), out_shape=(jax.Sh...  4.38 us
    pallas_call x2, Pallas kernels, edge_images(): pl.pallas_call(functools.partial(edge_kernel, orbitals.shape[0] // BLK, o...  4.33 us
    reshape x1, local copies, waits for them, and re-layouts, per_device(): blocks = jnp.transpose(dipole_blocks * mask_full[None, :, :, None, None],...  3.36 us
  transfers between devices with their start and end apart: 44, of which 24 were waited for; matrix products, arithmetic and copies ran while one was open for 5% of the time, Pallas kernels for 15%

profile of v5, /device:TPU:0, one launch (start us, length us, event | category | flops | bytes accessed | tf_op | source)
XLA Modules:
  0.0 140.3 jit_solution(17741982048386961277)
XLA Ops:
  0.0 2.2 %edge_rows.1 = (bf16[128,2048]{1,0:T(8,128)(2,1)}, bf16[128,2048]{1,0:T(8,128)(2,1)}) custom-call(s32[1]{0:T(128)} %bitcast.me_ref, bf16[512,2048]{1,0:T(8,128)(2,1)} %cols_ref.8), custom_call_target="tpu_custom_call" | custom-call | tf_op jit(solution)/shard_map/edge_rows/pallas_call | solution.py:78
  4.8 2.2 %copy.17 = bf16[4,3,128,3,128]{4,3,2,1,0:T(4,128)(2,1)} copy(bf16[4,3,128,3,128]{4,2,3,0,1:T(8,128)(2,1)S(1)} %multiply_bitcast_fusion) | data formatting | bytes 2359296 | tf_op jit(solution)/shard_map/transpose | solution.py:572
  7.0 3.4 %reshape.59.blocks_ref = bf16[4,384,384]{2,1,0:T(8,128)(2,1)S(1)} reshape(bf16[4,3,128,3,128]{4,3,2,1,0:T(4,128)(2,1)} %copy.17) | data formatting | bytes 2359296 | tf_op jit(solution)/shard_map/reshape | solution.py:574
  14.4 2.2 %edge_images.3 = (bf16[3,512,2048]{2,1,0:T(8,128)(2,1)S(1)}, f32[3,16,128]{2,1,0:T(8,128)S(1)}) custom-call(s32[1]{0:T(128)} %bitcast.me_ref, bf16[4,384,384]{2,1,0:T(8,128)(2,1)S(1)} %reshape.59.blocks_ref, bf16[512,2048]{1,0:T(8,128)(2,1)S(1)} %copy-done, ...), custom_call_target="tpu_custom_call", output_to_operand_aliasing={{0}: (4, {}), {1}: (5, {})} | custom-call | tf_op jit(solution)/shard_map/edge_images/pallas_call | solution.py:156
  16.6 5.0 %collective-permute-start.2 = (f32[3,16,128]{2,1,0:T(8,128)S(1)}, f32[3,16,128]{2,1,0:T(8,128)S(1)}, u32[]{:S(2)}, u32[]{:S(2)}) collective-permute-start(f32[3,16,128]{2,1,0:T(8,128)S(1)} %get-tuple-element.128), channel_id=1, source_target_pairs={{0,1},{1,0},{2,3},{3,2},{4,5},{5,4},{6,7},{7,6},{8,9},{9,8},{10,11... | collective-permute-start | bytes 73736 | tf_op jit(solution)/shard_map/ppermute | solution.py:38
  23.2 2.4 %collective-permute-start.3 = (f32[3,16,128]{2,1,0:T(8,128)S(1)}, f32[3,16,128]{2,1,0:T(8,128)S(1)}, u32[]{:S(2)}, u32[]{:S(2)}) collective-permute-start(f32[3,16,128]{2,1,0:T(8,128)S(1)} %add.48), channel_id=1, source_target_pairs={{0,2},{1,3},{2,0},{3,1},{4,6},{5,7},{6,4},{7,5},{8,10},{9,11},{10,... | collective-permute-start | bytes 73736 | tf_op jit(solution)/shard_map/ppermute | solution.py:38
  32.9 2.3 %collective-permute-start.5 = (f32[3,16,128]{2,1,0:T(8,128)S(1)}, f32[3,16,128]{2,1,0:T(8,128)S(1)}, u32[]{:S(2)}, u32[]{:S(2)}) collective-permute-start(f32[3,16,128]{2,1,0:T(8,128)S(1)} %add.50), channel_id=1, source_target_pairs={{0,8},{1,9},{2,10},{3,11},{4,12},{5,13},{6,14},{7,15},{8,0},{9,1},... | collective-permute-start | bytes 73736 | tf_op jit(solution)/shard_map/ppermute | solution.py:38
  35.2 2.4 %collective-permute-done.5 = f32[3,16,128]{2,1,0:T(8,128)S(1)} collective-permute-done((f32[3,16,128]{2,1,0:T(8,128)S(1)}, f32[3,16,128]{2,1,0:T(8,128)S(1)}, u32[]{:S(2)}, u32[]{:S(2)}) %collective-permute-start.5) | collective-permute-done | bytes 24608 | tf_op jit(solution)/shard_map/ppermute | solution.py:38
  41.4 2.6 %collective-permute-done.10 = bf16[4,128,128]{2,1,0:T(8,128)(2,1)S(1)} collective-permute-done((bf16[4,128,128]{2,1,0:T(8,128)(2,1)S(1)}, bf16[4,128,128]{2,1,0:T(8,128)(2,1)S(1)}, u32[]{:S(2)}, u32[]{:S(2)}) %collective-permute-start.10) | collective-permute-done | bytes 131104 | tf_op jit(solution)/shard_map/ppermute | solution.py:38
  44.1 3.3 %collective-permute-start.11 = (bf16[1,128,128]{2,1,0:T(8,128)(2,1)S(1)}, bf16[1,128,128]{2,1,0:T(8,128)(2,1)S(1)}, u32[]{:S(2)}, u32[]{:S(2)}) collective-permute-start(bf16[1,128,128]{2,1,0:T(8,128)(2,1)S(1)} %get-tuple-element.216), channel_id=1, source_target_pairs={{0,12},{1,13},{2,14},{3,15},{4,8},{5,9},{6,10},{7,11},{8,4},{9,5},... | collective-permute-start | bytes 98312 | tf_op jit(solution)/shard_map/ppermute | solution.py:38
  53.6 4.4 %rotation.2 = bf16[128,256]{1,0:T(8,128)(2,1)S(1)} custom-call(s32[1]{0:T(128)} %bitcast.me_ref, f32[2,128,128]{2,1,0:T(8,128)S(1)} %pad_maximum_fusion.4.packed_ref), custom_call_target="tpu_custom_call" | custom-call | tf_op jit(solution)/shard_map/rotation/pallas_call | solution.py:336
  60.2 2.2 %collective-permute-start.19 = (bf16[1,128,256]{2,1,0:T(8,128)(2,1)S(1)}, bf16[1,128,256]{2,1,0:T(8,128)(2,1)S(1)}, u32[]{:S(2)}, u32[]{:S(2)}) collective-permute-start(bf16[1,128,256]{2,1,0:T(8,128)(2,1)S(1)} %bitcast.17), channel_id=1, source_target_pairs={{0,12},{1,13},{2,14},{3,15},{4,8},{5,9},{6,10},{7,11},{8,4},{9,5},... | collective-permute-start | bytes 196616 | tf_op jit(solution)/shard_map/ppermute | solution.py:38
  62.8 2.8 %collective-permute-start.15 = (bf16[1,128,256]{2,1,0:T(8,128)(2,1)S(1)}, bf16[1,128,256]{2,1,0:T(8,128)(2,1)S(1)}, u32[]{:S(2)}, u32[]{:S(2)}) collective-permute-start(bf16[1,128,256]{2,1,0:T(8,128)(2,1)S(1)} %bitcast.19), channel_id=1, source_target_pairs={{0,2},{1,3},{2,0},{3,1},{4,6},{5,7},{6,4},{7,5},{8,10},{9,11},{10,... | collective-permute-start | bytes 196616 | tf_op jit(solution)/shard_map/ppermute | solution.py:38
  66.6 2.7 %collective-permute-done.18 = bf16[1,128,256]{2,1,0:T(8,128)(2,1)S(1)} collective-permute-done((bf16[1,128,256]{2,1,0:T(8,128)(2,1)S(1)}, bf16[1,128,256]{2,1,0:T(8,128)(2,1)S(1)}, u32[]{:S(2)}, u32[]{:S(2)}) %collective-permute-start.18) | collective-permute-done | bytes 65568 | tf_op jit(solution)/shard_map/ppermute | solution.py:38
  70.0 2.3 %collective-permute-start.20 = (bf16[2,128,256]{2,1,0:T(8,128)(2,1)S(1)}, bf16[2,128,256]{2,1,0:T(8,128)(2,1)S(1)}, u32[]{:S(2)}, u32[]{:S(2)}) collective-permute-start(bf16[2,128,256]{2,1,0:T(8,128)(2,1)S(1)} %pad_maximum_fusion.5), channel_id=1, source_target_pairs={{0,2},{1,3},{2,0},{3,1},{4,6},{5,7},{6,4},{7,5},{8,10},{9,11},{10,... | collective-permute-start | bytes 393224 | tf_op jit(solution)/shard_map/ppermute | solution.py:38
  75.6 2.2 %rotate.2 = (bf16[512,2048]{1,0:T(8,128)(2,1)S(1)}, bf16[3,512,2048]{2,1,0:T(8,128)(2,1)S(1)}, f32[3,16,128]{2,1,0:T(8,128)S(1)}) custom-call(s32[16]{0:T(128)S(1)} %get-tuple-element.113.place_ref, s32[1]{0:T(128)} %bitcast.me_ref, bf16[8,128,256]{2,1,0:T(8,128)(2,1)S(1)} %constant_dynamic-update-slice_fusion.gathered_ref, bf16[512,2048]{1,0:T(8,128)(2,1)S(1)} %copy-done, ...), custom_call_target="tpu_custom_call" | custom-call | flops 1073741824 | bytes 8388608 | tf_op jit(solution)/shard_map/rotate/pallas_call | solution.py:378
  77.8 2.2 %rotate.3 = (bf16[512,2048]{1,0:T(8,128)(2,1)S(1)}, bf16[3,512,2048]{2,1,0:T(8,128)(2,1)S(1)}, f32[3,16,128]{2,1,0:T(8,128)S(1)}) custom-call(s32[16]{0:T(128)S(1)} %get-tuple-element.113.place_ref, s32[1]{0:T(128)} %bitcast.me_ref, ...), custom_call_target="tpu_custom_call", output_to_operand_aliasing={{0}: (5, {}), {1}: (6, {}), {2}: (7, {})} | custom-call | flops 1073741824 | bytes 8388608 | tf_op jit(solution)/shard_map/rotate/pallas_call | solution.py:378
  92.8 2.9 %collective-permute-done.26 = f32[3,16,128]{2,1,0:T(8,128)S(1)} collective-permute-done((f32[3,16,128]{2,1,0:T(8,128)S(1)}, f32[3,16,128]{2,1,0:T(8,128)S(1)}, u32[]{:S(2)}, u32[]{:S(2)}) %collective-permute-start.26) | collective-permute-done | bytes 24608 | tf_op jit(solution)/shard_map/ppermute | solution.py:38
  99.8 2.4 %collective-permute-done.31 = bf16[4,128,128]{2,1,0:T(8,128)(2,1)S(1)} collective-permute-done((bf16[4,128,128]{2,1,0:T(8,128)(2,1)S(1)}, bf16[4,128,128]{2,1,0:T(8,128)(2,1)S(1)}, u32[]{:S(2)}, u32[]{:S(2)}) %collective-permute-start.31) | collective-permute-done | bytes 131104 | tf_op jit(solution)/shard_map/ppermute | solution.py:38
  102.2 2.6 %collective-permute-start.32 = (bf16[1,128,128]{2,1,0:T(8,128)(2,1)S(1)}, bf16[1,128,128]{2,1,0:T(8,128)(2,1)S(1)}, u32[]{:S(2)}, u32[]{:S(2)}) collective-permute-start(bf16[1,128,128]{2,1,0:T(8,128)(2,1)S(1)} %get-tuple-element.213), channel_id=1, source_target_pairs={{0,12},{1,13},{2,14},{3,15},{4,8},{5,9},{6,10},{7,11},{8,4},{9,5},... | collective-permute-start | bytes 98312 | tf_op jit(solution)/shard_map/ppermute | solution.py:38
  111.0 9.2 %rotation.3 = bf16[128,256]{1,0:T(8,128)(2,1)S(1)} custom-call(s32[1]{0:T(128)} %bitcast.me_ref, f32[2,128,128]{2,1,0:T(8,128)S(1)} %pad_maximum_fusion.6.packed_ref), custom_call_target="tpu_custom_call" | custom-call | tf_op jit(solution)/shard_map/rotation/pallas_call | solution.py:336
  125.8 2.9 %collective-permute-done.40 = bf16[1,128,256]{2,1,0:T(8,128)(2,1)S(1)} collective-permute-done((bf16[1,128,256]{2,1,0:T(8,128)(2,1)S(1)}, bf16[1,128,256]{2,1,0:T(8,128)(2,1)S(1)}, u32[]{:S(2)}, u32[]{:S(2)}) %collective-permute-start.40) | collective-permute-done | bytes 65568 | tf_op jit(solution)/shard_map/ppermute | solution.py:38
  132.5 3.7 %collective-permute-done.41 = bf16[2,128,256]{2,1,0:T(8,128)(2,1)S(1)} collective-permute-done((bf16[2,128,256]{2,1,0:T(8,128)(2,1)S(1)}, bf16[2,128,256]{2,1,0:T(8,128)(2,1)S(1)}, u32[]{:S(2)}, u32[]{:S(2)}) %collective-permute-start.41) | collective-permute-done | bytes 131104 | tf_op jit(solution)/shard_map/ppermute | solution.py:38
  137.9 2.2 %rotate_last.1 = bf16[512,2048]{1,0:T(8,128)(2,1)} custom-call(s32[16]{0:T(128)S(1)} %get-tuple-element.111.place_ref, s32[16]{0:T(128)S(1)} %get-tuple-element.225.home_ref, s32[1]{0:T(128)} %bitcast.me_ref, bf16[512,1024]{1,0:T(8,128)(2,1)S(1)} %turn_near.1.turned_ref, bf16[8,128,256]{2,1,0:T(8,128)(2,1)S(1)} %constant_dynamic-update-slice_fusion.15.gathered_ref, ...), custom_call_target="tpu_custom_call" | custom-call | tf_op jit(solution)/shard_map/rotate_last/pallas_call | solution.py:454
  (145 shorter events, 66.7 us)
Async XLA Ops:
  2.2 10.1 %collective-permute-start.1 = (bf16[128,2048]{1,0:T(8,128)(2,1)}, bf16[128,2048]{1,0:T(8,128)(2,1)}, u32[]{:S(2)}, u32[]{:S(2)}) collective-permute-start(bf16[128,2048]{1,0:T(8,128)(2,1)} %get-tuple-element.115), channel_id=1, source_target_pairs={{0,1},{1,0},{2,3},{3,2},{4,5},{5,4},{6,7},{7,6},{8,9},{9,8},{10,11... | collective-permute-start | bytes 1572872 | tf_op jit(solution)/shard_map/ppermute | solution.py:38
  2.7 11.6 %collective-permute-start = (bf16[128,2048]{1,0:T(8,128)(2,1)}, bf16[128,2048]{1,0:T(8,128)(2,1)}, u32[]{:S(2)}, u32[]{:S(2)}) collective-permute-start(bf16[128,2048]{1,0:T(8,128)(2,1)} %get-tuple-element.108), channel_id=1, source_target_pairs={{1,2},{3,4},{5,6},{7,8},{9,10},{11,12},{13,14},{2,1},{4,3},{6,5},{... | collective-permute-start | bytes 1572872 | tf_op jit(solution)/shard_map/ppermute | solution.py:556
  16.6 6.6 %collective-permute-start.2 = (f32[3,16,128]{2,1,0:T(8,128)S(1)}, f32[3,16,128]{2,1,0:T(8,128)S(1)}, u32[]{:S(2)}, u32[]{:S(2)}) collective-permute-start(f32[3,16,128]{2,1,0:T(8,128)S(1)} %get-tuple-element.128), channel_id=1, source_target_pairs={{0,1},{1,0},{2,3},{3,2},{4,5},{5,4},{6,7},{7,6},{8,9},{9,8},{10,11... | collective-permute-start | bytes 73736 | tf_op jit(solution)/shard_map/ppermute | solution.py:38
  23.2 5.4 %collective-permute-start.3 = (f32[3,16,128]{2,1,0:T(8,128)S(1)}, f32[3,16,128]{2,1,0:T(8,128)S(1)}, u32[]{:S(2)}, u32[]{:S(2)}) collective-permute-start(f32[3,16,128]{2,1,0:T(8,128)S(1)} %add.48), channel_id=1, source_target_pairs={{0,2},{1,3},{2,0},{3,1},{4,6},{5,7},{6,4},{7,5},{8,10},{9,11},{10,... | collective-permute-start | bytes 73736 | tf_op jit(solution)/shard_map/ppermute | solution.py:38
  30.3 7.3 %collective-permute-start.6 = (f32[2,3,128,128]{3,2,1,0:T(8,128)S(1)}, f32[2,3,128,128]{3,2,1,0:T(8,128)S(1)}, u32[]{:S(2)}, u32[]{:S(2)}) collective-permute-start(f32[2,3,128,128]{3,2,1,0:T(8,128)S(1)} %get-tuple-element.149), channel_id=1, source_target_pairs={{0,1},{1,0},{2,3},{3,2},{4,5},{5,4},{6,7},{7,6},{8,9},{9,8},{10,11... | collective-permute-start | bytes 1179656 | tf_op jit(solution)/shard_map/ppermute | solution.py:38
  30.3 7.3 %collective-permute-start.7 = (f32[2,3,128,128]{3,2,1,0:T(8,128)S(1)}, f32[2,3,128,128]{3,2,1,0:T(8,128)S(1)}, u32[]{:S(2)}, u32[]{:S(2)}) collective-permute-start(f32[2,3,128,128]{3,2,1,0:T(8,128)S(1)} %get-tuple-element.150), channel_id=1, source_target_pairs={{0,1},{1,0},{2,3},{3,2},{4,5},{5,4},{6,7},{7,6},{8,9},{9,8},{10,11... | collective-permute-start | bytes 1179656 | tf_op jit(solution)/shard_map/ppermute | solution.py:38
  30.8 6.9 %collective-permute-start.8 = (f32[2,3,128,128]{3,2,1,0:T(8,128)S(1)}, f32[2,3,128,128]{3,2,1,0:T(8,128)S(1)}, u32[]{:S(2)}, u32[]{:S(2)}) collective-permute-start(f32[2,3,128,128]{3,2,1,0:T(8,128)S(1)} %get-tuple-element.151), channel_id=1, source_target_pairs={{0,1},{1,0},{2,3},{3,2},{4,5},{5,4},{6,7},{7,6},{8,9},{9,8},{10,11... | collective-permute-start | bytes 1179656 | tf_op jit(solution)/shard_map/ppermute | solution.py:38
  32.6 5.1 %collective-permute-start.9 = (f32[2,3,128,128]{3,2,1,0:T(8,128)S(1)}, f32[2,3,128,128]{3,2,1,0:T(8,128)S(1)}, u32[]{:S(2)}, u32[]{:S(2)}) collective-permute-start(f32[2,3,128,128]{3,2,1,0:T(8,128)S(1)} %get-tuple-element.152), channel_id=1, source_target_pairs={{0,1},{1,0},{2,3},{3,2},{4,5},{5,4},{6,7},{7,6},{8,9},{9,8},{10,11... | collective-permute-start | bytes 1179656 | tf_op jit(solution)/shard_map/ppermute | solution.py:38
  39.0 5.0 %collective-permute-start.10 = (bf16[4,128,128]{2,1,0:T(8,128)(2,1)S(1)}, bf16[4,128,128]{2,1,0:T(8,128)(2,1)S(1)}, u32[]{:S(2)}, u32[]{:S(2)}) collective-permute-start(bf16[4,128,128]{2,1,0:T(8,128)(2,1)S(1)} %weigh.4), channel_id=1, source_target_pairs={{0,2},{1,3},{2,0},{3,1},{4,6},{5,7},{6,4},{7,5},{8,10},{9,11},{10,... | collective-permute-start | bytes 393224 | tf_op jit(solution)/shard_map/ppermute | solution.py:38
  44.1 5.9 %collective-permute-start.11 = (bf16[1,128,128]{2,1,0:T(8,128)(2,1)S(1)}, bf16[1,128,128]{2,1,0:T(8,128)(2,1)S(1)}, u32[]{:S(2)}, u32[]{:S(2)}) collective-permute-start(bf16[1,128,128]{2,1,0:T(8,128)(2,1)S(1)} %get-tuple-element.216), channel_id=1, source_target_pairs={{0,12},{1,13},{2,14},{3,15},{4,8},{5,9},{6,10},{7,11},{8,4},{9,5},... | collective-permute-start | bytes 98312 | tf_op jit(solution)/shard_map/ppermute | solution.py:38
  58.1 7.6 %collective-permute-start.16 = (bf16[1,128,256]{2,1,0:T(8,128)(2,1)S(1)}, bf16[1,128,256]{2,1,0:T(8,128)(2,1)S(1)}, u32[]{:S(2)}, u32[]{:S(2)}) collective-permute-start(bf16[1,128,256]{2,1,0:T(8,128)(2,1)S(1)} %bitcast.16), channel_id=1, source_target_pairs={{0,4},{1,5},{2,6},{3,7},{4,0},{5,1},{6,2},{7,3},{8,12},{9,13},{10,... | collective-permute-start | bytes 196616 | tf_op jit(solution)/shard_map/ppermute | solution.py:38
  60.2 6.4 %collective-permute-start.19 = (bf16[1,128,256]{2,1,0:T(8,128)(2,1)S(1)}, bf16[1,128,256]{2,1,0:T(8,128)(2,1)S(1)}, u32[]{:S(2)}, u32[]{:S(2)}) collective-permute-start(bf16[1,128,256]{2,1,0:T(8,128)(2,1)S(1)} %bitcast.17), channel_id=1, source_target_pairs={{0,12},{1,13},{2,14},{3,15},{4,8},{5,9},{6,10},{7,11},{8,4},{9,5},... | collective-permute-start | bytes 196616 | tf_op jit(solution)/shard_map/ppermute | solution.py:38
  62.4 6.9 %collective-permute-start.18 = (bf16[1,128,256]{2,1,0:T(8,128)(2,1)S(1)}, bf16[1,128,256]{2,1,0:T(8,128)(2,1)S(1)}, u32[]{:S(2)}, u32[]{:S(2)}) collective-permute-start(bf16[1,128,256]{2,1,0:T(8,128)(2,1)S(1)} %bitcast.18), channel_id=1, source_target_pairs={{0,8},{1,9},{2,10},{3,11},{4,12},{5,13},{6,14},{7,15},{8,0},{9,1},... | collective-permute-start | bytes 196616 | tf_op jit(solution)/shard_map/ppermute | solution.py:38
  62.8 6.5 %collective-permute-start.15 = (bf16[1,128,256]{2,1,0:T(8,128)(2,1)S(1)}, bf16[1,128,256]{2,1,0:T(8,128)(2,1)S(1)}, u32[]{:S(2)}, u32[]{:S(2)}) collective-permute-start(bf16[1,128,256]{2,1,0:T(8,128)(2,1)S(1)} %bitcast.19), channel_id=1, source_target_pairs={{0,2},{1,3},{2,0},{3,1},{4,6},{5,7},{6,4},{7,5},{8,10},{9,11},{10,... | collective-permute-start | bytes 196616 | tf_op jit(solution)/shard_map/ppermute | solution.py:38
  70.0 5.4 %collective-permute-start.20 = (bf16[2,128,256]{2,1,0:T(8,128)(2,1)S(1)}, bf16[2,128,256]{2,1,0:T(8,128)(2,1)S(1)}, u32[]{:S(2)}, u32[]{:S(2)}) collective-permute-start(bf16[2,128,256]{2,1,0:T(8,128)(2,1)S(1)} %pad_maximum_fusion.5), channel_id=1, source_target_pairs={{0,2},{1,3},{2,0},{3,1},{4,6},{5,7},{6,4},{7,5},{8,10},{9,11},{10,... | collective-permute-start | bytes 393224 | tf_op jit(solution)/shard_map/ppermute | solution.py:38
  88.4 7.3 %collective-permute-start.27 = (f32[2,3,128,128]{3,2,1,0:T(8,128)S(1)}, f32[2,3,128,128]{3,2,1,0:T(8,128)S(1)}, u32[]{:S(2)}, u32[]{:S(2)}) collective-permute-start(f32[2,3,128,128]{3,2,1,0:T(8,128)S(1)} %get-tuple-element.197), channel_id=1, source_target_pairs={{0,1},{1,0},{2,3},{3,2},{4,5},{5,4},{6,7},{7,6},{8,9},{9,8},{10,11... | collective-permute-start | bytes 1179656 | tf_op jit(solution)/shard_map/ppermute | solution.py:38
  89.9 5.8 %collective-permute-start.28 = (f32[2,3,128,128]{3,2,1,0:T(8,128)S(1)}, f32[2,3,128,128]{3,2,1,0:T(8,128)S(1)}, u32[]{:S(2)}, u32[]{:S(2)}) collective-permute-start(f32[2,3,128,128]{3,2,1,0:T(8,128)S(1)} %get-tuple-element.198), channel_id=1, source_target_pairs={{0,1},{1,0},{2,3},{3,2},{4,5},{5,4},{6,7},{7,6},{8,9},{9,8},{10,11... | collective-permute-start | bytes 1179656 | tf_op jit(solution)/shard_map/ppermute | solution.py:38
  90.5 5.3 %collective-permute-start.29 = (f32[2,3,128,128]{3,2,1,0:T(8,128)S(1)}, f32[2,3,128,128]{3,2,1,0:T(8,128)S(1)}, u32[]{:S(2)}, u32[]{:S(2)}) collective-permute-start(f32[2,3,128,128]{3,2,1,0:T(8,128)S(1)} %get-tuple-element.199), channel_id=1, source_target_pairs={{0,1},{1,0},{2,3},{3,2},{4,5},{5,4},{6,7},{7,6},{8,9},{9,8},{10,11... | collective-permute-start | bytes 1179656 | tf_op jit(solution)/shard_map/ppermute | solution.py:38
  102.2 5.9 %collective-permute-start.32 = (bf16[1,128,128]{2,1,0:T(8,128)(2,1)S(1)}, bf16[1,128,128]{2,1,0:T(8,128)(2,1)S(1)}, u32[]{:S(2)}, u32[]{:S(2)}) collective-permute-start(bf16[1,128,128]{2,1,0:T(8,128)(2,1)S(1)} %get-tuple-element.213), channel_id=1, source_target_pairs={{0,12},{1,13},{2,14},{3,15},{4,8},{5,9},{6,10},{7,11},{8,4},{9,5},... | collective-permute-start | bytes 98312 | tf_op jit(solution)/shard_map/ppermute | solution.py:38
  122.2 6.5 %collective-permute-start.40 = (bf16[1,128,256]{2,1,0:T(8,128)(2,1)S(1)}, bf16[1,128,256]{2,1,0:T(8,128)(2,1)S(1)}, u32[]{:S(2)}, u32[]{:S(2)}) collective-permute-start(bf16[1,128,256]{2,1,0:T(8,128)(2,1)S(1)} %bitcast.11), channel_id=1, source_target_pairs={{0,12},{1,13},{2,14},{3,15},{4,8},{5,9},{6,10},{7,11},{8,4},{9,5},... | collective-permute-start | bytes 196616 | tf_op jit(solution)/shard_map/ppermute | solution.py:38
  123.5 7.2 %collective-permute-start.39 = (bf16[1,128,256]{2,1,0:T(8,128)(2,1)S(1)}, bf16[1,128,256]{2,1,0:T(8,128)(2,1)S(1)}, u32[]{:S(2)}, u32[]{:S(2)}) collective-permute-start(bf16[1,128,256]{2,1,0:T(8,128)(2,1)S(1)} %bitcast.12), channel_id=1, source_target_pairs={{0,8},{1,9},{2,10},{3,11},{4,12},{5,13},{6,14},{7,15},{8,0},{9,1},... | collective-permute-start | bytes 196616 | tf_op jit(solution)/shard_map/ppermute | solution.py:38
  123.8 6.9 %collective-permute-start.36 = (bf16[1,128,256]{2,1,0:T(8,128)(2,1)S(1)}, bf16[1,128,256]{2,1,0:T(8,128)(2,1)S(1)}, u32[]{:S(2)}, u32[]{:S(2)}) collective-permute-start(bf16[1,128,256]{2,1,0:T(8,128)(2,1)S(1)} %bitcast.13), channel_id=1, source_target_pairs={{0,2},{1,3},{2,0},{3,1},{4,6},{5,7},{6,4},{7,5},{8,10},{9,11},{10,... | collective-permute-start | bytes 196616 | tf_op jit(solution)/shard_map/ppermute | solution.py:38
  124.6 6.1 %collective-permute-start.38 = (bf16[1,128,256]{2,1,0:T(8,128)(2,1)S(1)}, bf16[1,128,256]{2,1,0:T(8,128)(2,1)S(1)}, u32[]{:S(2)}, u32[]{:S(2)}) collective-permute-start(bf16[1,128,256]{2,1,0:T(8,128)(2,1)S(1)} %collective-permute-done.37), channel_id=1, source_target_pairs={{0,2},{1,3},{2,0},{3,1},{4,6},{5,7},{6,4},{7,5},{8,10},{9,11},{10,... | collective-permute-start | bytes 196616 | tf_op jit(solution)/shard_map/ppermute | solution.py:38
  130.8 5.5 %collective-permute-start.41 = (bf16[2,128,256]{2,1,0:T(8,128)(2,1)S(1)}, bf16[2,128,256]{2,1,0:T(8,128)(2,1)S(1)}, u32[]{:S(2)}, u32[]{:S(2)}) collective-permute-start(bf16[2,128,256]{2,1,0:T(8,128)(2,1)S(1)} %pad_maximum_fusion.7), channel_id=1, source_target_pairs={{0,2},{1,3},{2,0},{3,1},{4,6},{5,7},{6,4},{7,5},{8,10},{9,11},{10,... | collective-permute-start | bytes 393224 | tf_op jit(solution)/shard_map/ppermute | solution.py:38
  (24 other events, 88.9 us)
